TPU v7x, 32 devices: a whole 2x2x4 slice. The times are simulated.
32 devices in a mesh: rows: 4 (over x, core), batch: 8 (over z, y).
Axes of the slice: x: 2, y: 2, z: 4, core: 2. Of those that a mesh axis runs over, the one named last changes fastest.
Arguments:
- features: bfloat16 [256, 16, 16, 512], P('batch', 'rows'), may hold values from -6 to 6
- target: float32 [256, 8, 8, 12], P('batch', 'rows'), may hold values from -6 to 6
- mask: int32 [256, 8, 8, 4], P('batch', 'rows'), may hold values 0 or 1
- codes: int32 [256, 8, 8, 4], P('batch', 'rows'), may hold values from 0 to 16383
- conv_w: float32 [4608, 3, 512], P('batch'), may hold values from -0.09375 to 0.09375
- proj_w: float32 [512, 256], P('batch'), may hold values from -0.25 to 0.25
- code_w: float32 [16384, 256], P('batch'), may hold values from -3 to 3
- head_w: float32 [256, 12], P('batch'), may hold values from -0.375 to 0.375
- gains: float32 [4, 512], replicated, may hold values from 0.1 to 1.9
- conv_row: float32 [4608, 3], P('batch'), may hold values from 5.811453e-10 to 9.834766e-08
- conv_col: float32 [3, 512], replicated, may hold values from 5.811453e-10 to 9.834766e-08
- proj_row: float32 [512], P('batch'), may hold values from 1.0728836e-07 to 1.7285347e-06
- proj_col: float32 [256], replicated, may hold values from 1.0728836e-07 to 1.7285347e-06
- code_row: float32 [16384], P('batch'), may hold values from 2.9296875e-12 to 1.4648437e-11
- code_col: float32 [256], replicated, may hold values from 2.9296875e-12 to 1.4648437e-11
- head_row: float32 [256], P('batch'), may hold values from 1.5625e-06 to 2.5e-05
- head_col: float32 [12], replicated, may hold values from 1.5625e-06 to 2.5e-05
- gain_state: float32 [4, 512], replicated, may hold values from 6.8359374e-11 to 3.4179687e-10
Outputs:
- loss: float32 [], replicated
- conv_grad: float32 [4608, 3, 512], P('batch')
- conv_row_new: float32 [4608, 3], P('batch')
- conv_col_new: float32 [3, 512], replicated
- conv_new: float32 [4608, 3, 512], P('batch')
- conv_low: bfloat16 [4608, 3, 512], P('batch')
- proj_grad: float32 [512, 256], P('batch')
- proj_row_new: float32 [512], P('batch')
- proj_col_new: float32 [256], replicated
- proj_new: float32 [512, 256], P('batch')
- proj_low: bfloat16 [512, 256], P('batch')
- code_grad: float32 [16384, 256], P('batch')
- code_row_new: float32 [16384], P('batch')
- code_col_new: float32 [256], replicated
- code_new: float32 [16384, 256], P('batch')
- code_low: bfloat16 [16384, 256], P('batch')
- head_grad: float32 [256, 12], P('batch')
- head_row_new: float32 [256], P('batch')
- head_col_new: float32 [12], replicated
- head_new: float32 [256, 12], P('batch')
- head_low: bfloat16 [256, 12], P('batch')
- gain_grad: float32 [4, 512], replicated
- gain_state_new: float32 [4, 512], replicated
- gains_new: float32 [4, 512], replicated
All inputs are finite; a program needn't handle non-finite values. No bound on the sum of `mask` on one device may be relied on, other than what follows from the above.
Results may differ from a plain program's by a relative error of at most 0.0095.
Values may be sent and summed in bfloat16 or wider, within the bound.
A program may use at most 256 MiB of HBM per device.

v0:
```python
import functools

import jax
import jax.numpy as jnp
from jax import lax
from jax.experimental import pallas as pl
from jax.experimental.pallas import tpu as pltpu
from jax.sharding import PartitionSpec as P

GROUPS = 32
BETA = 0.25
RATE = 0.5
EPS_NORM = 1e-05
EPS_SQ = 1e-30
BF = jnp.bfloat16
F32 = jnp.float32
BOTH = ("batch", "rows")
MIB = 1 << 20
VM = pl.BlockSpec(memory_space=pltpu.VMEM)


def group_sum(v):
    lane = lax.broadcasted_iota(jnp.int32, v.shape, 1)
    width = v.shape[1]
    for k in (1, 2, 4, 8):
        up = pltpu.roll(v, k, 1)
        down = pltpu.roll(v, width - k, 1)
        v = v + jnp.where((lane & k) != 0, up, down)
    return v


def moments(v):
    count = v.shape[0] * (v.shape[1] // GROUPS)
    sums = jnp.concatenate(
        [jnp.sum(v, axis=0, keepdims=True), jnp.sum(v * v, axis=0, keepdims=True)]
        + [jnp.zeros((6, v.shape[1]), F32)],
        axis=0,
    )
    sums = group_sum(sums) / count
    mean = sums[0:1]
    return mean, lax.rsqrt(sums[1:2] - mean * mean + EPS_NORM)


def shifted(v, by):
    cells = v.shape[0]
    col = lax.broadcasted_iota(jnp.int32, v.shape, 0) & 15
    edge = 0 if by == 1 else 15
    return jnp.where(col == edge, 0.0, pltpu.roll(v, by % cells, 0))


def fill_three(dst, left, mid, right):
    ch = mid.shape[1]
    for k, v in enumerate((left, mid, right)):
        dst[1:17, :, k * ch : (k + 1) * ch] = v.astype(BF).reshape(16, 16, ch)


def zero_edges(dst):
    dst[0] = jnp.zeros(dst.shape[1:], dst.dtype)
    dst[17] = jnp.zeros(dst.shape[1:], dst.dtype)


def put_lanes(dst, rows, v):
    for k in range(dst.shape[0]):
        dst[k, rows, :] = v[:, k * 128 : (k + 1) * 128]


def get_lanes(src, rows):
    return jnp.concatenate([src[k, rows, :] for k in range(src.shape[0])], axis=1)


def conv_rows(src, w_ref):
    acc = None
    width = src.shape[2]
    for dy in range(3):
        lhs = src[dy : dy + 16].reshape(256, width)
        d = jnp.dot(lhs, w_ref[dy * width : (dy + 1) * width, :], preferred_element_type=F32)
        acc = d if acc is None else acc + d
    return acc


def conv_rows_back(src, w_ref):
    acc = None
    ch = src.shape[2] // 3
    for dy in range(3):
        for dx in range(3):
            lhs = src[2 - dy : 18 - dy, :, dx * ch : (dx + 1) * ch].reshape(256, ch)
            t = (dy * 3 + dx) * ch
            d = lax.dot_general(
                lhs, w_ref[t : t + ch, :], (((1,), (1,)), ((), ())), preferred_element_type=F32
            )
            acc = d if acc is None else acc + d
    return acc


def conv_weight_grad(a_ref, d3_ref, dw_ref):
    crops, cells, ch = a_ref.shape
    nb = 256

    def block(j, carry):
        dx = j // (ch // nb)
        n = j % (ch // nb)
        lane = pl.multiple_of(j * nb, nb)
        for dy in range(3):
            rhs = d3_ref[:, 2 - dy : 18 - dy, :, pl.ds(lane, nb)].reshape(crops * cells, nb)
            d = lax.dot_general(
                a_ref[...].reshape(crops * cells, ch),
                rhs,
                (((0,), (0,)), ((), ())),
                preferred_element_type=F32,
            )
            row = pl.multiple_of((dy * 3 + dx) * ch, ch)
            dw_ref[pl.ds(row, ch), pl.ds(pl.multiple_of(n * nb, nb), nb)] = d.astype(dw_ref.dtype)
        return carry

    lax.fori_loop(0, 3 * (ch // nb), block, 0)


def silu(h):
    return h * jax.nn.sigmoid(h)


def first_conv_kernel(x_ref, gains_ref, w_ref, a_ref, c_ref, a3):
    zero_edges(a3)

    def crop(i, carry):
        v = x_ref[i].astype(F32)
        mean, rstd = moments(v)
        a = silu((v - mean) * rstd * gains_ref[0:1, :] + gains_ref[1:2, :])
        a_ref[i] = a.astype(BF)
        fill_three(a3, shifted(a, 1), a, shifted(a, -1))
        c_ref[i] = conv_rows(a3, w_ref)
        return carry

    lax.fori_loop(0, x_ref.shape[0], crop, 0)


def second_conv_kernel(c_in_ref, x_ref, gains_ref, w_ref, a_ref, l_ref, a3, y32):
    zero_edges(a3)
    ch = x_ref.shape[2]

    def crop(i, carry):
        v = c_in_ref[i]
        mean, rstd = moments(v)
        a = silu((v - mean) * rstd * gains_ref[2:3, :] + gains_ref[3:4, :])
        a_ref[i] = a.astype(BF)
        fill_three(a3, shifted(a, 1), a, shifted(a, -1))
        put_lanes(y32, slice(None), conv_rows(a3, w_ref) + x_ref[i].astype(F32))
        even = get_lanes(y32, pl.ds(0, 128, stride=2))
        odd = get_lanes(y32, pl.ds(1, 128, stride=2))
        cell = lax.broadcasted_iota(jnp.int32, odd.shape, 0) & 7
        before = jnp.where(cell == 0, 0.0, pltpu.roll(odd, 1, 0))
        for dx, part in enumerate((before, even, odd)):
            part = part.reshape(8, 2, 8, ch)
            upper = part[:, 0].reshape(64, ch)
            lower = part[:, 1].reshape(64, ch)
            above = jnp.concatenate([jnp.zeros((8, ch), F32), lower[:56]], axis=0)
            for dy, rows in enumerate((above, upper, lower)):
                lane = (dy * 3 + dx) * ch
                l_ref[pl.ds(pl.multiple_of(i * 64, 64), 64), lane : lane + ch] = rows.astype(BF)
        return carry

    lax.fori_loop(0, x_ref.shape[0], crop, 0)


def down_back_kernel(ds_ref, l_ref, w_ref, dc_ref, dw_ref, y32):
    cells, ch = ds_ref.shape
    crops = cells // 64

    def dot_t(lhs, tap):
        return lax.dot_general(
            lhs.astype(BF),
            w_ref[tap * ch : (tap + 1) * ch, :],
            (((1,), (1,)), ((), ())),
            preferred_element_type=F32,
        )

    def crop(i, carry):
        here = ds_ref[pl.ds(pl.multiple_of(i * 64, 64), 64), :].astype(F32)
        at = lax.broadcasted_iota(jnp.int32, here.shape, 0)

        def next_col(v):
            return jnp.where((at & 7) == 7, 0.0, pltpu.roll(v, 63, 0))

        right = next_col(here)
        under = jnp.concatenate([here[8:], jnp.zeros((8, ch), F32)], axis=0)
        corner = next_col(under)
        ee = dot_t(here, 4)
        eo = dot_t(here, 5) + dot_t(right, 3)
        oe = dot_t(here, 7) + dot_t(under, 1)
        oo = dot_t(here, 8) + dot_t(right, 6) + dot_t(under, 2) + dot_t(corner, 0)

        def both_rows(top, bottom):
            top, bottom = top.reshape(8, 1, 8, ch), bottom.reshape(8, 1, 8, ch)
            return jnp.concatenate([top, bottom], axis=1).reshape(128, ch)

        put_lanes(y32, pl.ds(0, 128, stride=2), both_rows(ee, oe))
        put_lanes(y32, pl.ds(1, 128, stride=2), both_rows(eo, oo))
        dc_ref[i] = get_lanes(y32, slice(None)).astype(BF)
        return carry

    lax.fori_loop(0, crops, crop, 0)

    def block(t, carry):
        lane = pl.multiple_of(t * ch, ch)
        d = lax.dot_general(
            l_ref[:, pl.ds(lane, ch)],
            ds_ref[...],
            (((0,), (0,)), ((), ())),
            preferred_element_type=F32,
        )
        dw_ref[pl.ds(lane, ch), :] = d.astype(BF)
        return carry

    lax.fori_loop(0, 9, block, 0)


def hidden_grad(v, gain, shift, d_act):
    mean, rstd = moments(v)
    vhat = (v - mean) * rstd
    h = vhat * gain + shift
    sig = jax.nn.sigmoid(h)
    return d_act * sig * (1.0 + h * (1.0 - sig)), vhat, rstd


def unit_back_kernel(dc_ref, v_ref, gains_ref, w_ref, a_ref, *outs, row, inner):
    if inner:
        din_ref, dw_ref, dg_ref, d3 = outs
    else:
        dw_ref, dg_ref, d3 = outs
    crops, cells, ch = dc_ref.shape
    dg_ref[...] = jnp.zeros_like(dg_ref)

    def crop(i, carry):
        d = dc_ref[i].astype(F32)
        slot = d3.at[i]
        zero_edges(slot)
        fill_three(slot, shifted(d, -1), d, shifted(d, 1))
        d_act = conv_rows_back(slot, w_ref)
        gain = gains_ref[row : row + 1, :]
        hg, vhat, rstd = hidden_grad(
            v_ref[i].astype(F32), gain, gains_ref[row + 1 : row + 2, :], d_act
        )
        one = jnp.sum(hg * vhat, axis=0, keepdims=True)
        two = jnp.sum(hg, axis=0, keepdims=True)
        dg_ref[0:1, :] += one
        dg_ref[1:2, :] += two
        if inner:
            count = cells * (ch // GROUPS)
            sums = jnp.concatenate([two * gain, one * gain, jnp.zeros((6, ch), F32)], axis=0)
            sums = group_sum(sums) / count
            din_ref[i] = (rstd * (hg * gain - sums[0:1] - vhat * sums[1:2])).astype(BF)
        return carry

    lax.fori_loop(0, crops, crop, 0)
    conv_weight_grad(a_ref, d3, dw_ref)


def kernel_call(body, outs, scratch, flops, *args):
    bytes_accessed = sum(a.size * a.dtype.itemsize for a in args)
    bytes_accessed += sum(o.size * o.dtype.itemsize for o in outs)
    return pl.pallas_call(
        body,
        out_shape=outs,
        in_specs=[VM] * len(args),
        out_specs=[VM] * len(outs),
        scratch_shapes=scratch,
        compiler_params=pltpu.CompilerParams(vmem_limit_bytes=56 * MIB),
        cost_estimate=pl.CostEstimate(
            flops=flops, bytes_accessed=bytes_accessed, transcendentals=0
        ),
    )(*args)


def contract_last(left, right):
    return lax.dot_general(left, right, (((1,), (0,)), ((), ())), preferred_element_type=F32)


def contract_back(left, right):
    return lax.dot_general(left, right, (((1,), (1,)), ((), ())), preferred_element_type=F32)


def contract_rows(left, right):
    return lax.dot_general(left, right, (((0,), (0,)), ((), ())), preferred_element_type=F32)


def row_part(grad, row):
    g_sq = grad * grad + EPS_SQ
    row_new = 0.5 * row + 0.5 * jnp.mean(g_sq, axis=2)
    over_row = jnp.sum(grad * grad / row_new[:, :, None], axis=0)
    return row_new, jnp.sum(g_sq, axis=0), jnp.sum(row_new, axis=0), over_row


def finish(grad, weight, row_new, col, col_sum, row_sum, over_row, wt_sq):
    total = grad.shape[0] * lax.axis_size("batch")
    count = total * grad.shape[2]
    col_new = 0.5 * col + 0.5 * col_sum / total
    row_mean = row_sum / total
    upd_sq = row_mean * jnp.sum(over_row / col_new, axis=1)
    rms_u = jnp.sqrt(upd_sq / count)
    scale = jnp.sqrt(wt_sq / count)
    vhat = row_new[:, :, None] * col_new[None] / row_mean[None, :, None]
    update = grad * lax.rsqrt(vhat)
    new = weight - RATE * (scale / jnp.maximum(1.0, rms_u))[None, :, None] * update
    return col_new, new


def local(
    features,
    target,
    mask,
    codes,
    conv_w,
    proj_w,
    code_w,
    head_w,
    gains,
    conv_row,
    conv_col,
    proj_row,
    proj_col,
    code_row,
    code_col,
    head_row,
    head_col,
    gain_state,
):
    ranks = lax.axis_size("rows")
    shards = lax.axis_size("batch")
    me = lax.axis_index("rows")
    crops_all = features.shape[0] * shards
    ch = features.shape[3]
    lat = proj_w.shape[1]
    rgb = head_w.shape[1]
    height = features.shape[1] * ranks
    width = features.shape[2]

    def whole_crops(v):
        return lax.all_to_all(v, "rows", split_axis=0, concat_axis=1, tiled=True)

    def my_part(v):
        size = v.shape[0] // ranks
        return lax.dynamic_slice_in_dim(v, me * size, size, 0)

    conv_piece = jnp.transpose(my_part(conv_w).astype(BF), (1, 0, 2))
    head_wide = jnp.pad(head_w, ((0, 0), (0, lat - rgb)))
    rest_piece = jnp.concatenate(
        [my_part(code_w).astype(BF), my_part(proj_w).astype(BF), my_part(head_wide).astype(BF)]
    )
    n_code, n_proj, n_head = (v.shape[0] // ranks for v in (code_w, proj_w, head_w))
    w_all = [lax.all_gather(conv_piece[0], BOTH, axis=0, tiled=True)]
    later = lax.all_gather(conv_piece[1:], BOTH, axis=0)
    later = jnp.transpose(later, (1, 0, 2, 3)).reshape(2, -1, ch)
    w_all += [later[0], later[1]]
    rest = lax.all_gather(rest_piece, BOTH, axis=0)
    code_all = rest[:, :n_code].reshape(-1, lat)
    proj_all = rest[:, n_code : n_code + n_proj].reshape(-1, lat)
    head_all = rest[:, n_code + n_proj :, :rgb].reshape(-1, rgb)

    x = whole_crops(features)
    target, mask, codes = whole_crops(target), whole_crops(mask), whole_crops(codes)
    crops = x.shape[0]
    cells = height * width
    x = x.reshape(crops, cells, ch)
    lat_cells = crops * cells // 4
    target = target.reshape(lat_cells, rgb)
    mask = mask.reshape(lat_cells, -1)
    codes = codes.reshape(lat_cells, -1)

    conv_flops = 2 * crops * cells * 9 * ch * ch
    three = pltpu.VMEM((18, 16, 3 * ch), BF)
    fold = pltpu.VMEM((ch // 128, cells, 128), F32)

    def big(dtype):
        return jax.ShapeDtypeStruct((crops, cells, ch), dtype)

    dw_shape = jax.ShapeDtypeStruct((9 * ch, ch), BF)
    dg_shape = jax.ShapeDtypeStruct((2, ch), F32)

    a_one, c_one = kernel_call(
        first_conv_kernel, [big(BF), big(F32)], [three], conv_flops, x, gains, w_all[0]
    )
    a_two, windows = kernel_call(
        second_conv_kernel,
        [big(BF), jax.ShapeDtypeStruct((lat_cells, 9 * ch), BF)],
        [three, fold],
        conv_flops,
        c_one,
        x,
        gains,
        w_all[1],
    )
    s_low = contract_last(windows, w_all[2]).astype(BF)

    lat_count = crops_all * cells // 4 * lat
    pix_count = crops_all * cells * 3
    latent = contract_last(s_low, proj_all)
    picked = code_all[codes].astype(F32)
    cum = jnp.cumsum(picked, axis=1)
    resid = latent[:, None, :] - cum
    quant_part = (1.0 + BETA) * jnp.sum(resid * resid) / lat_count
    zq_low = cum[:, -1].astype(BF)
    pred = contract_last(zq_low, head_all)
    diff = pred - target
    weight_mask = jnp.repeat(mask.astype(F32), 3, axis=-1)
    smooth = jnp.sqrt(diff * diff + 1.0)
    recon_part = jnp.sum(weight_mask * (smooth - 1.0)) / pix_count
    d_pred = (weight_mask * (diff / smooth) / pix_count).astype(BF)
    d_head = contract_rows(zq_low, d_pred)
    d_zq = contract_back(d_pred, head_all)
    d_cum = -2.0 / lat_count * resid
    d_picked = jnp.flip(jnp.cumsum(jnp.flip(d_cum, 1), axis=1), 1)
    d_code = jax.ops.segment_sum(
        d_picked.reshape(-1, lat), codes.reshape(-1), num_segments=code_all.shape[0]
    )
    d_lat_low = (jnp.sum(resid, axis=1) * (2.0 * BETA / lat_count) + d_zq).astype(BF)
    d_proj = contract_rows(s_low, d_lat_low)
    d_s_low = contract_back(d_lat_low, proj_all).astype(BF)

    d_c_two, d_down = kernel_call(
        down_back_kernel,
        [big(BF), dw_shape],
        [fold],
        conv_flops // 2,
        d_s_low,
        windows,
        w_all[2],
    )
    d_three = pltpu.VMEM((crops, 18, 16, 3 * ch), BF)
    d_c_one, d_second, gain_two = kernel_call(
        functools.partial(unit_back_kernel, row=2, inner=True),
        [big(BF), dw_shape, dg_shape],
        [d_three],
        2 * conv_flops,
        d_c_two,
        c_one,
        gains,
        w_all[1],
        a_two,
    )
    d_first, gain_one = kernel_call(
        functools.partial(unit_back_kernel, row=0, inner=False),
        [dw_shape, dg_shape],
        [d_three],
        2 * conv_flops,
        d_c_one,
        x,
        gains,
        w_all[0],
        a_one,
    )
    d_gains = jnp.concatenate([gain_one, gain_two], axis=0)

    devices = ranks * shards

    def to_owner(v):
        return lax.psum_scatter(v, BOTH, scatter_dimension=0, tiled=True)

    def to_rows(v):
        return lax.all_gather(v, "rows", axis=0)

    pad = jnp.pad(d_head, ((0, 0), (0, lat - rgb)))
    rest_grad = jnp.concatenate(
        [v.astype(BF).reshape(devices, -1, lat) for v in (d_code, d_proj, pad)], axis=1
    )
    rest_mine = to_owner(rest_grad.reshape(-1, lat))
    conv_mine = [to_owner(v) for v in (d_first, d_second, d_down)]
    rest_full = to_rows(rest_mine).astype(F32)
    conv_full = to_rows(jnp.stack(conv_mine)).astype(F32)
    g_conv = jnp.transpose(conv_full, (0, 2, 1, 3)).reshape(-1, 3, ch)
    g_code = rest_full[:, :n_code].reshape(-1, lat)
    g_proj = rest_full[:, n_code : n_code + n_proj].reshape(-1, lat)
    g_head = rest_full[:, n_code + n_proj :, :rgb].reshape(-1, rgb)

    mats = [
        (g_conv, conv_w, conv_row, conv_col),
        (g_proj[:, None, :], proj_w[:, None, :], proj_row[:, None], proj_col[None, :]),
        (g_code[:, None, :], code_w[:, None, :], code_row[:, None], code_col[None, :]),
        (g_head[:, None, :], head_w[:, None, :], head_row[:, None], head_col[None, :]),
    ]
    rows_new = [row_part(grad, row) for grad, weight, row, col in mats]
    wt_sq = [jnp.sum(weight * weight, axis=(0, 2)) for grad, weight, row, col in mats]
    sums = lax.psum([r[1:] + (w,) for r, w in zip(rows_new, wt_sq)], "batch")
    loss, g_gain = lax.psum((recon_part + quant_part, d_gains), BOTH)
    done = [
        finish(m[0], m[1], r[0], m[3], *s) for m, r, s in zip(mats, rows_new, sums)
    ]

    state_new = 0.5 * gain_state + 0.5 * (g_gain * g_gain + EPS_SQ)
    update = g_gain * lax.rsqrt(state_new)
    rms_u = jnp.sqrt(jnp.mean(update * update))
    scale = jnp.sqrt(jnp.mean(gains * gains))
    gains_new = gains - RATE * scale * update / jnp.maximum(1.0, rms_u)
    conv_new = done[0][1]
    proj_new, code_new, head_new = (d[1][:, 0, :] for d in done[1:])
    return (
        loss,
        g_conv,
        rows_new[0][0],
        done[0][0],
        conv_new,
        conv_new.astype(BF),
        g_proj,
        rows_new[1][0][:, 0],
        done[1][0][0],
        proj_new,
        proj_new.astype(BF),
        g_code,
        rows_new[2][0][:, 0],
        done[2][0][0],
        code_new,
        code_new.astype(BF),
        g_head,
        rows_new[3][0][:, 0],
        done[3][0][0],
        head_new,
        head_new.astype(BF),
        g_gain,
        state_new,
        gains_new,
    )


def solution(mesh):
    cell = P("batch", "rows", None, None)
    mat, vec = P("batch", None), P("batch")
    placed = (cell,) * 4 + (P("batch", None, None), mat, mat, mat, P())
    placed += (mat, P()) + (vec, P()) * 3 + (P(),)
    conv_outs = (P("batch", None, None), mat, P(), P("batch", None, None), P("batch", None, None))
    mat_outs = (mat, vec, P(), mat, mat)
    return jax.shard_map(
        local,
        mesh=mesh,
        in_specs=placed,
        out_specs=(P(),) + conv_outs + mat_outs * 3 + (P(),) * 3,
        check_vma=False,
    )
```

profile of v0, /device:TPU:0, one launch (start us, length us, event | category | flops | bytes accessed | tf_op | source)
XLA Modules:
  0.0 1000.3 jit_solution(15068189076411357615)
XLA Ops:
  14.3 4.2 all-to-all-start
  19.4 2.9 all-to-all-done
  22.3 3.2 all-to-all-start.1
  26.0 3.4 all-to-all-done.1
  29.4 6.2 all_to_all.54
  35.6 3.6 all-to-all-start.3
  45.6 28.8 %all-to-all-done.3 = bf16[32,4,16,512]{3,2,1,0:T(8,128)(2,1)S(1)} async-done(((bf16[32,4,16,512]{3,2,1,0:T(8,128)(2,1)}), bf16[32,4,16,512]{3,2,1,0:T(8,128)(2,1)S(1)}, u32[]{:S(2)}, u32[]{:S(2)}) %all-to-all-start.3) | async-done | bytes 2097184 | tf_op jit(solution)/shard_map/all_to_all | solution.py:338
  75.9 10.3 %all-gather.13.cloned.1.call-done = bf16[1,4608,512]{2,1,0:T(8,128)(2,1)} async-done(((bf16[1,144,512]{2,1,0:T(8,128)(2,1)}), bf16[1,4608,512]{2,1,0:T(8,128)(2,1)}) %all-gather.13.cloned.1.call-update) | async-done | bytes 4718608 | tf_op jit(solution)/shard_map/all_gather | solution.py:350
  86.2 21.0 %shard_map.361 = (bf16[8,256,512]{2,1,0:T(8,128)(2,1)}, f32[8,256,512]{2,1,0:T(8,128)}) custom-call(bf16[8,256,512]{2,1,0:T(8,128)(2,1)} %bitcast.173, f32[4,512]{1,0:T(4,128)} %gains_ref.7, bf16[4608,512]{1,0:T(8,128)(2,1)} %bitcast.200), custom_call_target="tpu_custom_call" | custom-call | flops 9663676416 | bytes 13115392 | tf_op jit(solution)/shard_map/pallas_call | solution.py:261
  107.1 60.4 %all-gather.11.cloned.1.call-done = bf16[17152,256]{1,0:T(8,128)(2,1)} async-done(((bf16[536,256]{1,0:T(8,128)(2,1)}), bf16[17152,256]{1,0:T(8,128)(2,1)}) %all-gather.11.cloned.1.call-update) | async-done | bytes 8781840 | tf_op jit(solution)/shard_map/all_gather | solution.py:354
  168.5 7.6 slice.48
  176.1 11.4 %gather_fusion = bf16[2048,256]{1,0:T(8,128)(2,1)S(1)} fusion(bf16[16384,256]{1,0:T(8,128)(2,1)} %bitcast.150, s32[2048]{0:T(1024)S(1)} %broadcast_clamp_fusion), kind=kCustom, calls=%fused_computation | custom fusion | bytes 2105344 | tf_op jit(solution)/shard_map/gather | solution.py:397
  189.1 62.5 %all-gather.15.cloned.1.call-done = bf16[64,144,512]{2,1,0:T(8,128)(2,1)} async-done(((bf16[2,144,512]{2,1,0:T(8,128)(2,1)}), bf16[64,144,512]{2,1,0:T(8,128)(2,1)}) %all-gather.15.cloned.1.call-update) | async-done | bytes 9437200 | tf_op jit(solution)/shard_map/all_gather | solution.py:351
  251.7 8.1 copy.197
  259.8 6.5 fusion.28
  266.3 23.8 %shard_map.362 = (bf16[8,256,512]{2,1,0:T(8,128)(2,1)}, bf16[512,4608]{1,0:T(8,128)(2,1)}) custom-call(f32[8,256,512]{2,1,0:T(8,128)} %get-tuple-element.35.c_in_ref.v_ref, bf16[8,256,512]{2,1,0:T(8,128)(2,1)} %bitcast.174, f32[4,512]{1,0:T(4,128)} %gains_ref.7, bf16[4608,512]{1,0:T(8,128)(2,1)} %bitcast.165), custom_call_target="tpu_custom_call" | custom-call | flops 9663676416 | bytes 17833984 | tf_op jit(solution)/shard_map/pallas_call | solution.py:261
  290.2 5.1 convolution_convert_fusion
  296.9 1.7 multiply_convert_fusion
  300.8 23.1 %shard_map.363 = (bf16[8,256,512]{2,1,0:T(8,128)(2,1)}, bf16[4608,512]{1,0:T(8,128)(2,1)}) custom-call(bf16[512,512]{1,0:T(8,128)(2,1)} %convolution_convert_fusion.1.ds_ref, bf16[512,4608]{1,0:T(8,128)(2,1)} %get-tuple-element.36.l_ref, bf16[4608,512]{1,0:T(8,128)(2,1)} %bitcast.168), custom_call_target="tpu_custom_call" | custom-call | flops 4831838208 | bytes 16777216 | tf_op jit(solution)/shard_map/pallas_call | solution.py:261
  323.9 33.5 %shard_map.364 = (bf16[8,256,512]{2,1,0:T(8,128)(2,1)}, bf16[4608,512]{1,0:T(8,128)(2,1)}, f32[2,512]{1,0:T(2,128)}) custom-call(bf16[8,256,512]{2,1,0:T(8,128)(2,1)} %get-tuple-element.37.dc_ref, f32[8,256,512]{2,1,0:T(8,128)} %get-tuple-element.35.c_in_ref.v_ref, f32[4,512]{1,0:T(4,128)} %gains_ref.7, bf16[4608,512]{1,0:T(8,128)(2,1)} %bitcast.166, ...), custom_call_target="tpu_custom_call" | custom-call | flops 19327352832 | bytes 19935232 | tf_op jit(solution)/shard_map/pallas_call | solution.py:261
  357.4 29.3 %shard_map.365 = (bf16[4608,512]{1,0:T(8,128)(2,1)}, f32[2,512]{1,0:T(2,128)}) custom-call(bf16[8,256,512]{2,1,0:T(8,128)(2,1)} %get-tuple-element.39.dc_ref, bf16[8,256,512]{2,1,0:T(8,128)(2,1)} %bitcast.175, f32[4,512]{1,0:T(4,128)} %gains_ref.7, bf16[4608,512]{1,0:T(8,128)(2,1)} %bitcast.201, bf16[8,256,512]{2,1,0:T(8,128)(2,1)} %get-tuple-element.40.a_ref), custom_call_target="tpu_custom_call" | custom-call | flops 19327352832 | bytes 15740928 | tf_op jit(solution)/shard_map/pallas_call | solution.py:261
  390.8 1.7 fusion.4
  394.0 3.0 copy.181
  397.0 1.7 reshape.403
  398.7 19.0 %scatter_custom_fusion = f32[16384,256]{1,0:T(8,128)} fusion(s32[2048]{0:T(1024)S(1)} %reshape.401, f32[2048,256]{1,0:T(8,128)} %reshape.403, f32[]{:T(128)} %constant.51.clone.1), kind=kCustom, calls=%fused_computation.4 | custom fusion | flops 524288 | bytes 16777728 | tf_op jit(solution)/shard_map/scatter-add | solution.py:412
  417.7 6.7 convert_element_type.89
  424.8 3.7 pad_maximum_fusion
  428.6 63.8 %reduce-scatter.5.cloned.1.call-done = bf16[144,512]{1,0:T(8,128)(2,1)} async-done(((bf16[4608,512]{1,0:T(8,128)(2,1)}), bf16[144,512]{1,0:T(8,128)(2,1)}) %reduce-scatter.5.cloned.1.call-update) | async-done | bytes 147472 | tf_op jit(solution)/shard_map/reduce_scatter | solution.py:456
  492.4 112.4 %reduce-scatter.7.cloned.1.call-done = bf16[144,512]{1,0:T(8,128)(2,1)} async-done(((bf16[4608,512]{1,0:T(8,128)(2,1)}), bf16[144,512]{1,0:T(8,128)(2,1)}) %reduce-scatter.7.cloned.1.call-update) | async-done | bytes 147472 | tf_op jit(solution)/shard_map/reduce_scatter | solution.py:456
  604.8 111.4 %reduce-scatter.9.cloned.1.call-done = bf16[144,512]{1,0:T(8,128)(2,1)} async-done(((bf16[4608,512]{1,0:T(8,128)(2,1)}), bf16[144,512]{1,0:T(8,128)(2,1)}) %reduce-scatter.9.cloned.1.call-update) | async-done | bytes 147472 | tf_op jit(solution)/shard_map/reduce_scatter | solution.py:456
  716.2 1.9 pad_maximum_fusion.1
  722.9 2.9 multiply_reduce_fusion.1
  731.9 42.1 %all-reduce.2 = (f32[]{:T(128)}, f32[4,512]{1,0:T(4,128)}) all-reduce(f32[]{:T(128)S(6)} %add.167, f32[4,512]{1,0:T(4,128)} %pad_maximum_fusion.3), channel_id=1, replica_groups=mesh['rows'=4,'batch'=8] {'batch','rows'}, use_global_device_ids=true, to_apply=%region_3.4 | all-reduce | flops 2049 | bytes 16392 | tf_op jit(solution)/shard_map/psum | solution.py:483
  774.0 1.9 multiply_reduce_fusion.5
  776.6 90.8 %reduce-scatter.11.cloned.1.call-done = bf16[536,256]{1,0:T(8,128)(2,1)} async-done(((bf16[17152,256]{1,0:T(8,128)(2,1)}), bf16[536,256]{1,0:T(8,128)(2,1)}) %reduce-scatter.11.cloned.1.call-update) | async-done | bytes 274448 | tf_op jit(solution)/shard_map/reduce_scatter | solution.py:456
  868.8 17.5 %all-gather.17.cloned.1.call-done = bf16[12,144,512]{2,1,0:T(8,128)(2,1)} async-done(((bf16[3,144,512]{2,1,0:T(8,128)(2,1)}), bf16[12,144,512]{2,1,0:T(8,128)(2,1)}) %all-gather.17.cloned.1.call-update) | async-done | bytes 1769488 | tf_op jit(solution)/shard_map/all_gather | solution.py:459
  886.3 2.0 add_reduce_fusion.1
  890.4 1.9 fusion.27
  894.4 2.1 convert_bitcast_fusion
  896.5 2.2 copy.178
  900.1 4.8 all-gather.19.cloned.1.call-done
  906.4 2.7 slice.57
  911.8 2.4 add_reduce_fusion.2
  928.6 2.5 fusion.6
  931.1 38.5 %all-reduce.3 = (f32[3,512]{1,0:T(4,128)}, f32[3]{0:T(128)}, f32[3,512]{1,0:T(4,128)}, f32[3]{0:T(128)}, f32[1,256]{1,0:T(1,128)}, /*index=5*/f32[1]{0:T(128)}, ...) all-reduce(f32[3,512]{1,0:T(4,128)} %get-tuple-element.223, ...), channel_id=1, replica_groups=mesh['rows'=4,'batch'=8] {'batch'}, use_global_device_ids=true, to_apply=%region_10.11 | all-reduce | flops 4132 | bytes 33056 | tf_op jit(solution)/shard_map/psum | solution.py:482
  972.3 1.9 divide_reduce_fusion.2
  986.3 4.6 fusion.21
  990.9 2.9 fusion.23
  (137 shorter events, 71.4 us)
Async XLA Ops:
  7.2 6.2 copy-start.11
  7.2 11.3 %copy-start.12 = (s32[32,2,8,4]{0,3,2,1:T(4,128)S(1)}, s32[32,2,8,4]{0,3,2,1:T(4,128)}, u32[]{:S(2)}) copy-start(s32[32,2,8,4]{0,3,2,1:T(4,128)} %param.21) | copy-start | bytes 24580
  7.2 18.4 %copy-start.8 = (f32[32,2,8,12]{0,2,3,1:T(8,128)S(1)}, f32[32,2,8,12]{0,2,3,1:T(8,128)}, u32[]{:S(2)}) copy-start(f32[32,2,8,12]{0,2,3,1:T(8,128)} %param.19) | copy-start | bytes 73732
  7.2 79.0 %all-gather.13.cloned.1.call-start = ((), (), s32[]{:S(2)}) async-start(), calls=%async_computation.13 | async-start | bytes 4866048 | tf_op jit(solution)/shard_map/all_gather | solution.py:350
  9.2 158.3 %all-gather.11.cloned.1.call-start = ((), (), s32[]{:S(2)}) async-start(), calls=%async_computation.12 | async-start | bytes 9056256 | tf_op jit(solution)/shard_map/all_gather | solution.py:354
  12.6 239.1 %all-gather.15.cloned.1.call-start = ((), (), s32[]{:S(2)}) async-start(), calls=%async_computation.14 | async-start | bytes 9732096 | tf_op jit(solution)/shard_map/all_gather | solution.py:351
  14.3 8.0 all-to-all-start
  22.3 7.0 all-to-all-start.1
  35.6 38.8 %all-to-all-start.3 = ((bf16[32,4,16,512]{3,2,1,0:T(8,128)(2,1)}), bf16[32,4,16,512]{3,2,1,0:T(8,128)(2,1)S(1)}, u32[]{:S(2)}, u32[]{:S(2)}) async-start(bf16[32,4,16,512]{3,2,1,0:T(8,128)(2,1)} %param.18), calls=%async_computation.3 | async-start | bytes 4194304 | tf_op jit(solution)/shard_map/all_to_all | solution.py:338
  39.2 453.2 %reduce-scatter.5.cloned.1.call-start = ((), (), s32[]{:S(2)}) async-start(), calls=%async_computation.8 | async-start | bytes 4866048 | tf_op jit(solution)/shard_map/reduce_scatter | solution.py:456
  266.3 23.8 %copy-start.6 = (bf16[1,32,144,512]{3,2,1,0:T(8,128)(2,1)}, bf16[1,32,144,512]{3,2,1,0:T(8,128)(2,1)S(1)}, u32[]{:S(2)}) copy-start(bf16[1,32,144,512]{3,2,1,0:T(8,128)(2,1)S(1)} %get-tuple-element.267) | copy-start | bytes 14155780
  290.2 5.4 copy-start.5
  296.9 2.8 copy-start.7
  386.7 218.1 %reduce-scatter.7.cloned.1.call-start = ((), (), s32[]{:S(2)}) async-start(), calls=%async_computation.9 | async-start | bytes 4866048 | tf_op jit(solution)/shard_map/reduce_scatter | solution.py:456
  387.3 328.9 %reduce-scatter.9.cloned.1.call-start = ((), (), s32[]{:S(2)}) async-start(), calls=%async_computation.10 | async-start | bytes 4866048 | tf_op jit(solution)/shard_map/reduce_scatter | solution.py:456
  387.9 479.6 %reduce-scatter.11.cloned.1.call-start = ((), (), s32[]{:S(2)}) async-start(), calls=%async_computation.11 | async-start | bytes 9056256 | tf_op jit(solution)/shard_map/reduce_scatter | solution.py:456
  428.5 299.7 %copy-start = (f32[576,3,512]{2,0,1:T(8,128)S(1)}, f32[576,3,512]{2,0,1:T(8,128)}, u32[]{:S(2)}) copy-start(f32[576,3,512]{2,0,1:T(8,128)} %param.22) | copy-start | bytes 10616836
  428.6 457.8 %all-gather.17.cloned.1.call-start = ((), (), s32[]{:S(2)}) async-start(), calls=%async_computation.15 | async-start | bytes 2211840 | tf_op jit(solution)/shard_map/all_gather | solution.py:459
  718.1 186.8 %all-gather.19.cloned.1.call-start = ((), (), s32[]{:S(2)}) async-start(), calls=%async_computation.16 | async-start | bytes 1372160 | tf_op jit(solution)/shard_map/all_gather | solution.py:459
  896.5 2.2 copy-start.1
  904.9 4.2 copy-start.3
  909.3 2.5 copy-start.4
  917.4 0.5 copy-start.15
  925.1 2.8 copy-start.14
  928.0 0.6 copy-start.10
  978.2 2.2 copy-start.16
  983.9 7.0 copy-start.13
  986.3 4.6 copy-start.2
  986.3 4.6 copy-start.9
Sparse Core Ops, SparseCore 0:
  11.5 74.6 all-gather.12
  89.6 77.8 all-gather.10
  171.0 80.6 all-gather.14
  386.8 105.5 reduce-scatter.4
  498.7 106.0 reduce-scatter.6
  610.1 106.0 reduce-scatter.8
  718.6 148.7 reduce-scatter.10
  869.6 16.6 all-gather.16
  887.9 16.9 all-gather.18
where the time goes:
time: 1000 us
  waiting for transfers between devices  570 us (57%)
  Pallas kernels  131 us (13%)
  other arithmetic  92.4 us (9%)
  blocking collectives  86.9 us (9%)
  local copies, waits for them, and re-layouts  75.1 us (8%)
  between operations  23 us (2%)
  starting transfers between devices  11.4 us (1%)
  matrix products  10.7 us (1%)
    reduce_scatter x4, waiting for transfers between devices, to_owner(): return lax.psum_scatter(v, BOTH, scatter_dimension=0, tiled=True)  378 us
    pallas_call x5, Pallas kernels, kernel_call(): pl.pallas_call(body, out_shape=outs, in_specs=[VM] * len(args), out_specs...  131 us
    all_gather x1, waiting for transfers between devices, local(): later = lax.all_gather(conv_piece[1:], BOTH, axis=0)  62.5 us
    all_gather x1, waiting for transfers between devices, local(): rest = lax.all_gather(rest_piece, BOTH, axis=0)  60.4 us
    psum x1, blocking collectives, local(): loss, g_gain = lax.psum((recon_part + quant_part, d_gains), BOTH)  42.1 us
    psum x1, blocking collectives, local(): sums = lax.psum([r[1:] + (w,) for r, w in zip(rows_new, wt_sq)], 'batch')  38.5 us
    all_to_all x3, waiting for transfers between devices, whole_crops(): return lax.all_to_all(v, 'rows', split_axis=0, concat_axis=1, tiled=True)  35.1 us
    all_gather x2, waiting for transfers between devices, to_rows(): return lax.all_gather(v, 'rows', axis=0)  22.3 us
  transfers between devices with their start and end apart: 12, of which 12 were waited for; matrix products, arithmetic and copies ran while one was open for 11% of the time, Pallas kernels for 2%

commit v1 on v0

--- a/solution.py
+++ b/solution.py
@@ -17,6 +17,8 @@
 BOTH = ("batch", "rows")
 MIB = 1 << 20
 VM = pl.BlockSpec(memory_space=pltpu.VMEM)
+ANY = pl.BlockSpec(memory_space=pl.ANY)
+MESH = pl.DeviceIdType.MESH
 
 
 def group_sum(v):
@@ -119,47 +121,78 @@
     return h * jax.nn.sigmoid(h)
 
 
+def first_crop(v, gains_ref, w_ref, a3):
+    mean, rstd = moments(v)
+    a = silu((v - mean) * rstd * gains_ref[0:1, :] + gains_ref[1:2, :])
+    fill_three(a3, shifted(a, 1), a, shifted(a, -1))
+    return a.astype(BF), conv_rows(a3, w_ref)
+
+
+def second_crop(v, x, gains_ref, w_ref, l_ref, a3, y32):
+    ch = v.shape[1]
+    mean, rstd = moments(v)
+    a = silu((v - mean) * rstd * gains_ref[2:3, :] + gains_ref[3:4, :])
+    fill_three(a3, shifted(a, 1), a, shifted(a, -1))
+    put_lanes(y32, slice(None), conv_rows(a3, w_ref) + x)
+    even = get_lanes(y32, pl.ds(0, 128, stride=2))
+    odd = get_lanes(y32, pl.ds(1, 128, stride=2))
+    cell = lax.broadcasted_iota(jnp.int32, odd.shape, 0) & 7
+    before = jnp.where(cell == 0, 0.0, pltpu.roll(odd, 1, 0))
+    for dx, part in enumerate((before, even, odd)):
+        part = part.reshape(8, 2, 8, ch)
+        upper = part[:, 0].reshape(64, ch)
+        lower = part[:, 1].reshape(64, ch)
+        above = jnp.concatenate([jnp.zeros((8, ch), F32), lower[:56]], axis=0)
+        for dy, rows in enumerate((above, upper, lower)):
+            lane = (dy * 3 + dx) * ch
+            l_ref[:, lane : lane + ch] = rows.astype(BF)
+    return a.astype(BF)
+
+
+def down_dot(l_ref, w_ref, s_ref):
+    ch = s_ref.shape[1]
+    nb = 256
+
+    def block(j, carry):
+        lane = pl.ds(pl.multiple_of(j * nb, nb), nb)
+        d = jnp.dot(l_ref[...], w_ref[:, lane], preferred_element_type=F32)
+        s_ref[:, lane] = d.astype(BF)
+        return carry
+
+    lax.fori_loop(0, ch // nb, block, 0)
+
+
+def crop_rows(i):
+    return pl.ds(pl.multiple_of(i * 64, 64), 64)
+
+
 def first_conv_kernel(x_ref, gains_ref, w_ref, a_ref, c_ref, a3):
     zero_edges(a3)
 
     def crop(i, carry):
-        v = x_ref[i].astype(F32)
-        mean, rstd = moments(v)
-        a = silu((v - mean) * rstd * gains_ref[0:1, :] + gains_ref[1:2, :])
-        a_ref[i] = a.astype(BF)
-        fill_three(a3, shifted(a, 1), a, shifted(a, -1))
-        c_ref[i] = conv_rows(a3, w_ref)
+        a_ref[i], c_ref[i] = first_crop(x_ref[i].astype(F32), gains_ref, w_ref, a3)
         return carry
 
     lax.fori_loop(0, x_ref.shape[0], crop, 0)
 
 
-def second_conv_kernel(c_in_ref, x_ref, gains_ref, w_ref, a_ref, l_ref, a3, y32):
+def second_conv_kernel(c_in_ref, x_ref, gains_ref, w_ref, w_down_ref, a_ref, l_ref, s_ref, a3, y32):
     zero_edges(a3)
-    ch = x_ref.shape[2]
 
     def crop(i, carry):
-        v = c_in_ref[i]
-        mean, rstd = moments(v)
-        a = silu((v - mean) * rstd * gains_ref[2:3, :] + gains_ref[3:4, :])
-        a_ref[i] = a.astype(BF)
-        fill_three(a3, shifted(a, 1), a, shifted(a, -1))
-        put_lanes(y32, slice(None), conv_rows(a3, w_ref) + x_ref[i].astype(F32))
-        even = get_lanes(y32, pl.ds(0, 128, stride=2))
-        odd = get_lanes(y32, pl.ds(1, 128, stride=2))
-        cell = lax.broadcasted_iota(jnp.int32, odd.shape, 0) & 7
-        before = jnp.where(cell == 0, 0.0, pltpu.roll(odd, 1, 0))
-        for dx, part in enumerate((before, even, odd)):
-            part = part.reshape(8, 2, 8, ch)
-            upper = part[:, 0].reshape(64, ch)
-            lower = part[:, 1].reshape(64, ch)
-            above = jnp.concatenate([jnp.zeros((8, ch), F32), lower[:56]], axis=0)
-            for dy, rows in enumerate((above, upper, lower)):
-                lane = (dy * 3 + dx) * ch
-                l_ref[pl.ds(pl.multiple_of(i * 64, 64), 64), lane : lane + ch] = rows.astype(BF)
+        a_ref[i] = second_crop(
+            c_in_ref[i],
+            x_ref[i].astype(F32),
+            gains_ref,
+            w_ref,
+            l_ref.at[crop_rows(i)],
+            a3,
+            y32,
+        )
         return carry
 
     lax.fori_loop(0, x_ref.shape[0], crop, 0)
+    down_dot(l_ref, w_down_ref, s_ref)
 
 
 def down_back_kernel(ds_ref, l_ref, w_ref, dc_ref, dw_ref, y32):
@@ -269,6 +302,544 @@
             flops=flops, bytes_accessed=bytes_accessed, transcendentals=0
         ),
     )(*args)
+
+
+class Place:
+    def __init__(self):
+        rows, batch = lax.axis_index("rows"), lax.axis_index("batch")
+        self.x, self.c = rows // 2, rows % 2
+        self.z, self.y = batch // 2, batch % 2
+        self.part = self.c * 2 + self.x
+
+    def at(self, x=None, c=None, z=None, y=None):
+        x = self.x if x is None else x
+        c = self.c if c is None else c
+        z = self.z if z is None else z
+        y = self.y if y is None else y
+        return {"rows": 2 * x + c, "batch": 2 * z + y}
+
+    def row_peers(self):
+        return [
+            self.at(c=1 - self.c),
+            self.at(x=1 - self.x),
+            self.at(x=1 - self.x, c=1 - self.c),
+        ]
+
+    def z_peers(self):
+        return [self.at(z=(self.z + d) % 4) for d in (1, 2, 3)]
+
+    def greet(self):
+        barrier = pltpu.get_barrier_semaphore()
+        peers = self.row_peers() + self.z_peers() + [self.at(y=1 - self.y)]
+        for peer in peers:
+            pl.semaphore_signal(barrier, inc=1, device_id=peer, device_id_type=MESH)
+        pl.semaphore_wait(barrier, len(peers))
+
+
+def remote(src, dst, send, recv, peer):
+    return pltpu.make_async_remote_copy(
+        src_ref=src, dst_ref=dst, send_sem=send, recv_sem=recv, device_id=peer, device_id_type=MESH
+    )
+
+
+class Gather:
+    def __init__(self, place, src, dst, send, recv, by_x):
+        self.p, self.src, self.dst, self.send, self.recv = place, src, dst, send, recv
+        self.by_x = by_x
+        self.steps = 4 if by_x else 3
+
+    def copies(self, step):
+        p, src, dst, send, recv = self.p, self.src, self.dst, self.send, self.recv
+        if step == 0:
+            mine = (p.c, p.x) if self.by_x else (p.c,)
+            here, there = src.at[mine], dst.at[(p.z, p.y) + mine]
+            out = [
+                remote(here, there, send.at[k], recv.at[k], q) for k, q in enumerate(p.z_peers())
+            ]
+            return out + [pltpu.make_async_copy(here, there, recv.at[6])]
+        if step == 1:
+            part = dst.at[:, p.y, p.c, p.x] if self.by_x else dst.at[:, p.y, p.c]
+            return [remote(part, part, send.at[3], recv.at[3], p.at(y=1 - p.y))]
+        if step == 2 and self.by_x:
+            part = dst.at[:, :, p.c, p.x]
+            return [remote(part, part, send.at[4], recv.at[4], p.at(x=1 - p.x))]
+        part = dst.at[:, :, p.c]
+        return [remote(part, part, send.at[5], recv.at[5], p.at(c=1 - p.c))]
+
+    def start(self, step):
+        for copy in self.copies(step):
+            copy.start()
+
+    def arrive(self, step):
+        for copy in self.copies(step):
+            copy.wait_recv()
+
+    def go(self, step):
+        self.arrive(step - 1)
+        self.start(step)
+
+    def finish(self):
+        for step in range(self.steps):
+            for copy in self.copies(step):
+                if copy.is_remote:
+                    copy.wait_send()
+
+
+class Reduce:
+    steps = 5
+
+    def __init__(self, place, src, out, mine, one, two, three, four, send, recv):
+        self.p, self.src, self.out = place, src, out
+        self.mine, self.one, self.two, self.three, self.four = mine, one, two, three, four
+        self.send, self.recv = send, recv
+        first_x = place.c == 0
+        self.f = jnp.where(first_x, place.x, place.y)
+        self.g = jnp.where(first_x, place.y, place.x)
+        self.f_peer = place.at(
+            x=jnp.where(first_x, 1 - place.x, place.x), y=jnp.where(first_x, place.y, 1 - place.y)
+        )
+        self.g_peer = place.at(
+            x=jnp.where(first_x, place.x, 1 - place.x), y=jnp.where(first_x, 1 - place.y, place.y)
+        )
+        self.slot = 2 * self.f + self.g
+
+    @staticmethod
+    def scratch(rows, lanes):
+        def buf(*lead):
+            return pltpu.VMEM(lead + (rows, lanes), BF)
+
+        return [
+            buf(4, 4),
+            buf(4, 4),
+            buf(2, 4),
+            buf(4),
+            buf(3),
+            pltpu.SemaphoreType.DMA((12,)),
+            pltpu.SemaphoreType.DMA((16,)),
+        ]
+
+    def copies(self, step):
+        p, src, mine = self.p, self.src, self.mine
+        if step == 0:
+            out = []
+            for k in range(4):
+                y, x = k // 2, k % 2
+                there = jnp.where(p.c == 1, 2 * x + y, 2 * y + x)
+                here = jnp.where(p.c == 0, 2 * x + y, 2 * y + x)
+                out.append(
+                    remote(
+                        src.at[:, y, 1 - p.c, x],
+                        self.one.at[there],
+                        self.send.at[k],
+                        self.recv.at[k],
+                        p.at(c=1 - p.c),
+                    )
+                )
+                out.append(
+                    pltpu.make_async_copy(src.at[:, y, p.c, x], mine.at[here], self.recv.at[12 + k])
+                )
+            return out
+        if step == 1:
+            return [
+                remote(
+                    mine.at[pl.ds(2 * (1 - self.f), 2)],
+                    self.two,
+                    self.send.at[4],
+                    self.recv.at[4],
+                    self.f_peer,
+                )
+            ]
+        if step == 2:
+            return [
+                remote(
+                    mine.at[2 * self.f + 1 - self.g],
+                    self.three,
+                    self.send.at[5],
+                    self.recv.at[5],
+                    self.g_peer,
+                )
+            ]
+        if step == 3:
+            return [
+                remote(
+                    mine.at[self.slot, (p.z + d) % 4],
+                    self.four.at[d - 1],
+                    self.send.at[5 + d],
+                    self.recv.at[5 + d],
+                    peer,
+                )
+                for d, peer in zip((1, 2, 3), p.z_peers())
+            ]
+        return [
+            remote(
+                self.out.at[p.part], self.out.at[p.part], self.send.at[9 + k], self.recv.at[9 + k], q
+            )
+            for k, q in enumerate(p.row_peers())
+        ]
+
+    def start(self, step):
+        for copy in self.copies(step):
+            copy.start()
+
+    def arrive(self, step):
+        p, mine = self.p, self.mine
+        for copy in self.copies(step):
+            copy.wait_recv()
+
+        def add(dst, src):
+            dst[...] = (dst[...].astype(F32) + src[...].astype(F32)).astype(BF)
+
+        if step == 0:
+
+            def body(i, carry):
+                add(mine.at[i // 4, i % 4], self.one.at[i // 4, i % 4])
+                return carry
+
+            lax.fori_loop(0, 16, body, 0)
+        if step == 1:
+
+            def body(i, carry):
+                add(mine.at[2 * self.f + i // 4, i % 4], self.two.at[i // 4, i % 4])
+                return carry
+
+            lax.fori_loop(0, 8, body, 0)
+        if step == 2:
+
+            def body(i, carry):
+                add(mine.at[self.slot, i], self.three.at[i])
+                return carry
+
+            lax.fori_loop(0, 4, body, 0)
+        if step == 3:
+            total = mine[self.slot, p.z].astype(F32)
+            for d in range(3):
+                total = total + self.four[d].astype(F32)
+            self.out[p.part] = total.astype(BF)
+
+    def end(self):
+        for step in range(self.steps):
+            for copy in self.copies(step):
+                if copy.is_remote:
+                    copy.wait_send()
+
+
+def forward_kernel(
+    feat,
+    side,
+    w_mine,
+    rest_mine,
+    gains_ref,
+    x_out,
+    side_out,
+    w_out0,
+    w_out1,
+    w_out2,
+    rest_out,
+    a_one_ref,
+    c_one_ref,
+    a_two_ref,
+    l_ref,
+    s_ref,
+    xv,
+    wv0,
+    wv1,
+    wv2,
+    a3,
+    y32,
+    x_send,
+    x_recv,
+    g_send,
+    g_recv,
+    o_sem,
+):
+    place = Place()
+    rank = 2 * place.x + place.c
+    place.greet()
+
+    def view(ref, lanes):
+        n = ref.shape[0] // 32
+        return ref.reshape(4, 2, 2, 2, n, ref.shape[1]).at[..., lanes]
+
+    def job(k, src, dst, by_x):
+        return Gather(place, src, dst, g_send.at[k], g_recv.at[k], by_x)
+
+    halves = [slice(0, 256), slice(256, 512)]
+    w0 = [job(k, w_mine.at[0, ..., h], view(wv0, h), False) for k, h in enumerate(halves)]
+    w1 = [job(2 + k, w_mine.at[1, ..., h], view(wv1, h), False) for k, h in enumerate(halves)]
+    w2 = [job(4 + k, w_mine.at[2, ..., h], view(wv2, h), True) for k, h in enumerate(halves)]
+    ends = [slice(0, 128), slice(128, 256)]
+    rest = [
+        job(6 + k, rest_mine.at[..., h], rest_out.at[..., h], k == 0) for k, h in enumerate(ends)
+    ]
+
+    cells = []
+    for src, dst, base in ((feat, xv, 0), (side, side_out, 4)):
+        for k, q in enumerate(place.row_peers()):
+            to = q["rows"]
+            cells.append(
+                remote(src.at[to], dst.at[:, rank], x_send.at[base + k], x_recv.at[base + k], q)
+            )
+        cells.append(pltpu.make_async_copy(src.at[rank], dst.at[:, rank], x_recv.at[base + 3]))
+
+    w0[0].start(0)
+    for copy in cells:
+        copy.start()
+    w0[1].start(0)
+    w0[0].go(1)
+    w0[1].arrive(0)
+    w1[0].start(0)
+    rest[0].start(0)
+    w0[0].go(2)
+    w0[1].start(1)
+    w0[0].arrive(2)
+    w0[1].go(2)
+    zero_edges(a3)
+    for copy in cells:
+        copy.wait_recv()
+    keep_x = pltpu.make_async_copy(xv, x_out, o_sem.at[0])
+    keep_x.start()
+    w0[1].arrive(2)
+    keep_w = [
+        pltpu.make_async_copy(v, o, o_sem.at[1 + k])
+        for k, (v, o) in enumerate(((wv0, w_out0), (wv1, w_out1), (wv2, w_out2)))
+    ]
+    keep_w[0].start()
+    count, _, _, ch = xv.shape
+
+    def crop_x(i):
+        return xv[i].reshape(256, ch).astype(F32)
+
+    def first(i, carry):
+        @pl.when(i == 1)
+        def _():
+            w1[0].go(1)
+            w1[1].start(0)
+
+        @pl.when(i == 2)
+        def _():
+            rest[0].go(1)
+            w2[0].start(0)
+
+        @pl.when(i == 5)
+        def _():
+            w1[0].go(2)
+            w1[1].go(1)
+            rest[0].go(2)
+            w2[1].start(0)
+
+        @pl.when(i == 7)
+        def _():
+            w2[0].go(1)
+
+        a_one_ref[i], c_one_ref[i] = first_crop(crop_x(i), gains_ref, wv0, a3)
+        return carry
+
+    lax.fori_loop(0, count, first, 0)
+    w1[0].arrive(2)
+    rest[1].start(0)
+    w1[1].go(2)
+    w1[1].arrive(2)
+    keep_w[1].start()
+
+    def second(i, carry):
+        @pl.when(i == 0)
+        def _():
+            w2[0].go(2)
+            w2[1].go(1)
+
+        @pl.when(i == 2)
+        def _():
+            w2[1].go(2)
+            rest[0].go(3)
+
+        @pl.when(i == 3)
+        def _():
+            rest[1].go(1)
+
+        @pl.when(i == 5)
+        def _():
+            w2[0].go(3)
+
+        @pl.when(i == 7)
+        def _():
+            w2[1].go(3)
+
+        a_two_ref[i] = second_crop(
+            c_one_ref[i], crop_x(i), gains_ref, wv1, l_ref.at[crop_rows(i)], a3, y32
+        )
+        return carry
+
+    lax.fori_loop(0, count, second, 0)
+    rest[1].go(2)
+    w2[0].arrive(3)
+    w2[1].arrive(3)
+    keep_w[2].start()
+    down_dot(l_ref, wv2, s_ref)
+    for part in (w0, w1, w2):
+        for g in part:
+            g.finish()
+    for g in rest:
+        g.arrive(g.steps - 1)
+        g.finish()
+    for copy in cells:
+        if copy.is_remote:
+            copy.wait_send()
+    keep_x.wait()
+    for copy in keep_w:
+        copy.wait()
+
+
+def forward_call(feat, side, w_mine, rest_mine, gains):
+    ranks, crops, cells, ch = feat.shape
+    lat_cells = crops * ranks * cells // 4
+    whole = 8 * w_mine.shape[1] * w_mine.shape[2] * w_mine.shape[3]
+
+    def shape(*dims, dtype=BF):
+        return jax.ShapeDtypeStruct(dims, dtype)
+
+    outs = [
+        shape(crops, ranks, cells, ch),
+        shape(crops, ranks, *side.shape[2:], dtype=F32),
+        shape(whole, ch),
+        shape(whole, ch),
+        shape(whole, ch),
+        shape(4, 2, *rest_mine.shape),
+        shape(crops, ranks * cells, ch),
+        shape(crops, ranks * cells, ch, dtype=F32),
+        shape(crops, ranks * cells, ch),
+        shape(lat_cells, 9 * ch),
+        shape(lat_cells, ch),
+    ]
+    return pl.pallas_call(
+        forward_kernel,
+        out_shape=outs,
+        in_specs=[ANY] * 4 + [VM],
+        out_specs=[ANY] * 6 + [VM] * 5,
+        scratch_shapes=[pltpu.VMEM((crops, ranks, cells, ch), BF)]
+        + [pltpu.VMEM((whole, ch), BF)] * 3
+        + [
+            pltpu.VMEM((18, 16, 3 * ch), BF),
+            pltpu.VMEM((ch // 128, ranks * cells, 128), F32),
+            pltpu.SemaphoreType.DMA((8,)),
+            pltpu.SemaphoreType.DMA((8,)),
+            pltpu.SemaphoreType.DMA((8, 8)),
+            pltpu.SemaphoreType.DMA((8, 8)),
+            pltpu.SemaphoreType.DMA((4,)),
+        ],
+        compiler_params=pltpu.CompilerParams(
+            vmem_limit_bytes=58 * MIB, collective_id=2, has_side_effects=True
+        ),
+        cost_estimate=pl.CostEstimate(
+            flops=45 * crops * ranks * cells * ch * ch,
+            bytes_accessed=0,
+            transcendentals=0,
+        ),
+    )(feat, side, w_mine, rest_mine, gains)
+
+
+def reduce_kernel(parts, *refs):
+    n_code, n_proj, n_head, rgb = parts
+    sources, refs = refs[:4], refs[4:]
+    vec_ref, conv_row_ref, rest_row_ref, refs = refs[0], refs[1], refs[2], refs[3:]
+    g_refs, refs = refs[:4], refs[4:]
+    conv_new_ref, rest_new_ref, tv_ref, refs = refs[0], refs[1], refs[2], refs[3:]
+    vec_in, tv_in, s_send, s_recv, refs = refs[0], refs[1], refs[2], refs[3], refs[4:]
+    place = Place()
+    per = len(refs) // 4
+    jobs = [
+        Reduce(place, sources[k], g_refs[k], *refs[k * per : (k + 1) * per]) for k in (3, 2, 1, 0)
+    ]
+    place.greet()
+    small = [
+        remote(vec_ref, vec_in.at[k], s_send.at[k], s_recv.at[k], q)
+        for k, q in enumerate(place.row_peers())
+    ]
+    for copy in small:
+        copy.start()
+    for job in jobs:
+        job.start(0)
+    for tick in range(len(jobs) + Reduce.steps - 1):
+        for k, job in enumerate(jobs):
+            step = tick - k
+            if 0 <= step < Reduce.steps:
+                job.arrive(step)
+                if step + 1 < Reduce.steps:
+                    job.start(step + 1)
+    for copy in small:
+        copy.wait_recv()
+    tv_ref[...] = jnp.zeros_like(tv_ref)
+    tv_ref[16:24, :] = vec_ref[...] + vec_in[0] + vec_in[1] + vec_in[2]
+    ch = tv_ref.shape[1]
+
+    def fold(g, row, width):
+        sq = g * g
+        new = 0.5 * row + 0.5 * (jnp.sum(sq, axis=1, keepdims=True) / width + EPS_SQ)
+        return (
+            new,
+            jnp.sum(sq, axis=0, keepdims=True),
+            jnp.sum(sq / new, axis=0, keepdims=True),
+            jnp.sum(new, axis=0, keepdims=True),
+        )
+
+    for j in range(3):
+        for k in range(4):
+            g = g_refs[j][k].astype(F32)
+            new, col, over, total = fold(g, conv_row_ref[j, k], ch)
+            conv_new_ref[j, k] = new
+            tv_ref[j : j + 1, :] += col
+            tv_ref[3 + j : 4 + j, :] += over
+            tv_ref[6 + j : 7 + j, :] += total
+    half = ch // 2
+    spans = ((0, n_code, half), (n_code, n_proj, half), (n_code + n_proj, n_head, rgb))
+    for k in range(4):
+        for m, (low, size, width) in enumerate(spans):
+            g = g_refs[3][k, low : low + size].astype(F32)
+            new, col, over, total = fold(g, rest_row_ref[k, low : low + size], width)
+            rest_new_ref[k, low : low + size] = new
+            tv_ref[9 + m : 10 + m, :half] += col
+            tv_ref[9 + m : 10 + m, half:] += over
+            tv_ref[12 + m : 13 + m, :half] += total
+    sends = [
+        remote(tv_ref, tv_in.at[k], s_send.at[3 + k], s_recv.at[3 + k], q)
+        for k, q in enumerate(
+            (place.at(y=1 - place.y), place.at(z=place.z ^ 1), place.at(z=place.z ^ 2))
+        )
+    ]
+    for k, copy in enumerate(sends):
+        copy.start()
+        copy.wait()
+        tv_ref[...] += tv_in[k]
+    for copy in small:
+        copy.wait_send()
+    for job in jobs:
+        job.end()
+
+
+def reduce_call(sources, vec, conv_row, rest_row, parts):
+    scratch = [
+        pltpu.VMEM((3,) + vec.shape, F32),
+        pltpu.VMEM((3, 24, vec.shape[1]), F32),
+        pltpu.SemaphoreType.DMA((6,)),
+        pltpu.SemaphoreType.DMA((6,)),
+    ]
+    for s in sources:
+        scratch += Reduce.scratch(*s.shape[-2:])
+    outs = [jax.ShapeDtypeStruct((4,) + s.shape[-2:], BF) for s in sources]
+    outs += [jax.ShapeDtypeStruct(v.shape, F32) for v in (conv_row, rest_row)]
+    outs += [jax.ShapeDtypeStruct((24, vec.shape[1]), F32)]
+    return pl.pallas_call(
+        functools.partial(reduce_kernel, parts),
+        out_shape=outs,
+        in_specs=[ANY] * len(sources) + [VM] * 3,
+        out_specs=[VM] * len(outs),
+        scratch_shapes=scratch,
+        compiler_params=pltpu.CompilerParams(
+            vmem_limit_bytes=56 * MIB, collective_id=1, has_side_effects=True
+        ),
+        cost_estimate=pl.CostEstimate(
+            flops=0, bytes_accessed=sum(s.size * 2 for s in sources), transcendentals=0
+        ),
+    )(*sources, vec, conv_row, rest_row)
 
 
 def contract_last(left, right):
@@ -326,6 +897,7 @@
 ):
     ranks = lax.axis_size("rows")
     shards = lax.axis_size("batch")
+    fast = (ranks, shards) == (4, 8)
     me = lax.axis_index("rows")
     crops_all = features.shape[0] * shards
     ch = features.shape[3]
@@ -341,31 +913,11 @@
         size = v.shape[0] // ranks
         return lax.dynamic_slice_in_dim(v, me * size, size, 0)
 
-    conv_piece = jnp.transpose(my_part(conv_w).astype(BF), (1, 0, 2))
+    n_code, n_proj, n_head = (v.shape[0] // ranks for v in (code_w, proj_w, head_w))
     head_wide = jnp.pad(head_w, ((0, 0), (0, lat - rgb)))
-    rest_piece = jnp.concatenate(
-        [my_part(code_w).astype(BF), my_part(proj_w).astype(BF), my_part(head_wide).astype(BF)]
-    )
-    n_code, n_proj, n_head = (v.shape[0] // ranks for v in (code_w, proj_w, head_w))
-    w_all = [lax.all_gather(conv_piece[0], BOTH, axis=0, tiled=True)]
-    later = lax.all_gather(conv_piece[1:], BOTH, axis=0)
-    later = jnp.transpose(later, (1, 0, 2, 3)).reshape(2, -1, ch)
-    w_all += [later[0], later[1]]
-    rest = lax.all_gather(rest_piece, BOTH, axis=0)
-    code_all = rest[:, :n_code].reshape(-1, lat)
-    proj_all = rest[:, n_code : n_code + n_proj].reshape(-1, lat)
-    head_all = rest[:, n_code + n_proj :, :rgb].reshape(-1, rgb)
-
-    x = whole_crops(features)
-    target, mask, codes = whole_crops(target), whole_crops(mask), whole_crops(codes)
-    crops = x.shape[0]
+    crops = features.shape[0] // ranks
     cells = height * width
-    x = x.reshape(crops, cells, ch)
     lat_cells = crops * cells // 4
-    target = target.reshape(lat_cells, rgb)
-    mask = mask.reshape(lat_cells, -1)
-    codes = codes.reshape(lat_cells, -1)
-
     conv_flops = 2 * crops * cells * 9 * ch * ch
     three = pltpu.VMEM((18, 16, 3 * ch), BF)
     fold = pltpu.VMEM((ch // 128, cells, 128), F32)
@@ -375,21 +927,72 @@
 
     dw_shape = jax.ShapeDtypeStruct((9 * ch, ch), BF)
     dg_shape = jax.ShapeDtypeStruct((2, ch), F32)
-
-    a_one, c_one = kernel_call(
-        first_conv_kernel, [big(BF), big(F32)], [three], conv_flops, x, gains, w_all[0]
-    )
-    a_two, windows = kernel_call(
-        second_conv_kernel,
-        [big(BF), jax.ShapeDtypeStruct((lat_cells, 9 * ch), BF)],
-        [three, fold],
-        conv_flops,
-        c_one,
-        x,
-        gains,
-        w_all[1],
-    )
-    s_low = contract_last(windows, w_all[2]).astype(BF)
+    wide_shape = jax.ShapeDtypeStruct((lat_cells, 9 * ch), BF)
+    s_shape = jax.ShapeDtypeStruct((lat_cells, ch), BF)
+
+    if fast:
+        w_mine = jnp.transpose(conv_w.astype(BF), (1, 0, 2)).reshape(3, 2, 2, -1, ch)
+        rest_piece = jnp.concatenate(
+            [v.astype(BF).reshape(ranks, -1, lat) for v in (code_w, proj_w, head_wide)]
+            + [jnp.zeros((ranks, 16 - n_head, lat), BF)],
+            axis=1,
+        )
+        side = jnp.concatenate(
+            [target, mask.astype(F32), codes.astype(F32)], axis=-1
+        ).reshape(ranks, crops, -1, rgb + 8)
+        out = forward_call(
+            features.reshape(ranks, crops, -1, ch),
+            side,
+            w_mine,
+            rest_piece.reshape(2, 2, -1, lat),
+            gains,
+        )
+        x = out[0].reshape(crops, cells, ch)
+        w_all = out[2:5]
+        rest = out[5].reshape(ranks * shards, -1, lat)
+        side = out[1].reshape(lat_cells, -1)
+        target, mask, codes = (side[:, :rgb], side[:, rgb : rgb + 4], side[:, rgb + 4 :])
+        codes = codes.astype(jnp.int32)
+        a_one, c_one, a_two, windows, s_low = out[6:]
+    else:
+
+        def whole_crops(v):
+            return lax.all_to_all(v, "rows", split_axis=0, concat_axis=1, tiled=True)
+
+        def my_part(v):
+            size = v.shape[0] // ranks
+            return lax.dynamic_slice_in_dim(v, me * size, size, 0)
+
+        conv_piece = jnp.transpose(my_part(conv_w).astype(BF), (1, 0, 2))
+        rest_piece = jnp.concatenate(
+            [my_part(code_w).astype(BF), my_part(proj_w).astype(BF), my_part(head_wide).astype(BF)]
+        )
+        w_all = [lax.all_gather(conv_piece[0], BOTH, axis=0, tiled=True)]
+        later = lax.all_gather(conv_piece[1:], BOTH, axis=0)
+        later = jnp.transpose(later, (1, 0, 2, 3)).reshape(2, -1, ch)
+        w_all += [later[0], later[1]]
+        rest = lax.all_gather(rest_piece, BOTH, axis=0)
+        x = whole_crops(features).reshape(crops, cells, ch)
+        target = whole_crops(target).reshape(lat_cells, rgb)
+        mask = whole_crops(mask).reshape(lat_cells, -1)
+        codes = whole_crops(codes).reshape(lat_cells, -1)
+        a_one, c_one = kernel_call(
+            first_conv_kernel, [big(BF), big(F32)], [three], conv_flops, x, gains, w_all[0]
+        )
+        a_two, windows, s_low = kernel_call(
+            second_conv_kernel,
+            [big(BF), wide_shape, s_shape],
+            [three, fold],
+            conv_flops,
+            c_one,
+            x,
+            gains,
+            w_all[1],
+            w_all[2],
+        )
+    code_all = rest[:, :n_code].reshape(-1, lat)
+    proj_all = rest[:, n_code : n_code + n_proj].reshape(-1, lat)
+    head_all = rest[:, n_code + n_proj : n_code + n_proj + n_head, :rgb].reshape(-1, rgb)
 
     lat_count = crops_all * cells // 4 * lat
     pix_count = crops_all * cells * 3
@@ -451,38 +1054,87 @@
     d_gains = jnp.concatenate([gain_one, gain_two], axis=0)
 
     devices = ranks * shards
-
-    def to_owner(v):
-        return lax.psum_scatter(v, BOTH, scatter_dimension=0, tiled=True)
-
-    def to_rows(v):
-        return lax.all_gather(v, "rows", axis=0)
-
     pad = jnp.pad(d_head, ((0, 0), (0, lat - rgb)))
-    rest_grad = jnp.concatenate(
-        [v.astype(BF).reshape(devices, -1, lat) for v in (d_code, d_proj, pad)], axis=1
-    )
-    rest_mine = to_owner(rest_grad.reshape(-1, lat))
-    conv_mine = [to_owner(v) for v in (d_first, d_second, d_down)]
-    rest_full = to_rows(rest_mine).astype(F32)
-    conv_full = to_rows(jnp.stack(conv_mine)).astype(F32)
-    g_conv = jnp.transpose(conv_full, (0, 2, 1, 3)).reshape(-1, 3, ch)
+    loss_part = recon_part + quant_part
+    mats_old = [
+        (conv_w, conv_row, conv_col),
+        (proj_w[:, None, :], proj_row[:, None], proj_col[None, :]),
+        (code_w[:, None, :], code_row[:, None], code_col[None, :]),
+        (head_w[:, None, :], head_row[:, None], head_col[None, :]),
+    ]
+    wt_sq = [jnp.sum(m[0] * m[0], axis=(0, 2)) for m in mats_old]
+    if fast:
+        packed = jnp.zeros((devices, 16 - n_head, lat), BF)
+        rest_grad = jnp.concatenate(
+            [v.astype(BF).reshape(devices, -1, lat) for v in (d_code, d_proj, pad)] + [packed],
+            axis=1,
+        )
+        sources = [d.reshape(4, 2, 2, 2, -1, ch) for d in (d_first, d_second, d_down)]
+        sources.append(rest_grad.reshape(4, 2, 2, 2, -1, lat))
+        quarter = jnp.concatenate(wt_sq) / 4
+        row5 = jnp.pad(jnp.concatenate([loss_part[None], quarter]), (0, ch - 1 - quarter.shape[0]))
+        vec = jnp.concatenate([d_gains, row5[None], jnp.zeros((3, ch), F32)])
+        conv_rows4 = jnp.transpose(conv_row).reshape(3, 4, -1, 1)
+        rest_rows4 = jnp.concatenate(
+            [v.reshape(4, -1) for v in (code_row, proj_row, head_row)]
+            + [jnp.ones((4, 16 - n_head), F32)],
+            axis=1,
+        )[:, :, None]
+        out = reduce_call(sources, vec, conv_rows4, rest_rows4, (n_code, n_proj, n_head, rgb))
+        conv_new_rows = jnp.transpose(out[4].reshape(3, -1))
+        rest_new = out[5][:, :, 0]
+        cuts = (n_code, n_code + n_proj, n_code + n_proj + n_head)
+        code_rn, proj_rn, head_rn = (
+            v.reshape(-1, 1) for v in jnp.split(rest_new, cuts, axis=1)[:3]
+        )
+        rows_one = [conv_new_rows, proj_rn, code_rn, head_rn]
+        tv = out[6]
+        loss = tv[20, 0]
+        g_gain = tv[16:20]
+        wt_all = tv[20, 1:7]
+        shard_rows = [m[0].shape[0] for m in mats_old]
+        eps = [EPS_SQ * n * shards for n in shard_rows]
+        sums = [
+            (tv[0:3] + eps[0], tv[6:9, 0], tv[3:6], wt_all[0:3]),
+            (tv[10:11, :lat] + eps[1], tv[13:14, 0], tv[10:11, lat:], wt_all[3:4]),
+            (tv[9:10, :lat] + eps[2], tv[12:13, 0], tv[9:10, lat:], wt_all[4:5]),
+            (tv[11:12, :rgb] + eps[3], tv[14:15, 0], tv[11:12, lat : lat + rgb], wt_all[5:6]),
+        ]
+        g_conv = jnp.transpose(
+            jnp.stack([v.reshape(-1, ch) for v in out[:3]]).astype(F32), (1, 0, 2)
+        )
+        rest_full = out[3].astype(F32)
+    else:
+
+        def to_owner(v):
+            return lax.psum_scatter(v, BOTH, scatter_dimension=0, tiled=True)
+
+        def to_rows(v):
+            return lax.all_gather(v, "rows", axis=0)
+
+        rest_grad = jnp.concatenate(
+            [v.astype(BF).reshape(devices, -1, lat) for v in (d_code, d_proj, pad)], axis=1
+        )
+        rest_mine = to_owner(rest_grad.reshape(-1, lat))
+        conv_mine = [to_owner(v) for v in (d_first, d_second, d_down)]
+        rest_full = to_rows(rest_mine).astype(F32)
+        conv_full = to_rows(jnp.stack(conv_mine)).astype(F32)
+        g_conv = jnp.transpose(conv_full, (0, 2, 1, 3)).reshape(-1, 3, ch)
+        loss, g_gain = lax.psum((loss_part, d_gains), BOTH)
+
     g_code = rest_full[:, :n_code].reshape(-1, lat)
     g_proj = rest_full[:, n_code : n_code + n_proj].reshape(-1, lat)
-    g_head = rest_full[:, n_code + n_proj :, :rgb].reshape(-1, rgb)
-
-    mats = [
-        (g_conv, conv_w, conv_row, conv_col),
-        (g_proj[:, None, :], proj_w[:, None, :], proj_row[:, None], proj_col[None, :]),
-        (g_code[:, None, :], code_w[:, None, :], code_row[:, None], code_col[None, :]),
-        (g_head[:, None, :], head_w[:, None, :], head_row[:, None], head_col[None, :]),
-    ]
-    rows_new = [row_part(grad, row) for grad, weight, row, col in mats]
-    wt_sq = [jnp.sum(weight * weight, axis=(0, 2)) for grad, weight, row, col in mats]
-    sums = lax.psum([r[1:] + (w,) for r, w in zip(rows_new, wt_sq)], "batch")
-    loss, g_gain = lax.psum((recon_part + quant_part, d_gains), BOTH)
+    g_head = rest_full[:, n_code + n_proj : n_code + n_proj + n_head, :rgb].reshape(-1, rgb)
+    grads = [g_conv, g_proj[:, None, :], g_code[:, None, :], g_head[:, None, :]]
+    if not fast:
+        rows_new = [row_part(grad, m[1]) for grad, m in zip(grads, mats_old)]
+        rows_one = [r[0] for r in rows_new]
+        sums = lax.psum([r[1:] for r in rows_new], "batch")
+        sums = [
+            (s[0], s[1], s[2], w) for s, w in zip(sums, lax.psum(wt_sq, "batch"))
+        ]
     done = [
-        finish(m[0], m[1], r[0], m[3], *s) for m, r, s in zip(mats, rows_new, sums)
+        finish(g, m[0], r, m[2], *s) for g, m, r, s in zip(grads, mats_old, rows_one, sums)
     ]
 
     state_new = 0.5 * gain_state + 0.5 * (g_gain * g_gain + EPS_SQ)
@@ -495,22 +1147,22 @@
     return (
         loss,
         g_conv,
-        rows_new[0][0],
+        rows_one[0],
         done[0][0],
         conv_new,
         conv_new.astype(BF),
         g_proj,
-        rows_new[1][0][:, 0],
+        rows_one[1][:, 0],
         done[1][0][0],
         proj_new,
         proj_new.astype(BF),
         g_code,
-        rows_new[2][0][:, 0],
+        rows_one[2][:, 0],
         done[2][0][0],
         code_new,
         code_new.astype(BF),
         g_head,
-        rows_new[3][0][:, 0],
+        rows_one[3][:, 0],
         done[3][0][0],
         head_new,
         head_new.astype(BF),

time: 1000 us -> 577 us (0.58)
  waiting for transfers between devices: 570 us -> 0 us
  Pallas kernels: 131 us -> 404 us
  blocking collectives: 86.9 us -> 0 us
  between operations: 23 us -> 9.91 us
  starting transfers between devices: 11.4 us -> 0 us
  local copies, waits for them, and re-layouts: 75.1 us -> 64.3 us
    reduce_scatter x4 -> x0, waiting for transfers between devices: 378 us -> none  [to_owner(): return lax.psum_scatter(v, BOTH, scatter_dimension=0, tiled=True)]
    pallas_call x0 -> x2, Pallas kernels: none -> 318 us  [the longest x1 177 us: reduce_call(): pl.pallas_call(functools.partial(reduce_kernel, parts), out_shape=outs, i...]
    all_gather x5 -> x0, waiting for transfers between devices: 156 us -> none  [the longest x1 62.5 us: local(): later = lax.all_gather(conv_piece[1:], BOTH, axis=0)]
    psum x2 -> x0, blocking collectives: 80.6 us -> none  [the longest x1 42.1 us: local(): loss, g_gain = lax.psum((recon_part + quant_part, d_gains), BOTH)]
    pallas_call x5 -> x3, Pallas kernels: 131 us -> 85.9 us  [kernel_call(): pl.pallas_call(body, out_shape=outs, in_specs=[VM] * len(args), out_specs...]
    all_to_all x3 -> x0, waiting for transfers between devices: 35.1 us -> none  [whole_crops(): return lax.all_to_all(v, 'rows', split_axis=0, concat_axis=1, tiled=True)]
    reduce_sum x16 -> x4, other arithmetic: 26.2 us -> 8.55 us  [local(): wt_sq = [jnp.sum(m[0] * m[0], axis=(0, 2)) for m in mats_old]]
    all_to_all x3 -> x0, starting transfers between devices: 11.1 us -> none  [whole_crops(): return lax.all_to_all(v, 'rows', split_axis=0, concat_axis=1, tiled=True)]
  transfers between devices with their start and end apart: 12 -> 0, of which waited for: 12 -> 0; matrix products, arithmetic and copies ran while one was open for 11% -> 0% of each run, Pallas kernels for 2% -> 0%
where the time goes in v1:
time: 577 us; the launch traced here: 575 us
  Pallas kernels  404 us (70%)
  other arithmetic  85.9 us (15%)
  local copies, waits for them, and re-layouts  64.3 us (11%)
  matrix products  10.4 us (2%)
  between operations  9.91 us (2%)
    pallas_call x1, Pallas kernels, reduce_call(): pl.pallas_call(functools.partial(reduce_kernel, parts), out_shape=outs, i...  177 us
    pallas_call x1, Pallas kernels, forward_call(): pl.pallas_call(forward_kernel, out_shape=outs, in_specs=[ANY] * 4 + [VM],...  142 us
    pallas_call x3, Pallas kernels, kernel_call(): pl.pallas_call(body, out_shape=outs, in_specs=[VM] * len(args), out_specs...  85.9 us
    scatter-add x1, other arithmetic, local(): jax.ops.segment_sum(d_picked.reshape(-1, lat), codes.reshape(-1), num_seg...  18.7 us
    gather x1, local copies, waits for them, and re-layouts, local(): picked = code_all[codes].astype(F32)  13 us

profile of v1, /device:TPU:0, one launch (start us, length us, event | category | flops | bytes accessed | tf_op | source)
XLA Modules:
  0.0 574.9 jit_solution(18239162446923536687)
XLA Ops:
  0.7 4.4 multiply_reduce_fusion.1
  7.7 2.5 maximum_maximum_fusion.1.rest_mine
  10.2 2.3 multiply_reduce_fusion
  13.3 1.8 copy.65
  15.1 142.0 %shard_map.361 = (bf16[8,4,64,512]{3,2,1,0:T(8,128)(2,1)}, f32[8,4,16,20]{3,2,1,0:T(8,128)}, bf16[4608,512]{1,0:T(8,128)(2,1)}, bf16[4608,512]{1,0:T(8,128)(2,1)...) custom-call(bf16[4,8,64,512]{3,2,1,0:T(8,128)(2,1)} %bitcast.134, ...), custom_call_target="tpu_custom_call" | custom-call | flops 24159191040 | tf_op jit(solution)/shard_map/pallas_call | solution.py:713
  157.0 7.5 %slice.124 = bf16[32,512,256]{2,1,0:T(8,128)(2,1)} slice(bf16[32,544,256]{2,1,0:T(8,128)(2,1)} %bitcast.96), slice={[0:32], [0:512], [0:256]} | slice | bytes 16777216 | tf_op jit(solution)/shard_map/slice | solution.py:993
  166.5 13.0 %gather_fusion = bf16[2048,256]{1,0:T(8,128)(2,1)} fusion(bf16[16384,256]{1,0:T(8,128)(2,1)} %bitcast.95, s32[2048]{0:T(1024)S(1)} %broadcast_clamp_fusion), kind=kCustom, calls=%fused_computation | custom fusion | bytes 2105344 | tf_op jit(solution)/shard_map/gather | solution.py:1000
  179.5 2.6 reshape.310
  185.1 4.9 multiply_reduce_fusion.2
  192.7 1.4 reshape.276
  194.1 1.7 copy.76
  195.8 1.8 multiply_reduce_fusion.4
  199.7 2.1 convolution_convert_fusion.ds_ref
  201.7 23.1 %shard_map.362 = (bf16[8,256,512]{2,1,0:T(8,128)(2,1)}, bf16[4608,512]{1,0:T(8,128)(2,1)}) custom-call(bf16[512,512]{1,0:T(8,128)(2,1)} %convolution_convert_fusion.ds_ref, bf16[512,4608]{1,0:T(8,128)(2,1)} %get-tuple-element.52.l_ref, bf16[4608,512]{1,0:T(8,128)(2,1)} %get-tuple-element.53.w_ref), custom_call_target="tpu_custom_call" | custom-call | flops 4831838208 | bytes 16777216 | tf_op jit(solution)/shard_map/pallas_call | solution.py:294
  224.8 33.5 %shard_map.363 = (bf16[8,256,512]{2,1,0:T(8,128)(2,1)}, bf16[4608,512]{1,0:T(8,128)(2,1)}, f32[2,512]{1,0:T(2,128)}) custom-call(bf16[8,256,512]{2,1,0:T(8,128)(2,1)} %get-tuple-element.54.dc_ref, f32[8,256,512]{2,1,0:T(8,128)} %get-tuple-element.55.v_ref, f32[4,512]{1,0:T(4,128)} %gains_ref.5, bf16[4608,512]{1,0:T(8,128)(2,1)} %get-tuple-element.56.w_ref, ...), custom_call_target="tpu_custom_call" | custom-call | flops 19327352832 | bytes 19935232 | tf_op jit(solution)/shard_map/pallas_call | solution.py:294
  258.3 29.4 %shard_map.364 = (bf16[4608,512]{1,0:T(8,128)(2,1)}, f32[2,512]{1,0:T(2,128)}) custom-call(bf16[8,256,512]{2,1,0:T(8,128)(2,1)} %get-tuple-element.58.dc_ref, bf16[8,256,512]{2,1,0:T(8,128)(2,1)} %bitcast.135, f32[4,512]{1,0:T(4,128)} %gains_ref.5, bf16[4608,512]{1,0:T(8,128)(2,1)} %get-tuple-element.60.w_ref, bf16[8,256,512]{2,1,0:T(8,128)(2,1)} %get-tuple-element.61.a_ref), custom_call_target="tpu_custom_call" | custom-call | flops 19327352832 | bytes 15740928 | tf_op jit(solution)/shard_map/pallas_call | solution.py:294
  289.0 2.7 maximum_multiply_fusion
  291.8 1.4 maximum_maximum_fusion.2.refs_4_
  293.2 2.2 convolution_convert_fusion.1
  295.3 1.7 convolution_convert_fusion.2
  297.0 1.4 copy.78
  298.5 1.5 pad.15.clone
  300.0 3.0 reverse.3
  303.0 3.1 fusion.4
  306.1 3.0 rev.8
  309.1 4.3 copy.70
  313.4 2.9 reshape.303
  317.4 18.7 %scatter_custom_fusion = f32[16384,256]{1,0:T(8,128)} fusion(s32[2048]{0:T(1024)S(1)} %reshape.301, f32[2048,256]{1,0:T(8,128)} %reshape.303, f32[]{:T(128)} %constant.45.clone.1), kind=kCustom, calls=%fused_computation.3 | custom fusion | flops 524288 | bytes 16777728 | tf_op jit(solution)/shard_map/scatter-add | solution.py:1015
  336.1 6.4 %convert_element_type.79 = bf16[16384,256]{1,0:T(8,128)(2,1)S(1)} convert(f32[16384,256]{1,0:T(8,128)} %scatter_custom_fusion) | non-fusion elementwise | flops 4194304 | bytes 25165824 | tf_op jit(solution)/shard_map/convert_element_type | solution.py:1069
  342.6 6.4 %maximum_maximum_fusion.refs_3_ = bf16[4,2,2,2,544,256]{5,4,3,2,1,0:T(8,128)(2,1)} fusion(bf16[4,2,2,2,8,256]{5,4,3,2,1,0:T(8,128)(2,1)S(1)} %bitcast.114, bf16[4,2,2,2,16,256]{5,4,3,2,1,0:T(8,128)(2,1)S(1)} %bitcast.115, bf16[4,2,2,2,512,256]{5,4,3,2,1,0:T(8,128)(2,1)S(1)} %bitcast.94, bf16[544]{0:T(1024)(128)(2,1)S(1)} %copy-done.18), kind=kLoop, calls=%fused_computation.2 | loop fusion | flops 35651584 | bytes 17695808 | tf_op jit(solution)/shard_map/concatenate | solution.py:1068
  352.5 1.4 copy.73.refs_6_
  353.9 2.4 reshape.311.refs_5_
  356.3 176.5 %shard_map.365 = (bf16[4,144,512]{2,1,0:T(8,128)(2,1)}, bf16[4,144,512]{2,1,0:T(8,128)(2,1)}, bf16[4,144,512]{2,1,0:T(8,128)(2,1)}, bf16[4,544,256]{2,1,0:T(8,12...) custom-call(bf16[4,2,2,2,144,512]{5,4,3,2,1,0:T(8,128)(2,1)} %bitcast.103, ...), custom_call_target="tpu_custom_call" | custom-call | bytes 23068672 | tf_op jit(solution)/shard_map/pallas_call | solution.py:830
  532.8 1.9 multiply_reduce_fusion.5
  538.1 1.5 fusion.21
  540.2 1.8 fusion.14
  543.4 1.4 convert_element_type.82
  545.6 1.7 reduce.11
  547.9 1.5 fusion.17
  550.8 1.9 fusion.13
  554.8 1.4 slice.131
  556.3 2.3 fusion.18
  560.7 1.4 slice.130
  562.2 1.6 fusion.19
  563.8 1.5 fusion.11
  566.1 1.3 fusion.15
  567.5 1.6 reduce.9
  569.8 5.1 fusion.20
  (92 shorter events, 24.0 us)
Async XLA Ops:
  0.7 4.4 copy-start.9
  0.7 5.6 copy-start.15
  0.7 9.5 %copy-start = (f32[576,3,512]{2,0,1:T(8,128)S(1)}, f32[576,3,512]{2,0,1:T(8,128)}, u32[]{:S(2)}) copy-start(f32[576,3,512]{2,0,1:T(8,128)} %param.22) | copy-start | bytes 10616836
  7.1 0.6 copy-start.17
  10.2 2.3 copy-start.12
  10.2 2.4 copy-start.13
  10.2 2.4 copy-start.10
  157.0 7.5 %copy-start.3 = (f32[8,4,16,20]{3,2,1,0:T(8,128)S(1)}, f32[8,4,16,20]{3,2,1,0:T(8,128)}, u32[]{:S(2)}) copy-start(f32[8,4,16,20]{3,2,1,0:T(8,128)} %get-tuple-element.51) | copy-start | bytes 122884
  183.1 0.7 copy-start.5
  185.1 4.9 copy-start.4
  199.0 0.7 copy-start.6
  336.1 6.4 %copy-start.7 = (bf16[256,256]{1,0:T(8,128)(2,1)S(1)}, bf16[256,256]{1,0:T(8,128)(2,1)}, u32[]{:S(2)}) copy-start(bf16[256,256]{1,0:T(8,128)(2,1)} %pad.15.clone) | copy-start | bytes 393220
  336.1 6.4 %copy-start.8 = (bf16[512,256]{1,0:T(8,128)(2,1)S(1)}, bf16[512,256]{1,0:T(8,128)(2,1)}, u32[]{:S(2)}) copy-start(bf16[512,256]{1,0:T(8,128)(2,1)} %convolution_convert_fusion.1) | copy-start | bytes 786436
  336.1 6.5 %copy-start.18 = (bf16[544]{0:T(1024)(128)(2,1)S(1)}, bf16[544]{0:T(1024)(128)(2,1)}, u32[]{:S(2)}) copy-start(bf16[544]{0:T(1024)(128)(2,1)} %copy-done.17) | copy-start | bytes 3268
  342.6 6.4 %copy-start.19 = (f32[2048]{0:T(1024)S(1)}, f32[2048]{0:T(1024)}, u32[]{:S(2)}) copy-start(f32[2048]{0:T(1024)} %param.31) | copy-start | bytes 24580
  342.6 7.1 %copy-start.23 = (f32[64]{0:T(128)S(1)}, f32[64]{0:T(128)}, u32[]{:S(2)}) copy-start(f32[64]{0:T(128)} %param.29) | copy-start | bytes 772
  356.3 176.5 %copy-start.20 = (f32[4,512]{1,0:T(4,128)S(1)}, f32[4,512]{1,0:T(4,128)}, u32[]{:S(2)}) copy-start(f32[4,512]{1,0:T(4,128)} %param.35) | copy-start | bytes 24580
  356.3 179.2 %copy-start.14 = (f32[4,512]{1,0:T(4,128)S(1)}, f32[4,512]{1,0:T(4,128)}, u32[]{:S(2)}) copy-start(f32[4,512]{1,0:T(4,128)} %gains_ref.5) | copy-start | bytes 24580
  534.7 8.7 %copy-start.16 = (f32[4,512]{1,0:T(4,128)}, f32[4,512]{1,0:T(4,128)S(1)}, u32[]{:S(2)}) copy-start(f32[4,512]{1,0:T(4,128)S(1)} %get-tuple-element.151) | copy-start | bytes 24580
  547.9 8.4 %copy-start.1 = (f32[2048,256]{1,0:T(8,128)S(1)}, f32[2048,256]{1,0:T(8,128)}, u32[]{:S(2)}) copy-start(f32[2048,256]{1,0:T(8,128)} %param.24) | copy-start | bytes 6291460
  552.7 5.8 %copy-start.21 = (f32[1,256]{1,0:T(1,128)}, f32[1,256]{1,0:T(1,128)S(1)}, u32[]{:S(2)}) copy-start(f32[1,256]{1,0:T(1,128)S(1)} %get-tuple-element.161) | copy-start | bytes 3076
  556.2 2.4 copy-start.2
  556.3 2.3 copy-start.11
  562.2 5.3 copy-start.22

commit v2 on v1

--- a/solution.py
+++ b/solution.py
@@ -94,14 +94,15 @@
     return acc
 
 
-def conv_weight_grad(a_ref, d3_ref, dw_ref):
+def conv_weight_grad(a_ref, d3_ref, dw_ref, half, tick=None):
     crops, cells, ch = a_ref.shape
     nb = 256
-
-    def block(j, carry):
-        dx = j // (ch // nb)
-        n = j % (ch // nb)
-        lane = pl.multiple_of(j * nb, nb)
+    out = slice(half * nb, (half + 1) * nb)
+
+    def block(dx, carry):
+        if tick is not None:
+            tick(dx)
+        lane = pl.multiple_of(dx * ch + half * nb, nb)
         for dy in range(3):
             rhs = d3_ref[:, 2 - dy : 18 - dy, :, pl.ds(lane, nb)].reshape(crops * cells, nb)
             d = lax.dot_general(
@@ -111,10 +112,10 @@
                 preferred_element_type=F32,
             )
             row = pl.multiple_of((dy * 3 + dx) * ch, ch)
-            dw_ref[pl.ds(row, ch), pl.ds(pl.multiple_of(n * nb, nb), nb)] = d.astype(dw_ref.dtype)
+            dw_ref[pl.ds(row, ch), out] = d.astype(dw_ref.dtype)
         return carry
 
-    lax.fori_loop(0, 3 * (ch // nb), block, 0)
+    lax.fori_loop(0, 3, block, 0)
 
 
 def silu(h):
@@ -195,7 +196,7 @@
     down_dot(l_ref, w_down_ref, s_ref)
 
 
-def down_back_kernel(ds_ref, l_ref, w_ref, dc_ref, dw_ref, y32):
+def down_input_grad(ds_ref, w_ref, dc_ref, y32, tick=None):
     cells, ch = ds_ref.shape
     crops = cells // 64
 
@@ -208,6 +209,8 @@
         )
 
     def crop(i, carry):
+        if tick is not None:
+            tick(i)
         here = ds_ref[pl.ds(pl.multiple_of(i * 64, 64), 64), :].astype(F32)
         at = lax.broadcasted_iota(jnp.int32, here.shape, 0)
 
@@ -232,6 +235,10 @@
         return carry
 
     lax.fori_loop(0, crops, crop, 0)
+
+
+def down_weight_grad(l_ref, ds_ref, dw_ref):
+    ch = ds_ref.shape[1]
 
     def block(t, carry):
         lane = pl.multiple_of(t * ch, ch)
@@ -247,6 +254,11 @@
     lax.fori_loop(0, 9, block, 0)
 
 
+def down_back_kernel(ds_ref, l_ref, w_ref, dc_ref, dw_ref, y32):
+    down_weight_grad(l_ref, ds_ref, dw_ref)
+    down_input_grad(ds_ref, w_ref, dc_ref, y32)
+
+
 def hidden_grad(v, gain, shift, d_act):
     mean, rstd = moments(v)
     vhat = (v - mean) * rstd
@@ -255,29 +267,25 @@
     return d_act * sig * (1.0 + h * (1.0 - sig)), vhat, rstd
 
 
-def unit_back_kernel(dc_ref, v_ref, gains_ref, w_ref, a_ref, *outs, row, inner):
-    if inner:
-        din_ref, dw_ref, dg_ref, d3 = outs
-    else:
-        dw_ref, dg_ref, d3 = outs
+def unit_back(dc_ref, v_of, gains_ref, w_ref, dg_ref, d3, row, din_ref=None, tick=None):
     crops, cells, ch = dc_ref.shape
     dg_ref[...] = jnp.zeros_like(dg_ref)
 
     def crop(i, carry):
+        if tick is not None:
+            tick(i)
         d = dc_ref[i].astype(F32)
         slot = d3.at[i]
         zero_edges(slot)
         fill_three(slot, shifted(d, -1), d, shifted(d, 1))
         d_act = conv_rows_back(slot, w_ref)
         gain = gains_ref[row : row + 1, :]
-        hg, vhat, rstd = hidden_grad(
-            v_ref[i].astype(F32), gain, gains_ref[row + 1 : row + 2, :], d_act
-        )
+        hg, vhat, rstd = hidden_grad(v_of(i), gain, gains_ref[row + 1 : row + 2, :], d_act)
         one = jnp.sum(hg * vhat, axis=0, keepdims=True)
         two = jnp.sum(hg, axis=0, keepdims=True)
         dg_ref[0:1, :] += one
         dg_ref[1:2, :] += two
-        if inner:
+        if din_ref is not None:
             count = cells * (ch // GROUPS)
             sums = jnp.concatenate([two * gain, one * gain, jnp.zeros((6, ch), F32)], axis=0)
             sums = group_sum(sums) / count
@@ -285,7 +293,21 @@
         return carry
 
     lax.fori_loop(0, crops, crop, 0)
-    conv_weight_grad(a_ref, d3, dw_ref)
+
+
+def unit_back_kernel(dc_ref, v_ref, gains_ref, w_ref, a_ref, *outs, row, inner):
+    if inner:
+        din_ref, dw_ref, dg_ref, d3 = outs
+    else:
+        dw_ref, dg_ref, d3 = outs
+        din_ref = None
+
+    def v_of(i):
+        return v_ref[i].astype(F32)
+
+    unit_back(dc_ref, v_of, gains_ref, w_ref, dg_ref, d3, row, din_ref)
+    for half in range(2):
+        conv_weight_grad(a_ref, d3, dw_ref, half)
 
 
 def kernel_call(body, outs, scratch, flops, *args):
@@ -386,9 +408,9 @@
 
 
 class Reduce:
-    steps = 5
-
-    def __init__(self, place, src, out, mine, one, two, three, four, send, recv):
+    steps = 6
+
+    def __init__(self, place, src, out, mine, one, two, three, kept, four, send, recv):
         self.p, self.src, self.out = place, src, out
         self.mine, self.one, self.two, self.three, self.four = mine, one, two, three, four
         self.send, self.recv = send, recv
@@ -402,80 +424,51 @@
             x=jnp.where(first_x, place.x, 1 - place.x), y=jnp.where(first_x, 1 - place.y, place.y)
         )
         self.slot = 2 * self.f + self.g
+        self.kept = kept
 
     @staticmethod
-    def scratch(rows, lanes):
-        def buf(*lead):
-            return pltpu.VMEM(lead + (rows, lanes), BF)
-
-        return [
-            buf(4, 4),
-            buf(4, 4),
-            buf(2, 4),
-            buf(4),
-            buf(3),
-            pltpu.SemaphoreType.DMA((12,)),
-            pltpu.SemaphoreType.DMA((16,)),
-        ]
+    def early(rows, lanes):
+        return [pltpu.VMEM(lead + (rows, lanes), BF) for lead in ((4, 4), (4, 4), (2, 4), (4,))]
+
+    @staticmethod
+    def late(rows, lanes, kept):
+        return [pltpu.VMEM(lead + (rows, lanes), BF) for lead in ((4,),) * kept + ((3,),)]
+
+    @staticmethod
+    def sems():
+        return [pltpu.SemaphoreType.DMA((11,)), pltpu.SemaphoreType.DMA((15,))]
 
     def copies(self, step):
-        p, src, mine = self.p, self.src, self.mine
+        p, src, mine, send, recv = self.p, self.src, self.mine, self.send, self.recv
         if step == 0:
             out = []
             for k in range(4):
                 y, x = k // 2, k % 2
                 there = jnp.where(p.c == 1, 2 * x + y, 2 * y + x)
                 here = jnp.where(p.c == 0, 2 * x + y, 2 * y + x)
-                out.append(
-                    remote(
-                        src.at[:, y, 1 - p.c, x],
-                        self.one.at[there],
-                        self.send.at[k],
-                        self.recv.at[k],
-                        p.at(c=1 - p.c),
-                    )
-                )
-                out.append(
-                    pltpu.make_async_copy(src.at[:, y, p.c, x], mine.at[here], self.recv.at[12 + k])
-                )
+                part = src.at[:, y, 1 - p.c, x]
+                peer = p.at(c=1 - p.c)
+                out.append(remote(part, self.one.at[there], send.at[k], recv.at[k], peer))
+                local = src.at[:, y, p.c, x]
+                out.append(pltpu.make_async_copy(local, mine.at[here], recv.at[10 + k]))
             return out
         if step == 1:
-            return [
-                remote(
-                    mine.at[pl.ds(2 * (1 - self.f), 2)],
-                    self.two,
-                    self.send.at[4],
-                    self.recv.at[4],
-                    self.f_peer,
-                )
-            ]
+            part = mine.at[pl.ds(2 * (1 - self.f), 2)]
+            return [remote(part, self.two, send.at[4], recv.at[4], self.f_peer)]
         if step == 2:
-            return [
-                remote(
-                    mine.at[2 * self.f + 1 - self.g],
-                    self.three,
-                    self.send.at[5],
-                    self.recv.at[5],
-                    self.g_peer,
-                )
-            ]
+            part = mine.at[2 * self.f + 1 - self.g]
+            return [remote(part, self.three, send.at[5], recv.at[5], self.g_peer)]
         if step == 3:
-            return [
-                remote(
-                    mine.at[self.slot, (p.z + d) % 4],
-                    self.four.at[d - 1],
-                    self.send.at[5 + d],
-                    self.recv.at[5 + d],
-                    peer,
-                )
-                for d, peer in zip((1, 2, 3), p.z_peers())
-            ]
-        return [
-            remote(
-                self.out.at[p.part], self.out.at[p.part], self.send.at[9 + k], self.recv.at[9 + k], q
-            )
-            for k, q in enumerate(p.row_peers())
-        ]
+            out = []
+            for d, peer in zip((1, 2, 3), p.z_peers()):
+                part = self.kept.at[(p.z + d) % 4]
+                out.append(remote(part, self.four.at[d - 1], send.at[5 + d], recv.at[5 + d], peer))
+            return out
+        if step == 4:
+            part = self.out.at[p.part]
+            return [remote(part, part, send.at[9], recv.at[9], p.at(x=1 - p.x))]
+        part = self.out.at[pl.ds(2 * p.c, 2)]
+        return [remote(part, part, send.at[10], recv.at[14], p.at(c=1 - p.c))]
 
     def start(self, step):
         for copy in self.copies(step):
@@ -486,38 +479,48 @@
         for copy in self.copies(step):
             copy.wait_recv()
 
-        def add(dst, src):
-            dst[...] = (dst[...].astype(F32) + src[...].astype(F32)).astype(BF)
+        def add(dst, a, b):
+            dst[...] = (a[...].astype(F32) + b[...].astype(F32)).astype(BF)
 
         if step == 0:
 
             def body(i, carry):
-                add(mine.at[i // 4, i % 4], self.one.at[i // 4, i % 4])
+                at = (i // 4, i % 4)
+                add(mine.at[at], mine.at[at], self.one.at[at])
                 return carry
 
             lax.fori_loop(0, 16, body, 0)
         if step == 1:
+            for copy in self.copies(step):
+                copy.wait_send()
 
             def body(i, carry):
-                add(mine.at[2 * self.f + i // 4, i % 4], self.two.at[i // 4, i % 4])
+                at = (2 * self.f + i // 4, i % 4)
+                add(mine.at[at], mine.at[at], self.two.at[i // 4, i % 4])
                 return carry
 
             lax.fori_loop(0, 8, body, 0)
         if step == 2:
 
             def body(i, carry):
-                add(mine.at[self.slot, i], self.three.at[i])
+                add(self.kept.at[i], mine.at[self.slot, i], self.three.at[i])
                 return carry
 
             lax.fori_loop(0, 4, body, 0)
         if step == 3:
-            total = mine[self.slot, p.z].astype(F32)
+            total = self.kept[p.z].astype(F32)
             for d in range(3):
                 total = total + self.four[d].astype(F32)
             self.out[p.part] = total.astype(BF)
 
-    def end(self):
-        for step in range(self.steps):
+    def go(self, step):
+        self.arrive(step - 1)
+        self.start(step)
+
+    def sent(self, first, last):
+        for step in range(first, last):
+            if step == 1:
+                continue
             for copy in self.copies(step):
                 if copy.is_remote:
                     copy.wait_send()
@@ -526,8 +529,10 @@
 def forward_kernel(
     feat,
     side,
-    w_mine,
-    rest_mine,
+    conv_ref,
+    code_ref,
+    proj_ref,
+    head_ref,
     gains_ref,
     x_out,
     side_out,
@@ -540,6 +545,9 @@
     a_two_ref,
     l_ref,
     s_ref,
+    wt_ref,
+    w_mine,
+    rest_mine,
     xv,
     wv0,
     wv1,
@@ -554,6 +562,31 @@
 ):
     place = Place()
     rank = 2 * place.x + place.c
+    ch, lat = conv_ref.shape[2], code_ref.shape[1]
+    n_code, n_proj, n_head = (v.shape[0] // 4 for v in (code_ref, proj_ref, head_ref))
+    wt_ref[...] = jnp.zeros_like(wt_ref)
+
+    def cast_conv(j):
+        n = w_mine.shape[3]
+        for k in range(4):
+            v = conv_ref[j, k * n : (k + 1) * n, :]
+            w_mine[j, k // 2, k % 2] = v.astype(BF)
+            wt_ref[j : j + 1, :] += jnp.sum(v * v, axis=0, keepdims=True)
+
+    def cast_rest():
+        for k in range(4):
+            low = 0
+            for m, (ref, n) in enumerate(
+                ((code_ref, n_code), (proj_ref, n_proj), (head_ref, n_head))
+            ):
+                v = ref[k * n : (k + 1) * n, :]
+                wt_ref[3 + m : 4 + m, :lat] += jnp.sum(v * v, axis=0, keepdims=True)
+                if n % 16:
+                    v = jnp.concatenate([v, jnp.zeros((-n % 16, lat), F32)], axis=0)
+                rest_mine[k // 2, k % 2, low : low + v.shape[0]] = v.astype(BF)
+                low += v.shape[0]
+
+    cast_conv(0)
     place.greet()
 
     def view(ref, lanes):
@@ -585,6 +618,9 @@
     for copy in cells:
         copy.start()
     w0[1].start(0)
+    cast_rest()
+    cast_conv(1)
+    cast_conv(2)
     w0[0].go(1)
     w0[1].arrive(0)
     w1[0].start(0)
@@ -604,7 +640,7 @@
         for k, (v, o) in enumerate(((wv0, w_out0), (wv1, w_out1), (wv2, w_out2)))
     ]
     keep_w[0].start()
-    count, _, _, ch = xv.shape
+    count = xv.shape[0]
 
     def crop_x(i):
         return xv[i].reshape(256, ch).astype(F32)
@@ -689,10 +725,13 @@
         copy.wait()
 
 
-def forward_call(feat, side, w_mine, rest_mine, gains):
+def forward_call(feat, side, conv_w, code_w, proj_w, head_w, gains):
     ranks, crops, cells, ch = feat.shape
+    lat = code_w.shape[1]
     lat_cells = crops * ranks * cells // 4
-    whole = 8 * w_mine.shape[1] * w_mine.shape[2] * w_mine.shape[3]
+    n_conv = conv_w.shape[1] // 4
+    n_rest = code_w.shape[0] // 4 + proj_w.shape[0] // 4 + 16
+    whole = 32 * n_conv
 
     def shape(*dims, dtype=BF):
         return jax.ShapeDtypeStruct(dims, dtype)
@@ -703,19 +742,24 @@
         shape(whole, ch),
         shape(whole, ch),
         shape(whole, ch),
-        shape(4, 2, *rest_mine.shape),
+        shape(4, 2, 2, 2, n_rest, lat),
         shape(crops, ranks * cells, ch),
         shape(crops, ranks * cells, ch, dtype=F32),
         shape(crops, ranks * cells, ch),
         shape(lat_cells, 9 * ch),
         shape(lat_cells, ch),
+        shape(8, ch, dtype=F32),
     ]
     return pl.pallas_call(
         forward_kernel,
         out_shape=outs,
-        in_specs=[ANY] * 4 + [VM],
-        out_specs=[ANY] * 6 + [VM] * 5,
-        scratch_shapes=[pltpu.VMEM((crops, ranks, cells, ch), BF)]
+        in_specs=[ANY] * 2 + [VM] * 5,
+        out_specs=[ANY] * 6 + [VM] * 6,
+        scratch_shapes=[
+            pltpu.VMEM((3, 2, 2, n_conv, ch), BF),
+            pltpu.VMEM((2, 2, n_rest, lat), BF),
+            pltpu.VMEM((crops, ranks, cells, ch), BF),
+        ]
         + [pltpu.VMEM((whole, ch), BF)] * 3
         + [
             pltpu.VMEM((18, 16, 3 * ch), BF),
@@ -734,112 +778,633 @@
             bytes_accessed=0,
             transcendentals=0,
         ),
-    )(feat, side, w_mine, rest_mine, gains)
-
-
-def reduce_kernel(parts, *refs):
-    n_code, n_proj, n_head, rgb = parts
-    sources, refs = refs[:4], refs[4:]
-    vec_ref, conv_row_ref, rest_row_ref, refs = refs[0], refs[1], refs[2], refs[3:]
-    g_refs, refs = refs[:4], refs[4:]
-    conv_new_ref, rest_new_ref, tv_ref, refs = refs[0], refs[1], refs[2], refs[3:]
-    vec_in, tv_in, s_send, s_recv, refs = refs[0], refs[1], refs[2], refs[3], refs[4:]
+    )(feat, side, conv_w, code_w, proj_w, head_w, gains)
+
+
+def quantizer_kernel(
+    consts,
+    codes_ref,
+    rest,
+    side_ref,
+    sl_ref,
+    l_ref,
+    ds_ref,
+    loss_ref,
+    rg_ref,
+    dw_ref,
+    tab,
+    stage,
+    proj_v,
+    head_v,
+    e_ref,
+    sems,
+):
+    lat_count, pix_count, rgb, n_code = consts
+    cells = sl_ref.shape[0]
+    pieces = rest.shape[0]
+    slots = stage.shape[0]
+    lat = tab.shape[1]
+    small = [
+        pltpu.make_async_copy(rest.at[:, n_code : n_code + 16], proj_v, sems.at[slots]),
+        pltpu.make_async_copy(rest.at[:, n_code + 16 :], head_v, sems.at[slots + 1]),
+    ]
+    for copy in small:
+        copy.start()
+
+    def fetch(p):
+        slot = p % slots
+        return pltpu.make_async_copy(rest.at[p, :n_code], stage.at[slot], sems.at[slot])
+
+    for p in range(slots):
+        fetch(p).start()
+
+    def widen(p, carry):
+        fetch(p).wait()
+        tab[pl.ds(pl.multiple_of(p * n_code, n_code), n_code), :] = stage[p % slots].astype(F32)
+
+        @pl.when(p + slots < pieces)
+        def _():
+            fetch(p + slots).start()
+
+        return carry
+
+    lax.fori_loop(0, pieces, widen, 0)
+    for copy in small:
+        copy.wait()
+    proj = proj_v[...].reshape(-1, lat)
+    head = head_v[...].astype(F32)[:, :8, :128].reshape(-1, 128).astype(BF)
+
+    def pick(b, carry):
+        for j in range(8):
+            for k in range(4):
+                row = codes_ref[(b * 8 + j) * 4 + k]
+                e_ref[k, pl.ds(b * 8 + j, 1), :] = tab[pl.ds(row, 1), :]
+        return carry
+
+    lax.fori_loop(0, cells // 8, pick, 0)
+
+    latent = jnp.dot(sl_ref[...], proj, preferred_element_type=F32)
+    cum = e_ref[0]
+    resid = []
+    square = None
+    for k in range(4):
+        if k:
+            cum = cum + e_ref[k]
+        r = latent - cum
+        resid.append(r)
+        part = jnp.sum(r * r, axis=0, keepdims=True)
+        square = part if square is None else square + part
+    zq = cum.astype(BF)
+    side = side_ref[...]
+    valid = lax.broadcasted_iota(jnp.int32, side.shape, 1) < rgb
+    weight = jnp.where(valid, pltpu.roll(side, 128 - 16, 1), 0.0)
+    diff = jnp.where(valid, jnp.dot(zq, head, preferred_element_type=F32) - side, 0.0)
+    smooth = jnp.sqrt(diff * diff + 1.0)
+    recon = jnp.sum(weight * (smooth - 1.0), axis=0, keepdims=True)
+    loss_ref[...] = jnp.zeros_like(loss_ref)
+    loss_ref[0:1, 0:lat] = square * ((1.0 + BETA) / lat_count)
+    loss_ref[0:1, lat : lat + 128] = recon / pix_count
+    d_pred = (weight * (diff / smooth) / pix_count).astype(BF)
+    back = (((1,), (1,)), ((), ()))
+    rows = (((0,), (0,)), ((), ()))
+    d_head = lax.dot_general(zq, d_pred, rows, preferred_element_type=F32)
+    total = resid[0] + resid[1] + resid[2] + resid[3]
+    d_zq = lax.dot_general(d_pred, head, back, preferred_element_type=F32)
+    d_lat = (total * (2.0 * BETA / lat_count) + d_zq).astype(BF)
+    d_proj = lax.dot_general(sl_ref[...], d_lat, rows, preferred_element_type=F32)
+    d_s = lax.dot_general(d_lat, proj, back, preferred_element_type=F32)
+    ds_ref[...] = d_s.astype(BF)
+    tail = None
+    for k in (3, 2, 1, 0):
+        tail = resid[k] if tail is None else tail + resid[k]
+        e_ref[k] = tail * (-2.0 / lat_count)
+
+    def clear(p, carry):
+        tab[pl.ds(pl.multiple_of(p * n_code, n_code), n_code), :] = jnp.zeros((n_code, lat), F32)
+        return carry
+
+    lax.fori_loop(0, pieces, clear, 0)
+
+    def scatter(b, carry):
+        for j in range(8):
+            for k in range(4):
+                row = codes_ref[(b * 8 + j) * 4 + k]
+                tab[pl.ds(row, 1), :] += e_ref[k, pl.ds(b * 8 + j, 1), :]
+        return carry
+
+    lax.fori_loop(0, cells // 8, scatter, 0)
+
+    def narrow(p, carry):
+        at = pl.ds(pl.multiple_of(p * n_code, n_code), n_code)
+        rg_ref[p, :n_code] = tab[at, :].astype(BF)
+        return carry
+
+    lax.fori_loop(0, pieces, narrow, 0)
+    rg_ref[:, n_code : n_code + 16] = d_proj.astype(BF).reshape(pieces, 16, lat)
+    d_head = jnp.concatenate([d_head, jnp.zeros((d_head.shape[0], lat - 128), F32)], axis=1)
+    d_head = d_head.reshape(pieces, 8, lat)
+    d_head = jnp.concatenate([d_head, jnp.zeros((pieces, 8, lat), F32)], axis=1)
+    rg_ref[:, n_code + 16 :] = d_head.astype(BF)
+    down_weight_grad(l_ref, ds_ref, dw_ref)
+
+
+def quantizer_call(codes, rest, side, s_low, windows, lat_count, pix_count, rgb, n_code):
+    pieces, rows, lat = rest.shape
+    cells, ch = s_low.shape
+    outs = [
+        jax.ShapeDtypeStruct((cells, ch), BF),
+        jax.ShapeDtypeStruct((8, ch), F32),
+        jax.ShapeDtypeStruct((pieces, rows, lat), BF),
+        jax.ShapeDtypeStruct((9 * ch, ch), BF),
+    ]
+    return pl.pallas_call(
+        functools.partial(quantizer_kernel, (lat_count, pix_count, rgb, n_code)),
+        out_shape=outs,
+        in_specs=[pl.BlockSpec(memory_space=pltpu.SMEM), ANY, VM, VM, VM],
+        out_specs=[VM] * 4,
+        scratch_shapes=[
+            pltpu.VMEM((pieces * n_code, lat), F32),
+            pltpu.VMEM((4, n_code, lat), BF),
+            pltpu.VMEM((pieces, 16, lat), BF),
+            pltpu.VMEM((pieces, rows - n_code - 16, lat), BF),
+            pltpu.VMEM((4, cells, lat), F32),
+            pltpu.SemaphoreType.DMA((6,)),
+        ],
+        compiler_params=pltpu.CompilerParams(vmem_limit_bytes=58 * MIB),
+        cost_estimate=pl.CostEstimate(flops=10**10, bytes_accessed=10**7, transcendentals=0),
+    )(codes, rest, side, s_low, windows)
+
+
+def second_back_kernel(
+    ds_ref,
+    w_down_ref,
+    w_ref,
+    c_ref,
+    a_ref,
+    gains_ref,
+    down_src,
+    rest_src,
+    din_ref,
+    dw_ref,
+    dg_ref,
+    g_down_ref,
+    rest_kept_ref,
+    dc,
+    d3,
+    y32,
+    *bufs,
+):
     place = Place()
-    per = len(refs) // 4
-    jobs = [
-        Reduce(place, sources[k], g_refs[k], *refs[k * per : (k + 1) * per]) for k in (3, 2, 1, 0)
+    down = Reduce(place, down_src, g_down_ref, *bufs[:8])
+    early, sems = bufs[8:12], bufs[12:]
+    rest = Reduce(place, rest_src.at[..., :128], None, *early, rest_kept_ref, None, *sems)
+    place.greet()
+    down.start(0)
+    rest.start(0)
+
+    def tick_down(i):
+        @pl.when(i == 4)
+        def _():
+            down.go(1)
+
+    def tick_crop(i):
+        @pl.when(i == 0)
+        def _():
+            rest.arrive(0)
+
+        @pl.when(i == 3)
+        def _():
+            down.go(2)
+            rest.start(1)
+
+        @pl.when(i == 6)
+        def _():
+            down.go(3)
+
+    down_input_grad(ds_ref, w_down_ref, dc, y32, tick_down)
+    unit_back(dc, lambda i: c_ref[i], gains_ref, w_ref, dg_ref, d3, 2, din_ref, tick_crop)
+    conv_weight_grad(a_ref, d3, dw_ref, 0)
+    rest.go(2)
+    conv_weight_grad(a_ref, d3, dw_ref, 1)
+    down.go(4)
+    rest.arrive(2)
+    down.go(5)
+    down.arrive(5)
+    down.sent(0, 6)
+    rest.sent(0, 3)
+
+
+def second_back_call(ds, w_down, w, c_one, a_two, gains, down_src, rest_src):
+    crops, cells, ch = c_one.shape
+    n_conv, n_rest = down_src.shape[-2], rest_src.shape[-2]
+    outs = [
+        jax.ShapeDtypeStruct((crops, cells, ch), BF),
+        jax.ShapeDtypeStruct(w.shape, BF),
+        jax.ShapeDtypeStruct((2, ch), F32),
+        jax.ShapeDtypeStruct((4, n_conv, ch), BF),
+        jax.ShapeDtypeStruct((4, n_rest, 128), BF),
     ]
+    return pl.pallas_call(
+        second_back_kernel,
+        out_shape=outs,
+        in_specs=[VM] * 6 + [ANY] * 2,
+        out_specs=[VM] * 5,
+        scratch_shapes=[
+            pltpu.VMEM((crops, cells, ch), BF),
+            pltpu.VMEM((crops, 18, 16, 3 * ch), BF),
+            pltpu.VMEM((ch // 128, cells, 128), F32),
+        ]
+        + Reduce.early(n_conv, ch)
+        + Reduce.late(n_conv, ch, 1)
+        + Reduce.sems()
+        + Reduce.early(n_rest, 128)
+        + Reduce.sems(),
+        compiler_params=pltpu.CompilerParams(
+            vmem_limit_bytes=58 * MIB, collective_id=3, has_side_effects=True
+        ),
+        cost_estimate=pl.CostEstimate(flops=2 * 10**10, bytes_accessed=0, transcendentals=0),
+    )(ds, w_down, w, c_one, a_two, gains, down_src, rest_src)
+
+
+def first_back_kernel(
+    sizes,
+    dc_ref,
+    x_ref,
+    gains_ref,
+    w_ref,
+    a_ref,
+    rest_kept_ref,
+    g_down_ref,
+    dg_two_ref,
+    loss_ref,
+    wt_ref,
+    conv_row_ref,
+    rest_row_ref,
+    rest_src,
+    second_src,
+    g_first0,
+    g_first1,
+    g_second,
+    g_rest0,
+    g_rest1,
+    conv_new_ref,
+    rest_new_ref,
+    tv_ref,
+    dw,
+    d3,
+    dg,
+    vec,
+    vec_in,
+    tv_in,
+    s_send,
+    s_recv,
+    *bufs,
+):
+    n_code, n_proj, n_head, rgb = sizes
+    place = Place()
+    bufs = list(bufs)
+
+    def take(n):
+        out = bufs[:n]
+        del bufs[:n]
+        return out
+
+    half = rest_src.shape[-1] // 2
+    ch = tv_ref.shape[1]
+    view = dw.reshape(4, 2, 2, 2, dw.shape[0] // 32, ch)
+    four, sems = take(1), take(2)
+    rest0 = Reduce(place, None, g_rest0, *[None] * 4, rest_kept_ref, *four, *sems)
+    rest1 = Reduce(place, rest_src.at[..., half:], g_rest1, *take(8))
+    second = Reduce(place, second_src, g_second, *take(8))
+    low = Reduce(place, view.at[..., : ch // 2], g_first0, *take(8))
+    high = Reduce(place, view.at[..., ch // 2 :], g_first1, *take(8))
     place.greet()
+    rest0.start(3)
+    rest1.start(0)
+    second.start(0)
+
+    def tick_crop(i):
+        @pl.when(i == 2)
+        def _():
+            rest1.go(1)
+            second.arrive(0)
+
+        @pl.when(i == 6)
+        def _():
+            rest0.go(4)
+
+    def tick_low(dx):
+        @pl.when(dx == 0)
+        def _():
+            rest1.go(2)
+            second.start(1)
+
+        @pl.when(dx == 1)
+        def _():
+            rest0.go(5)
+
+    def tick_high(dx):
+        @pl.when(dx == 0)
+        def _():
+            rest1.go(3)
+
+        @pl.when(dx == 1)
+        def _():
+            low.go(1)
+
+    def v_of(i):
+        return x_ref[i].astype(F32)
+
+    unit_back(dc_ref, v_of, gains_ref, w_ref, dg, d3, 0, None, tick_crop)
+    vec[...] = jnp.zeros_like(vec)
+    vec[0:2] = dg[...]
+    vec[2:4] = dg_two_ref[...]
+    vec[4:5] = loss_ref[0:1]
     small = [
-        remote(vec_ref, vec_in.at[k], s_send.at[k], s_recv.at[k], q)
+        remote(vec, vec_in.at[k], s_send.at[k], s_recv.at[k], q)
         for k, q in enumerate(place.row_peers())
     ]
     for copy in small:
         copy.start()
-    for job in jobs:
-        job.start(0)
-    for tick in range(len(jobs) + Reduce.steps - 1):
-        for k, job in enumerate(jobs):
-            step = tick - k
-            if 0 <= step < Reduce.steps:
-                job.arrive(step)
-                if step + 1 < Reduce.steps:
-                    job.start(step + 1)
+    conv_weight_grad(a_ref, d3, dw, 0, tick_low)
+    low.start(0)
+    conv_weight_grad(a_ref, d3, dw, 1, tick_high)
+    high.start(0)
+    second.go(2)
+    high.go(1)
+
+    tv_ref[...] = jnp.zeros_like(tv_ref)
     for copy in small:
         copy.wait_recv()
-    tv_ref[...] = jnp.zeros_like(tv_ref)
-    tv_ref[16:24, :] = vec_ref[...] + vec_in[0] + vec_in[1] + vec_in[2]
-    ch = tv_ref.shape[1]
-
-    def fold(g, row, width):
-        sq = g * g
-        new = 0.5 * row + 0.5 * (jnp.sum(sq, axis=1, keepdims=True) / width + EPS_SQ)
+    tv_ref[16:24, :] = vec[...] + vec_in[0] + vec_in[1] + vec_in[2]
+    tv_ref[24:32, :] = wt_ref[...]
+
+    def fold(parts, row, width):
+        squares = [g.astype(F32) for g in parts]
+        squares = [g * g for g in squares]
+        total = sum(jnp.sum(q, axis=1, keepdims=True) for q in squares)
+        new = 0.5 * row + 0.5 * (total / width + EPS_SQ)
+        inverse = 1.0 / new
+        col = [jnp.sum(q, axis=0, keepdims=True) for q in squares]
+        over = [jnp.sum(q * inverse, axis=0, keepdims=True) for q in squares]
         return (
             new,
-            jnp.sum(sq, axis=0, keepdims=True),
-            jnp.sum(sq / new, axis=0, keepdims=True),
+            jnp.concatenate(col, axis=1),
+            jnp.concatenate(over, axis=1),
             jnp.sum(new, axis=0, keepdims=True),
         )
 
-    for j in range(3):
+    def fold_conv(j, refs):
         for k in range(4):
-            g = g_refs[j][k].astype(F32)
-            new, col, over, total = fold(g, conv_row_ref[j, k], ch)
+            new, col, over, total = fold([r[k] for r in refs], conv_row_ref[j, k], ch)
             conv_new_ref[j, k] = new
             tv_ref[j : j + 1, :] += col
             tv_ref[3 + j : 4 + j, :] += over
             tv_ref[6 + j : 7 + j, :] += total
-    half = ch // 2
-    spans = ((0, n_code, half), (n_code, n_proj, half), (n_code + n_proj, n_head, rgb))
-    for k in range(4):
-        for m, (low, size, width) in enumerate(spans):
-            g = g_refs[3][k, low : low + size].astype(F32)
-            new, col, over, total = fold(g, rest_row_ref[k, low : low + size], width)
-            rest_new_ref[k, low : low + size] = new
-            tv_ref[9 + m : 10 + m, :half] += col
-            tv_ref[9 + m : 10 + m, half:] += over
-            tv_ref[12 + m : 13 + m, :half] += total
-    sends = [
+
+    def fold_rest():
+        lat = 2 * half
+        spans = ((0, n_code, lat), (n_code, n_proj, lat), (n_code + n_proj, n_head, rgb))
+        for k in range(4):
+            both = [r[k] for r in (g_rest0, g_rest1)]
+            for m, (start, size, width) in enumerate(spans):
+                parts = [v.astype(F32)[start : start + size] for v in both]
+                row = rest_row_ref[k, start : start + size]
+                new, col, over, total = fold(parts, row, width)
+                rest_new_ref[k, start : start + size] = new
+                tv_ref[9 + m : 10 + m, :lat] += col
+                tv_ref[9 + m : 10 + m, lat:] += over
+                tv_ref[12 + m : 13 + m, :] += total
+            size = rest_row_ref.shape[1] - n_code - n_proj - n_head
+            rest_new_ref[k, rest_row_ref.shape[1] - size :] = jnp.ones((size, 1), F32)
+
+    fold_conv(2, [g_down_ref])
+    rest0.arrive(5)
+    rest1.go(4)
+    second.go(3)
+    low.go(2)
+    low.go(3)
+    high.go(2)
+    rest1.go(5)
+    high.go(3)
+    rest1.arrive(5)
+    fold_rest()
+    second.go(4)
+    second.go(5)
+    low.go(4)
+    second.arrive(5)
+    fold_conv(1, [g_second])
+    low.go(5)
+    high.go(4)
+    low.arrive(5)
+    high.go(5)
+    high.arrive(5)
+    fold_conv(0, [g_first0, g_first1])
+
+    across = remote(tv_ref, tv_in.at[0], s_send.at[3], s_recv.at[3], place.at(y=1 - place.y))
+    across.start()
+    across.wait()
+    tv_ref[...] += tv_in[0]
+    along = [
         remote(tv_ref, tv_in.at[k], s_send.at[3 + k], s_recv.at[3 + k], q)
-        for k, q in enumerate(
-            (place.at(y=1 - place.y), place.at(z=place.z ^ 1), place.at(z=place.z ^ 2))
-        )
+        for k, q in zip((1, 2, 3), place.z_peers())
     ]
-    for k, copy in enumerate(sends):
+    for copy in along:
         copy.start()
+    for copy in along:
         copy.wait()
-        tv_ref[...] += tv_in[k]
+    tv_ref[...] += tv_in[1] + tv_in[2] + tv_in[3]
     for copy in small:
         copy.wait_send()
-    for job in jobs:
-        job.end()
-
-
-def reduce_call(sources, vec, conv_row, rest_row, parts):
-    scratch = [
-        pltpu.VMEM((3,) + vec.shape, F32),
-        pltpu.VMEM((3, 24, vec.shape[1]), F32),
-        pltpu.SemaphoreType.DMA((6,)),
-        pltpu.SemaphoreType.DMA((6,)),
+    rest0.sent(3, 6)
+    for job in (rest1, second, low, high):
+        job.sent(0, 6)
+
+
+def first_back_call(
+    sizes, dc, x, gains, w, a_one, rest_kept, g_down, dg_two, loss, wt, conv_row, rest_row,
+    rest_src, second_src
+):
+    crops, cells, ch = x.shape
+    n_conv, n_rest = second_src.shape[-2], rest_src.shape[-2]
+
+    def shape(*dims, dtype=BF):
+        return jax.ShapeDtypeStruct(dims, dtype)
+
+    outs = [
+        shape(4, n_conv, ch // 2),
+        shape(4, n_conv, ch // 2),
+        shape(4, n_conv, ch),
+        shape(4, n_rest, 128),
+        shape(4, n_rest, 128),
+        shape(*conv_row.shape, dtype=F32),
+        shape(*rest_row.shape, dtype=F32),
+        shape(32, ch, dtype=F32),
     ]
-    for s in sources:
-        scratch += Reduce.scratch(*s.shape[-2:])
-    outs = [jax.ShapeDtypeStruct((4,) + s.shape[-2:], BF) for s in sources]
-    outs += [jax.ShapeDtypeStruct(v.shape, F32) for v in (conv_row, rest_row)]
-    outs += [jax.ShapeDtypeStruct((24, vec.shape[1]), F32)]
+
+    def job(rows, lanes):
+        return Reduce.early(rows, lanes) + Reduce.late(rows, lanes, 1) + Reduce.sems()
+
     return pl.pallas_call(
-        functools.partial(reduce_kernel, parts),
+        functools.partial(first_back_kernel, sizes),
         out_shape=outs,
-        in_specs=[ANY] * len(sources) + [VM] * 3,
-        out_specs=[VM] * len(outs),
-        scratch_shapes=scratch,
+        in_specs=[VM] * 12 + [ANY] * 2,
+        out_specs=[VM] * 8,
+        scratch_shapes=[
+            pltpu.VMEM(w.shape, BF),
+            pltpu.VMEM((crops, 18, 16, 3 * ch), BF),
+            pltpu.VMEM((2, ch), F32),
+            pltpu.VMEM((8, ch), F32),
+            pltpu.VMEM((3, 8, ch), F32),
+            pltpu.VMEM((4, 32, ch), F32),
+            pltpu.SemaphoreType.DMA((7,)),
+            pltpu.SemaphoreType.DMA((7,)),
+        ]
+        + Reduce.late(n_rest, 128, 0)
+        + Reduce.sems()
+        + job(n_rest, 128)
+        + job(n_conv, ch)
+        + job(n_conv, ch // 2)
+        + job(n_conv, ch // 2),
         compiler_params=pltpu.CompilerParams(
-            vmem_limit_bytes=56 * MIB, collective_id=1, has_side_effects=True
+            vmem_limit_bytes=60 * MIB, collective_id=4, has_side_effects=True
         ),
-        cost_estimate=pl.CostEstimate(
-            flops=0, bytes_accessed=sum(s.size * 2 for s in sources), transcendentals=0
-        ),
-    )(*sources, vec, conv_row, rest_row)
+        cost_estimate=pl.CostEstimate(flops=2 * 10**10, bytes_accessed=0, transcendentals=0),
+    )(
+        dc, x, gains, w, a_one, rest_kept, g_down, dg_two, loss, wt, conv_row, rest_row,
+        rest_src, second_src
+    )
+
+
+def finish_kernel(
+    sizes,
+    g_first0,
+    g_first1,
+    g_second,
+    g_down,
+    g_rest0,
+    g_rest1,
+    conv_ref,
+    code_ref,
+    proj_ref,
+    head_ref,
+    conv_row_ref,
+    rest_row_ref,
+    tv_ref,
+    conv_col_ref,
+    code_col_ref,
+    proj_col_ref,
+    head_col_ref,
+    gains_ref,
+    state_ref,
+    loss_ref,
+    conv_outs,
+    rest_outs,
+    gain_outs,
+):
+    n_code, n_proj, n_head, rgb, shards = sizes
+    ch = conv_ref.shape[2]
+    lat = code_ref.shape[1]
+
+    def scales(col, col_sum, over, row_sum, weights, rows, width):
+        rows = rows * shards
+        col_new = 0.5 * col + 0.5 * (col_sum / rows + EPS_SQ)
+        row_mean = row_sum / rows
+        upd_sq = row_mean * jnp.sum(over / col_new, axis=1, keepdims=True)
+        rms_u = jnp.sqrt(upd_sq / (rows * width))
+        scale = jnp.sqrt(jnp.sum(weights, axis=1, keepdims=True) / (rows * width))
+        factor = RATE * scale / jnp.maximum(1.0, rms_u)
+        return col_new, factor * lax.rsqrt(col_new), row_mean
+
+    def line(k):
+        return tv_ref[k : k + 1, :]
+
+    cg, cc, cn, cl = conv_outs
+    for j, parts in enumerate(((g_first0, g_first1), (g_second,), (g_down,))):
+        n = conv_ref.shape[1]
+        col_new, q, row_mean = scales(
+            conv_col_ref[j : j + 1, :], line(j), line(3 + j), line(6 + j)[:, :1], line(24 + j), n, ch
+        )
+        cc[j : j + 1, :] = col_new
+        m = n // 4
+        for k in range(4):
+            r = lax.rsqrt(conv_row_ref[j, k] / row_mean)
+            rows = slice(k * m, (k + 1) * m)
+            for p, part in enumerate(parts):
+                width = part.shape[2]
+                lanes = slice(p * width, (p + 1) * width)
+                g = part[k].astype(F32)
+                new = conv_ref[j, rows, lanes] - g * r * q[:, lanes]
+                cg[j, rows, lanes] = g
+                cn[j, rows, lanes] = new
+                cl[j, rows, lanes] = new.astype(BF)
+    cols = (code_col_ref, proj_col_ref, head_col_ref)
+    spans = ((0, n_code, lat), (n_code, n_proj, lat), (n_code + n_proj, n_head, rgb))
+    for m, (w_ref, (start, size, width)) in enumerate(zip((code_ref, proj_ref, head_ref), spans)):
+        og, oc, on, ol = rest_outs[m]
+        col_new, q, row_mean = scales(
+            cols[m][...],
+            line(9 + m)[:, :lat],
+            line(9 + m)[:, lat:],
+            line(12 + m)[:, :1],
+            line(27 + m)[:, :lat],
+            w_ref.shape[0],
+            width,
+        )
+        oc[...] = col_new
+        news = []
+        for k in range(4):
+            g = jnp.concatenate([g_rest0[k].astype(F32), g_rest1[k].astype(F32)], axis=1)
+            g = g[start : start + size]
+            r = lax.rsqrt(rest_row_ref[k, start : start + size] / row_mean)
+            rows = slice(k * size, (k + 1) * size)
+            new = w_ref[rows, :] - g * r * q
+            og[rows, :] = g
+            on[rows, :] = new
+            if size % 16:
+                news.append(new)
+            else:
+                ol[rows, :] = new.astype(BF)
+        if news:
+            ol[...] = jnp.concatenate(news, axis=0).astype(BF)
+    loss_ref[...] = jnp.sum(line(20), axis=1, keepdims=True)
+    grad = tv_ref[16:20, :]
+    state = 0.5 * state_ref[...] + 0.5 * (grad * grad + EPS_SQ)
+    update = grad * lax.rsqrt(state)
+    gains = gains_ref[...]
+
+    def rms(v):
+        return jnp.sqrt(
+            jnp.sum(jnp.sum(v * v, axis=1, keepdims=True), axis=0, keepdims=True) / v.size
+        )
+
+    gain_outs[0][...] = grad
+    gain_outs[1][...] = state
+    gain_outs[2][...] = gains - RATE * rms(gains) * update / jnp.maximum(1.0, rms(update))
+
+
+def finish_call(sizes, grads, weights, rows, tv, cols, gains, state):
+    conv_w, code_w, proj_w, head_w = weights
+    lat = code_w.shape[1]
+
+    def shape(dims, dtype=F32):
+        return jax.ShapeDtypeStruct(dims, dtype)
+
+    def matrix(w, col):
+        return [shape(w.shape), shape(col), shape(w.shape), shape(w.shape, BF)]
+
+    outs = [shape((1, 1)), matrix(conv_w, (3, conv_w.shape[2]))]
+    outs += [[matrix(w, (1, lat)) for w in (code_w, proj_w, head_w)]]
+    outs += [[shape(gains.shape)] * 3]
+    args = [*grads, *weights, *rows, tv, *cols, gains, state]
+    return pl.pallas_call(
+        functools.partial(finish_kernel, sizes),
+        out_shape=outs,
+        in_specs=[VM] * len(args),
+        out_specs=jax.tree.map(lambda _: VM, outs),
+        compiler_params=pltpu.CompilerParams(vmem_limit_bytes=56 * MIB),
+        cost_estimate=pl.CostEstimate(flops=10**7, bytes_accessed=2 * 10**7, transcendentals=0),
+    )(*args)
 
 
 def contract_last(left, right):
@@ -875,7 +1440,7 @@
     return col_new, new
 
 
-def local(
+def local_any(
     features,
     target,
     mask,
@@ -897,7 +1462,6 @@
 ):
     ranks = lax.axis_size("rows")
     shards = lax.axis_size("batch")
-    fast = (ranks, shards) == (4, 8)
     me = lax.axis_index("rows")
     crops_all = features.shape[0] * shards
     ch = features.shape[3]
@@ -913,11 +1477,31 @@
         size = v.shape[0] // ranks
         return lax.dynamic_slice_in_dim(v, me * size, size, 0)
 
+    conv_piece = jnp.transpose(my_part(conv_w).astype(BF), (1, 0, 2))
+    head_wide = jnp.pad(head_w, ((0, 0), (0, lat - rgb)))
+    rest_piece = jnp.concatenate(
+        [my_part(code_w).astype(BF), my_part(proj_w).astype(BF), my_part(head_wide).astype(BF)]
+    )
     n_code, n_proj, n_head = (v.shape[0] // ranks for v in (code_w, proj_w, head_w))
-    head_wide = jnp.pad(head_w, ((0, 0), (0, lat - rgb)))
-    crops = features.shape[0] // ranks
+    w_all = [lax.all_gather(conv_piece[0], BOTH, axis=0, tiled=True)]
+    later = lax.all_gather(conv_piece[1:], BOTH, axis=0)
+    later = jnp.transpose(later, (1, 0, 2, 3)).reshape(2, -1, ch)
+    w_all += [later[0], later[1]]
+    rest = lax.all_gather(rest_piece, BOTH, axis=0)
+    code_all = rest[:, :n_code].reshape(-1, lat)
+    proj_all = rest[:, n_code : n_code + n_proj].reshape(-1, lat)
+    head_all = rest[:, n_code + n_proj :, :rgb].reshape(-1, rgb)
+
+    x = whole_crops(features)
+    target, mask, codes = whole_crops(target), whole_crops(mask), whole_crops(codes)
+    crops = x.shape[0]
     cells = height * width
+    x = x.reshape(crops, cells, ch)
     lat_cells = crops * cells // 4
+    target = target.reshape(lat_cells, rgb)
+    mask = mask.reshape(lat_cells, -1)
+    codes = codes.reshape(lat_cells, -1)
+
     conv_flops = 2 * crops * cells * 9 * ch * ch
     three = pltpu.VMEM((18, 16, 3 * ch), BF)
     fold = pltpu.VMEM((ch // 128, cells, 128), F32)
@@ -927,72 +1511,25 @@
 
     dw_shape = jax.ShapeDtypeStruct((9 * ch, ch), BF)
     dg_shape = jax.ShapeDtypeStruct((2, ch), F32)
-    wide_shape = jax.ShapeDtypeStruct((lat_cells, 9 * ch), BF)
-    s_shape = jax.ShapeDtypeStruct((lat_cells, ch), BF)
-
-    if fast:
-        w_mine = jnp.transpose(conv_w.astype(BF), (1, 0, 2)).reshape(3, 2, 2, -1, ch)
-        rest_piece = jnp.concatenate(
-            [v.astype(BF).reshape(ranks, -1, lat) for v in (code_w, proj_w, head_wide)]
-            + [jnp.zeros((ranks, 16 - n_head, lat), BF)],
-            axis=1,
-        )
-        side = jnp.concatenate(
-            [target, mask.astype(F32), codes.astype(F32)], axis=-1
-        ).reshape(ranks, crops, -1, rgb + 8)
-        out = forward_call(
-            features.reshape(ranks, crops, -1, ch),
-            side,
-            w_mine,
-            rest_piece.reshape(2, 2, -1, lat),
-            gains,
-        )
-        x = out[0].reshape(crops, cells, ch)
-        w_all = out[2:5]
-        rest = out[5].reshape(ranks * shards, -1, lat)
-        side = out[1].reshape(lat_cells, -1)
-        target, mask, codes = (side[:, :rgb], side[:, rgb : rgb + 4], side[:, rgb + 4 :])
-        codes = codes.astype(jnp.int32)
-        a_one, c_one, a_two, windows, s_low = out[6:]
-    else:
-
-        def whole_crops(v):
-            return lax.all_to_all(v, "rows", split_axis=0, concat_axis=1, tiled=True)
-
-        def my_part(v):
-            size = v.shape[0] // ranks
-            return lax.dynamic_slice_in_dim(v, me * size, size, 0)
-
-        conv_piece = jnp.transpose(my_part(conv_w).astype(BF), (1, 0, 2))
-        rest_piece = jnp.concatenate(
-            [my_part(code_w).astype(BF), my_part(proj_w).astype(BF), my_part(head_wide).astype(BF)]
-        )
-        w_all = [lax.all_gather(conv_piece[0], BOTH, axis=0, tiled=True)]
-        later = lax.all_gather(conv_piece[1:], BOTH, axis=0)
-        later = jnp.transpose(later, (1, 0, 2, 3)).reshape(2, -1, ch)
-        w_all += [later[0], later[1]]
-        rest = lax.all_gather(rest_piece, BOTH, axis=0)
-        x = whole_crops(features).reshape(crops, cells, ch)
-        target = whole_crops(target).reshape(lat_cells, rgb)
-        mask = whole_crops(mask).reshape(lat_cells, -1)
-        codes = whole_crops(codes).reshape(lat_cells, -1)
-        a_one, c_one = kernel_call(
-            first_conv_kernel, [big(BF), big(F32)], [three], conv_flops, x, gains, w_all[0]
-        )
-        a_two, windows, s_low = kernel_call(
-            second_conv_kernel,
-            [big(BF), wide_shape, s_shape],
-            [three, fold],
-            conv_flops,
-            c_one,
-            x,
-            gains,
-            w_all[1],
-            w_all[2],
-        )
-    code_all = rest[:, :n_code].reshape(-1, lat)
-    proj_all = rest[:, n_code : n_code + n_proj].reshape(-1, lat)
-    head_all = rest[:, n_code + n_proj : n_code + n_proj + n_head, :rgb].reshape(-1, rgb)
+
+    a_one, c_one = kernel_call(
+        first_conv_kernel, [big(BF), big(F32)], [three], conv_flops, x, gains, w_all[0]
+    )
+    a_two, windows, s_low = kernel_call(
+        second_conv_kernel,
+        [
+            big(BF),
+            jax.ShapeDtypeStruct((lat_cells, 9 * ch), BF),
+            jax.ShapeDtypeStruct((lat_cells, ch), BF),
+        ],
+        [three, fold],
+        conv_flops,
+        c_one,
+        x,
+        gains,
+        w_all[1],
+        w_all[2],
+    )
 
     lat_count = crops_all * cells // 4 * lat
     pix_count = crops_all * cells * 3
@@ -1054,87 +1591,38 @@
     d_gains = jnp.concatenate([gain_one, gain_two], axis=0)
 
     devices = ranks * shards
+
+    def to_owner(v):
+        return lax.psum_scatter(v, BOTH, scatter_dimension=0, tiled=True)
+
+    def to_rows(v):
+        return lax.all_gather(v, "rows", axis=0)
+
     pad = jnp.pad(d_head, ((0, 0), (0, lat - rgb)))
-    loss_part = recon_part + quant_part
-    mats_old = [
-        (conv_w, conv_row, conv_col),
-        (proj_w[:, None, :], proj_row[:, None], proj_col[None, :]),
-        (code_w[:, None, :], code_row[:, None], code_col[None, :]),
-        (head_w[:, None, :], head_row[:, None], head_col[None, :]),
-    ]
-    wt_sq = [jnp.sum(m[0] * m[0], axis=(0, 2)) for m in mats_old]
-    if fast:
-        packed = jnp.zeros((devices, 16 - n_head, lat), BF)
-        rest_grad = jnp.concatenate(
-            [v.astype(BF).reshape(devices, -1, lat) for v in (d_code, d_proj, pad)] + [packed],
-            axis=1,
-        )
-        sources = [d.reshape(4, 2, 2, 2, -1, ch) for d in (d_first, d_second, d_down)]
-        sources.append(rest_grad.reshape(4, 2, 2, 2, -1, lat))
-        quarter = jnp.concatenate(wt_sq) / 4
-        row5 = jnp.pad(jnp.concatenate([loss_part[None], quarter]), (0, ch - 1 - quarter.shape[0]))
-        vec = jnp.concatenate([d_gains, row5[None], jnp.zeros((3, ch), F32)])
-        conv_rows4 = jnp.transpose(conv_row).reshape(3, 4, -1, 1)
-        rest_rows4 = jnp.concatenate(
-            [v.reshape(4, -1) for v in (code_row, proj_row, head_row)]
-            + [jnp.ones((4, 16 - n_head), F32)],
-            axis=1,
-        )[:, :, None]
-        out = reduce_call(sources, vec, conv_rows4, rest_rows4, (n_code, n_proj, n_head, rgb))
-        conv_new_rows = jnp.transpose(out[4].reshape(3, -1))
-        rest_new = out[5][:, :, 0]
-        cuts = (n_code, n_code + n_proj, n_code + n_proj + n_head)
-        code_rn, proj_rn, head_rn = (
-            v.reshape(-1, 1) for v in jnp.split(rest_new, cuts, axis=1)[:3]
-        )
-        rows_one = [conv_new_rows, proj_rn, code_rn, head_rn]
-        tv = out[6]
-        loss = tv[20, 0]
-        g_gain = tv[16:20]
-        wt_all = tv[20, 1:7]
-        shard_rows = [m[0].shape[0] for m in mats_old]
-        eps = [EPS_SQ * n * shards for n in shard_rows]
-        sums = [
-            (tv[0:3] + eps[0], tv[6:9, 0], tv[3:6], wt_all[0:3]),
-            (tv[10:11, :lat] + eps[1], tv[13:14, 0], tv[10:11, lat:], wt_all[3:4]),
-            (tv[9:10, :lat] + eps[2], tv[12:13, 0], tv[9:10, lat:], wt_all[4:5]),
-            (tv[11:12, :rgb] + eps[3], tv[14:15, 0], tv[11:12, lat : lat + rgb], wt_all[5:6]),
-        ]
-        g_conv = jnp.transpose(
-            jnp.stack([v.reshape(-1, ch) for v in out[:3]]).astype(F32), (1, 0, 2)
-        )
-        rest_full = out[3].astype(F32)
-    else:
-
-        def to_owner(v):
-            return lax.psum_scatter(v, BOTH, scatter_dimension=0, tiled=True)
-
-        def to_rows(v):
-            return lax.all_gather(v, "rows", axis=0)
-
-        rest_grad = jnp.concatenate(
-            [v.astype(BF).reshape(devices, -1, lat) for v in (d_code, d_proj, pad)], axis=1
-        )
-        rest_mine = to_owner(rest_grad.reshape(-1, lat))
-        conv_mine = [to_owner(v) for v in (d_first, d_second, d_down)]
-        rest_full = to_rows(rest_mine).astype(F32)
-        conv_full = to_rows(jnp.stack(conv_mine)).astype(F32)
-        g_conv = jnp.transpose(conv_full, (0, 2, 1, 3)).reshape(-1, 3, ch)
-        loss, g_gain = lax.psum((loss_part, d_gains), BOTH)
-
+    rest_grad = jnp.concatenate(
+        [v.astype(BF).reshape(devices, -1, lat) for v in (d_code, d_proj, pad)], axis=1
+    )
+    rest_mine = to_owner(rest_grad.reshape(-1, lat))
+    conv_mine = [to_owner(v) for v in (d_first, d_second, d_down)]
+    rest_full = to_rows(rest_mine).astype(F32)
+    conv_full = to_rows(jnp.stack(conv_mine)).astype(F32)
+    g_conv = jnp.transpose(conv_full, (0, 2, 1, 3)).reshape(-1, 3, ch)
     g_code = rest_full[:, :n_code].reshape(-1, lat)
     g_proj = rest_full[:, n_code : n_code + n_proj].reshape(-1, lat)
-    g_head = rest_full[:, n_code + n_proj : n_code + n_proj + n_head, :rgb].reshape(-1, rgb)
-    grads = [g_conv, g_proj[:, None, :], g_code[:, None, :], g_head[:, None, :]]
-    if not fast:
-        rows_new = [row_part(grad, m[1]) for grad, m in zip(grads, mats_old)]
-        rows_one = [r[0] for r in rows_new]
-        sums = lax.psum([r[1:] for r in rows_new], "batch")
-        sums = [
-            (s[0], s[1], s[2], w) for s, w in zip(sums, lax.psum(wt_sq, "batch"))
-        ]
+    g_head = rest_full[:, n_code + n_proj :, :rgb].reshape(-1, rgb)
+
+    mats = [
+        (g_conv, conv_w, conv_row, conv_col),
+        (g_proj[:, None, :], proj_w[:, None, :], proj_row[:, None], proj_col[None, :]),
+        (g_code[:, None, :], code_w[:, None, :], code_row[:, None], code_col[None, :]),
+        (g_head[:, None, :], head_w[:, None, :], head_row[:, None], head_col[None, :]),
+    ]
+    rows_new = [row_part(grad, row) for grad, weight, row, col in mats]
+    wt_sq = [jnp.sum(weight * weight, axis=(0, 2)) for grad, weight, row, col in mats]
+    sums = lax.psum([r[1:] + (w,) for r, w in zip(rows_new, wt_sq)], "batch")
+    loss, g_gain = lax.psum((recon_part + quant_part, d_gains), BOTH)
     done = [
-        finish(g, m[0], r, m[2], *s) for g, m, r, s in zip(grads, mats_old, rows_one, sums)
+        finish(m[0], m[1], r[0], m[3], *s) for m, r, s in zip(mats, rows_new, sums)
     ]
 
     state_new = 0.5 * gain_state + 0.5 * (g_gain * g_gain + EPS_SQ)
@@ -1147,28 +1635,169 @@
     return (
         loss,
         g_conv,
-        rows_one[0],
+        rows_new[0][0],
         done[0][0],
         conv_new,
         conv_new.astype(BF),
         g_proj,
-        rows_one[1][:, 0],
+        rows_new[1][0][:, 0],
         done[1][0][0],
         proj_new,
         proj_new.astype(BF),
         g_code,
-        rows_one[2][:, 0],
+        rows_new[2][0][:, 0],
         done[2][0][0],
         code_new,
         code_new.astype(BF),
         g_head,
-        rows_one[3][:, 0],
+        rows_new[3][0][:, 0],
         done[3][0][0],
         head_new,
         head_new.astype(BF),
         g_gain,
         state_new,
         gains_new,
+    )
+
+
+def local_fast(
+    features,
+    target,
+    mask,
+    codes,
+    conv_w,
+    proj_w,
+    code_w,
+    head_w,
+    gains,
+    conv_row,
+    conv_col,
+    proj_row,
+    proj_col,
+    code_row,
+    code_col,
+    head_row,
+    head_col,
+    gain_state,
+):
+    ranks = lax.axis_size("rows")
+    shards = lax.axis_size("batch")
+    crops_all = features.shape[0] * shards
+    crops = features.shape[0] // ranks
+    ch = features.shape[3]
+    cells = features.shape[1] * ranks * features.shape[2]
+    lat, rgb = proj_w.shape[1], head_w.shape[1]
+    lat_cells = crops * cells // 4
+    n_code, n_proj, n_head = (v.shape[0] // ranks for v in (code_w, proj_w, head_w))
+    sizes = (n_code, n_proj, n_head, rgb)
+    conv_rows = jnp.transpose(conv_w, (1, 0, 2))
+    head_wide = jnp.pad(head_w, ((0, 0), (0, lat - rgb)))
+
+    def lanes(v, n):
+        return jnp.pad(v, ((0, 0),) * (v.ndim - 1) + ((0, n - v.shape[-1]),))
+
+    side = [lanes(target, 16), lanes(jnp.repeat(mask.astype(F32), 3, axis=-1), 16)]
+    side = lanes(jnp.concatenate(side + [codes.astype(F32)], axis=-1), 128)
+    out = forward_call(
+        features.reshape(ranks, crops, -1, ch),
+        side.reshape(ranks, crops, -1, 128),
+        conv_rows,
+        code_w,
+        proj_w,
+        head_wide,
+        gains,
+    )
+    x = out[0].reshape(crops, cells, ch)
+    side = out[1].reshape(lat_cells, 128)
+    w_all, rest = out[2:5], out[5]
+    a_one, c_one, a_two, windows, s_low, wt = out[6:]
+    codes = side[:, 32:36].astype(jnp.int32).reshape(-1)
+    n_rest = rest.shape[-2]
+    d_s, loss, rest_grad, d_down = quantizer_call(
+        codes,
+        rest.reshape(-1, n_rest, lat),
+        side,
+        s_low,
+        windows,
+        crops_all * cells // 4 * lat,
+        crops_all * cells * 3,
+        rgb,
+        n_code,
+    )
+
+    def shards_of(v):
+        return v.reshape(4, 2, 2, 2, -1, v.shape[-1])
+
+    rest_src = shards_of(rest_grad)
+    d_c_one, d_second, dg_two, g_down, rest_kept = second_back_call(
+        d_s, w_all[2], w_all[1], c_one, a_two, gains, shards_of(d_down), rest_src
+    )
+    conv_row4 = jnp.transpose(conv_row).reshape(3, 4, -1, 1)
+    rest_row4 = [v.reshape(4, -1) for v in (code_row, proj_row, head_row)]
+    rest_row4.append(jnp.ones((4, n_rest - n_code - n_proj - n_head), F32))
+    rest_row4 = jnp.concatenate(rest_row4, axis=1)[:, :, None]
+    out = first_back_call(
+        sizes,
+        d_c_one,
+        x,
+        gains,
+        w_all[0],
+        a_one,
+        rest_kept,
+        g_down,
+        dg_two,
+        loss,
+        wt,
+        conv_row4,
+        rest_row4,
+        rest_src,
+        shards_of(d_second),
+    )
+    g_first0, g_first1, g_second, g_rest0, g_rest1, conv_rn, rest_rn, tv = out
+    head_col_wide = jnp.pad(head_col, (0, lat - rgb), constant_values=1.0)
+    loss, conv_outs, rest_outs, gain_outs = finish_call(
+        sizes + (shards,),
+        (g_first0, g_first1, g_second, g_down, g_rest0, g_rest1),
+        (conv_rows, code_w, proj_w, head_wide),
+        (conv_rn, rest_rn),
+        tv,
+        (conv_col, code_col[None], proj_col[None], head_col_wide[None]),
+        gains,
+        gain_state,
+    )
+    conv_g, conv_c, conv_n, conv_l = conv_outs
+    code_o, proj_o, head_o = rest_outs
+    cuts = (n_code, n_code + n_proj, n_code + n_proj + n_head)
+    code_r, proj_r, head_r = (
+        v.reshape(-1) for v in jnp.split(rest_rn[:, :, 0], cuts, axis=1)[:3]
+    )
+
+    def back(v):
+        return jnp.transpose(v, (1, 0, 2))
+
+    return (
+        loss[0, 0],
+        back(conv_g),
+        jnp.transpose(conv_rn.reshape(3, -1)),
+        conv_c,
+        back(conv_n),
+        back(conv_l),
+        proj_o[0],
+        proj_r,
+        proj_o[1][0],
+        proj_o[2],
+        proj_o[3],
+        code_o[0],
+        code_r,
+        code_o[1][0],
+        code_o[2],
+        code_o[3],
+        head_o[0][:, :rgb],
+        head_r,
+        head_o[1][0, :rgb],
+        head_o[2][:, :rgb],
+        head_o[3][:, :rgb],
+        *gain_outs,
     )
 
 
@@ -1179,8 +1808,9 @@
     placed += (mat, P()) + (vec, P()) * 3 + (P(),)
     conv_outs = (P("batch", None, None), mat, P(), P("batch", None, None), P("batch", None, None))
     mat_outs = (mat, vec, P(), mat, mat)
+    fast = (mesh.shape["rows"], mesh.shape["batch"]) == (4, 8)
     return jax.shard_map(
-        local,
+        local_fast if fast else local_any,
         mesh=mesh,
         in_specs=placed,
         out_specs=(P(),) + conv_outs + mat_outs * 3 + (P(),) * 3,

time: 577 us -> 398 us (0.69)
  other arithmetic: 85.9 us -> 4.5 us
  local copies, waits for them, and re-layouts: 64.3 us -> 14.9 us
  Pallas kernels: 404 us -> 377 us
  matrix products: 10.4 us -> 0 us
  between operations: 9.91 us -> 0.8 us
    pallas_call x5, Pallas kernels: 404 us -> 377 us  [the longest x1 144 us: forward_call(): pl.pallas_call(forward_kernel, out_shape=outs, in_specs=[ANY] * 2 + [VM]...]
    scatter-add x1 -> x0, other arithmetic: 18.7 us -> none  [local(): jax.ops.segment_sum(d_picked.reshape(-1, lat), codes.reshape(-1), num_seg...]
    convert_element_type x9 -> x3, other arithmetic: 19.4 us -> 2.61 us  [the longest x1 1.08 us: local_fast(): codes = side[:, 32:36].astype(jnp.int32).reshape(-1)]
    reduce_sum x9 -> x0, other arithmetic: 16.3 us -> none  [the longest x4 8.55 us: local(): wt_sq = [jnp.sum(m[0] * m[0], axis=(0, 2)) for m in mats_old]]
    gather x1 -> x0, local copies, waits for them, and re-layouts: 13 us -> none  [local(): picked = code_all[codes].astype(F32)]
    slice x6 -> x3, local copies, waits for them, and re-layouts: 13.9 us -> 2.14 us  [the longest x1 0.72 us: local_fast(): head_o[0][:, :rgb]]
    dot_general x6 -> x0, matrix products: 10.4 us -> none  [the longest x2 3.86 us: contract_rows(): lax.dot_general(left, right, (((0,), (0,)), ((), ())), preferred_element_...]
    concatenate x5 -> x1, other arithmetic: 11 us -> 0.92 us  [local_fast(): side = lanes(jnp.concatenate(side + [codes.astype(F32)], axis=-1), 128)]
where the time goes in v2:
time: 398 us
  Pallas kernels  377 us (95%)
  local copies, waits for them, and re-layouts  14.9 us (4%)
  other arithmetic  4.5 us (1%)
    pallas_call x1, Pallas kernels, forward_call(): pl.pallas_call(forward_kernel, out_shape=outs, in_specs=[ANY] * 2 + [VM]...  144 us
    pallas_call x1, Pallas kernels, first_back_call(): pl.pallas_call(functools.partial(first_back_kernel, sizes), out_shape=out...  108 us
    pallas_call x1, Pallas kernels, second_back_call(): pl.pallas_call(second_back_kernel, out_shape=outs, in_specs=[VM] * 6 + [A...  77.4 us
    pallas_call x1, Pallas kernels, quantizer_call(): pl.pallas_call(functools.partial(quantizer_kernel, (lat_count, pix_count,...  37.5 us
    pallas_call x1, Pallas kernels, finish_call(): pl.pallas_call(functools.partial(finish_kernel, sizes), out_shape=outs, i...  10.2 us

profile of v2, /device:TPU:0, one launch (start us, length us, event | category | flops | bytes accessed | tf_op | source)
XLA Modules:
  0.0 397.6 jit_solution(15189080469135220862)
XLA Ops:
  0.7 0.8 copy.52
  1.4 0.6 pad.22.head_ref
  2.1 0.8 convert_element_type.16
  2.8 0.8 convert_element_type.17
  3.6 0.9 fusion
  4.5 0.2 copy.58
  4.8 0.7 pad.21.clone
  5.5 143.8 %shard_map.361 = (bf16[8,4,64,512]{3,2,1,0:T(8,128)(2,1)}, f32[8,4,16,128]{3,2,1,0:T(8,128)}, bf16[4608,512]{1,0:T(8,128)(2,1)}, bf16[4608,512]{1,0:T(8,128)(2,1...) custom-call(bf16[4,8,64,512]{3,2,1,0:T(8,128)(2,1)} %bitcast.42, ...), custom_call_target="tpu_custom_call" | custom-call | flops 24159191040 | tf_op jit(solution)/shard_map/pallas_call | solution.py:753
  149.3 1.1 slice_convert_fusion
  150.4 0.8 reshape.106.codes_ref
  151.2 37.5 %shard_map.362 = (bf16[512,512]{1,0:T(8,128)(2,1)}, f32[8,512]{1,0:T(8,128)}, bf16[32,544,256]{2,1,0:T(8,128)(2,1)}, bf16[4608,512]{1,0:T(8,128)(2,1)}) custom-call(s32[2048]{0:T(1024)} %reshape.106.codes_ref, bf16[32,544,256]{2,1,0:T(8,128)(2,1)} %bitcast.48, f32[512,128]{1,0:T(8,128)} %bitcast.33, bf16[512,512]{1,0:T(8,128)(2,1)} %get-tuple-element.75.sl_ref, ...), custom_call_target="tpu_custom_call" | custom-call | flops 10000000000 | bytes 10000000 | tf_op jit(solution)/shard_map/pallas_call | solution.py:920
  188.7 0.0 copy-start.3
  188.7 0.0 copy-start.4
  188.7 0.0 copy-start.5
  188.7 0.0 copy-start.2
  188.7 77.4 %shard_map.363 = (bf16[8,256,512]{2,1,0:T(8,128)(2,1)}, bf16[4608,512]{1,0:T(8,128)(2,1)}, f32[2,512]{1,0:T(2,128)}, bf16[4,144,512]{2,1,0:T(8,128)(2,1)}, bf16[4,544,128]{2,1,0:T(8,128)(2,1)}) custom-call(bf16[512,512]{1,0:T(8,128)(2,1)} %get-tuple-element.77.ds_ref, bf16[4608,512]{1,0:T(8,128)(2,1)} %get-tuple-element.78.w_down_ref, ...), custom_call_target="tpu_custom_call" | custom-call | flops 20000000000 | tf_op jit(solution)/shard_map/pallas_call | solution.py:1007
  266.1 0.0 copy-done.3
  266.2 0.1 pad.27.clone
  266.2 0.0 copy-done.4
  266.2 0.1 reshape.113
  266.3 0.0 copy-done.5
  266.3 0.1 reshape.114
  266.4 0.1 maximum_bitcast_fusion
  266.5 1.4 copy.54.rest_row_ref
  267.9 0.0 copy-done.2
  267.9 1.7 reshape.120.conv_row_ref
  269.5 0.0 copy-start.6
  269.6 108.4 %shard_map.364 = (bf16[4,144,256]{2,1,0:T(8,128)(2,1)}, bf16[4,144,256]{2,1,0:T(8,128)(2,1)}, bf16[4,144,512]{2,1,0:T(8,128)(2,1)}, bf16[4,544,128]{2,1,0:T(8,12...) custom-call(bf16[8,256,512]{2,1,0:T(8,128)(2,1)} %get-tuple-element., ...), custom_call_target="tpu_custom_call" | custom-call | flops 20000000000 | tf_op jit(solution)/shard_map/pallas_call | solution.py:1248
  378.0 0.0 copy-done.6
  378.0 0.6 pad.23
  378.6 0.0 copy-start
  378.6 10.2 %shard_map.365 = (f32[1,1]{1,0:T(1,128)}, f32[3,576,512]{2,1,0:T(8,128)}, f32[3,512]{1,0:T(4,128)}, f32[3,576,512]{2,1,0:T(8,128)}, bf16[3,576,512]{2,1,0:T(8,12...) custom-call(bf16[4,144,256]{2,1,0:T(8,128)(2,1)} %get-tuple-element., ...), custom_call_target="tpu_custom_call" | custom-call | flops 10000000 | bytes 20000000 | tf_op jit(solution)/shard_map/pallas_call | solution.py:1400
  388.8 0.7 slice.16
  389.5 0.7 copy.55
  390.2 0.7 slice.18
  390.9 0.7 copy.56
  391.6 0.7 slice.19
  392.3 0.7 copy.57
  393.0 1.2 slice_bitcast_fusion.1
  394.2 0.0 copy-done
  394.2 0.4 reduce.1
  394.6 0.6 copy.59
  395.2 0.0 copy-done.1
  395.2 0.5 reduce
  395.7 0.7 reshape.116
  396.4 0.6 reshape.117
  397.0 0.1 split.14
  397.0 0.6 reshape.119
  (8 shorter events, 0.0 us)
Async XLA Ops:
  188.7 77.5 %copy-start.3 = (f32[2048]{0:T(1024)S(1)}, f32[2048]{0:T(1024)}, u32[]{:S(2)}) copy-start(f32[2048]{0:T(1024)} %param.31) | copy-start | bytes 24580
  188.7 77.6 %copy-start.4 = (f32[64]{0:T(128)S(1)}, f32[64]{0:T(128)}, u32[]{:S(2)}) copy-start(f32[64]{0:T(128)} %param.29) | copy-start | bytes 772
  188.7 77.6 %copy-start.5 = (f32[32]{0:T(128)S(1)}, f32[32]{0:T(128)}, u32[]{:S(2)}) copy-start(f32[32]{0:T(128)} %param.33) | copy-start | bytes 388
  188.7 79.2 %copy-start.2 = (f32[576,3]{0,1:T(4,128)S(1)}, f32[576,3]{0,1:T(4,128)}, u32[]{:S(2)}) copy-start(f32[576,3]{0,1:T(4,128)} %param.27) | copy-start | bytes 20740
  269.5 108.4 %copy-start.6 = (f32[12]{0:T(128)S(1)}, f32[12]{0:T(128)}, u32[]{:S(2)}) copy-start(f32[12]{0:T(128)} %param.34) | copy-start | bytes 148
  378.6 15.6 %copy-start = (f32[4,544,1]{2,1,0:T(8,128)S(1)}, f32[4,544,1]{2,1,0:T(8,128)}, u32[]{:S(2)}) copy-start(f32[4,544,1]{2,1,0:T(8,128)} %get-tuple-element.100.rest_row_ref) | copy-start | bytes 26116
  378.6 16.6 %copy-start.1 = (f32[3,4,144,1]{3,2,1,0:T(8,128)S(1)}, f32[3,4,144,1]{3,2,1,0:T(8,128)}, u32[]{:S(2)}) copy-start(f32[3,4,144,1]{3,2,1,0:T(8,128)} %get-tuple-element.99.conv_row_ref) | copy-start | bytes 20740

commit v3 on v2

--- a/solution.py
+++ b/solution.py
@@ -267,10 +267,7 @@
     return d_act * sig * (1.0 + h * (1.0 - sig)), vhat, rstd
 
 
-def unit_back(dc_ref, v_of, gains_ref, w_ref, dg_ref, d3, row, din_ref=None, tick=None):
-    crops, cells, ch = dc_ref.shape
-    dg_ref[...] = jnp.zeros_like(dg_ref)
-
+def shift_all(dc_ref, d3, tick=None):
     def crop(i, carry):
         if tick is not None:
             tick(i)
@@ -278,7 +275,19 @@
         slot = d3.at[i]
         zero_edges(slot)
         fill_three(slot, shifted(d, -1), d, shifted(d, 1))
-        d_act = conv_rows_back(slot, w_ref)
+        return carry
+
+    lax.fori_loop(0, dc_ref.shape[0], crop, 0)
+
+
+def unit_back(v_of, gains_ref, w_ref, dg_ref, d3, row, din_ref=None, tick=None):
+    crops, cells, ch = d3.shape[0], 256, d3.shape[3] // 3
+    dg_ref[...] = jnp.zeros_like(dg_ref)
+
+    def crop(i, carry):
+        if tick is not None:
+            tick(i)
+        d_act = conv_rows_back(d3.at[i], w_ref)
         gain = gains_ref[row : row + 1, :]
         hg, vhat, rstd = hidden_grad(v_of(i), gain, gains_ref[row + 1 : row + 2, :], d_act)
         one = jnp.sum(hg * vhat, axis=0, keepdims=True)
@@ -305,7 +314,8 @@
     def v_of(i):
         return v_ref[i].astype(F32)
 
-    unit_back(dc_ref, v_of, gains_ref, w_ref, dg_ref, d3, row, din_ref)
+    shift_all(dc_ref, d3)
+    unit_back(v_of, gains_ref, w_ref, dg_ref, d3, row, din_ref)
     for half in range(2):
         conv_weight_grad(a_ref, d3, dw_ref, half)
 
@@ -365,28 +375,29 @@
 
 
 class Gather:
-    def __init__(self, place, src, dst, send, recv, by_x):
+    def __init__(self, place, src, dst, send, recv, route):
         self.p, self.src, self.dst, self.send, self.recv = place, src, dst, send, recv
-        self.by_x = by_x
-        self.steps = 4 if by_x else 3
+        self.route = "z" + route + "c"
+        self.steps = len(self.route)
 
     def copies(self, step):
         p, src, dst, send, recv = self.p, self.src, self.dst, self.send, self.recv
-        if step == 0:
-            mine = (p.c, p.x) if self.by_x else (p.c,)
+        axis = self.route[step]
+        if axis == "z":
+            mine = (p.c, p.x) if "x" in self.route else (p.c,)
             here, there = src.at[mine], dst.at[(p.z, p.y) + mine]
             out = [
                 remote(here, there, send.at[k], recv.at[k], q) for k, q in enumerate(p.z_peers())
             ]
             return out + [pltpu.make_async_copy(here, there, recv.at[6])]
-        if step == 1:
-            part = dst.at[:, p.y, p.c, p.x] if self.by_x else dst.at[:, p.y, p.c]
-            return [remote(part, part, send.at[3], recv.at[3], p.at(y=1 - p.y))]
-        if step == 2 and self.by_x:
-            part = dst.at[:, :, p.c, p.x]
-            return [remote(part, part, send.at[4], recv.at[4], p.at(x=1 - p.x))]
-        part = dst.at[:, :, p.c]
-        return [remote(part, part, send.at[5], recv.at[5], p.at(c=1 - p.c))]
+        have_y = "y" in self.route[:step]
+        have_x = "x" in self.route[:step] or "x" not in self.route
+        part = dst.at[:, slice(None) if have_y else p.y, p.c]
+        if not have_x:
+            part = dst.at[:, slice(None) if have_y else p.y, p.c, p.x]
+        k = 3 + "yxc".index(axis)
+        peer = {"y": p.at(y=1 - p.y), "x": p.at(x=1 - p.x), "c": p.at(c=1 - p.c)}[axis]
+        return [remote(part, part, send.at[k], recv.at[k], peer)]
 
     def start(self, step):
         for copy in self.copies(step):
@@ -410,11 +421,12 @@
 class Reduce:
     steps = 6
 
-    def __init__(self, place, src, out, mine, one, two, three, kept, four, send, recv):
+    def __init__(self, place, src, out, mine, one, two, three, kept, four, send, recv, turn=True):
         self.p, self.src, self.out = place, src, out
         self.mine, self.one, self.two, self.three, self.four = mine, one, two, three, four
         self.send, self.recv = send, recv
-        first_x = place.c == 0
+        first_x = (place.c == 0) & turn
+        self.turn = turn
         self.f = jnp.where(first_x, place.x, place.y)
         self.g = jnp.where(first_x, place.y, place.x)
         self.f_peer = place.at(
@@ -444,8 +456,8 @@
             out = []
             for k in range(4):
                 y, x = k // 2, k % 2
-                there = jnp.where(p.c == 1, 2 * x + y, 2 * y + x)
-                here = jnp.where(p.c == 0, 2 * x + y, 2 * y + x)
+                there = jnp.where((p.c == 1) & self.turn, 2 * x + y, 2 * y + x)
+                here = jnp.where((p.c == 0) & self.turn, 2 * x + y, 2 * y + x)
                 part = src.at[:, y, 1 - p.c, x]
                 peer = p.at(c=1 - p.c)
                 out.append(remote(part, self.one.at[there], send.at[k], recv.at[k], peer))
@@ -524,6 +536,25 @@
             for copy in self.copies(step):
                 if copy.is_remote:
                     copy.wait_send()
+
+
+PARTS = (
+    ("w0b", "yx", 1, None),
+    ("w1a", "yx", 0, None),
+    ("w0a", "y", 0, None),
+    ("w1b", "yx", 1, None),
+    ("w2b", "yx", 1, None),
+    ("r0", "y", 0, 0),
+    ("r2", "yx", 0, 1),
+    ("r1", "yx", 1, 0),
+    ("w2a", "y", 0, None),
+    ("r3", "y", 1, 1),
+)
+BEFORE = ("w0b1", "w1a1", "w0b2", "w1a2", "w0a1", "w1b1", "w0b3", "w2b1", "w0a2")
+FIRST = {1: ("w1a3", "w1b2"), 2: ("r01",), 4: ("w2b2", "r21"), 7: ("r11", "w1b3")}
+BETWEEN = ("r02",)
+SECOND = {1: ("r22",), 2: ("w2a1",), 3: ("w2b3", "r12"), 6: ("r31", "r23"), 7: ("w2a2",)}
+AFTER = ("r13", "r32")
 
 
 def forward_kernel(
@@ -593,17 +624,34 @@
         n = ref.shape[0] // 32
         return ref.reshape(4, 2, 2, 2, n, ref.shape[1]).at[..., lanes]
 
-    def job(k, src, dst, by_x):
-        return Gather(place, src, dst, g_send.at[k], g_recv.at[k], by_x)
-
-    halves = [slice(0, 256), slice(256, 512)]
-    w0 = [job(k, w_mine.at[0, ..., h], view(wv0, h), False) for k, h in enumerate(halves)]
-    w1 = [job(2 + k, w_mine.at[1, ..., h], view(wv1, h), False) for k, h in enumerate(halves)]
-    w2 = [job(4 + k, w_mine.at[2, ..., h], view(wv2, h), True) for k, h in enumerate(halves)]
-    ends = [slice(0, 128), slice(128, 256)]
-    rest = [
-        job(6 + k, rest_mine.at[..., h], rest_out.at[..., h], k == 0) for k, h in enumerate(ends)
-    ]
+    jobs = {}
+    views = [view(wv0, slice(None)), view(wv1, slice(None)), view(wv2, slice(None)), rest_out]
+    for k, (name, route, lane, row) in enumerate(PARTS):
+        rest = name[0] == "r"
+        src = rest_mine if rest else w_mine.at[int(name[1])]
+        dst = views[3] if rest else views[int(name[1])]
+        n, m = src.shape[-2], src.shape[-1] // 2
+        rows = pl.ds(0, n) if row is None else pl.ds(row * n // 2, n // 2)
+        at = (..., rows, pl.ds(lane * m, m))
+        jobs[name] = Gather(place, src.at[at], dst.at[at], g_send.at[k], g_recv.at[k], route)
+
+    def go(words):
+        for word in words:
+            jobs[word[:-1]].go(int(word[-1]))
+
+    def ticks(table):
+        def tick(i):
+            for when, words in table.items():
+
+                @pl.when(i == when)
+                def _():
+                    go(words)
+
+        return tick
+
+    def whole(names):
+        for name in names:
+            jobs[name].arrive(jobs[name].steps - 1)
 
     cells = []
     for src, dst, base in ((feat, xv, 0), (side, side_out, 4)):
@@ -614,27 +662,23 @@
             )
         cells.append(pltpu.make_async_copy(src.at[rank], dst.at[:, rank], x_recv.at[base + 3]))
 
-    w0[0].start(0)
+    jobs["w0b"].start(0)
     for copy in cells:
         copy.start()
-    w0[1].start(0)
+    cast_conv(1)
+    for name in ("w1a", "w0a", "w1b"):
+        jobs[name].start(0)
+    cast_conv(2)
     cast_rest()
-    cast_conv(1)
-    cast_conv(2)
-    w0[0].go(1)
-    w0[1].arrive(0)
-    w1[0].start(0)
-    rest[0].start(0)
-    w0[0].go(2)
-    w0[1].start(1)
-    w0[0].arrive(2)
-    w0[1].go(2)
+    for name, *_ in PARTS[4:]:
+        jobs[name].start(0)
+    go(BEFORE)
     zero_edges(a3)
     for copy in cells:
         copy.wait_recv()
     keep_x = pltpu.make_async_copy(xv, x_out, o_sem.at[0])
     keep_x.start()
-    w0[1].arrive(2)
+    whole(("w0a", "w0b"))
     keep_w = [
         pltpu.make_async_copy(v, o, o_sem.at[1 + k])
         for k, (v, o) in enumerate(((wv0, w_out0), (wv1, w_out1), (wv2, w_out2)))
@@ -645,78 +689,33 @@
     def crop_x(i):
         return xv[i].reshape(256, ch).astype(F32)
 
+    tick_first, tick_second = ticks(FIRST), ticks(SECOND)
+
     def first(i, carry):
-        @pl.when(i == 1)
-        def _():
-            w1[0].go(1)
-            w1[1].start(0)
-
-        @pl.when(i == 2)
-        def _():
-            rest[0].go(1)
-            w2[0].start(0)
-
-        @pl.when(i == 5)
-        def _():
-            w1[0].go(2)
-            w1[1].go(1)
-            rest[0].go(2)
-            w2[1].start(0)
-
-        @pl.when(i == 7)
-        def _():
-            w2[0].go(1)
-
+        tick_first(i)
         a_one_ref[i], c_one_ref[i] = first_crop(crop_x(i), gains_ref, wv0, a3)
         return carry
 
     lax.fori_loop(0, count, first, 0)
-    w1[0].arrive(2)
-    rest[1].start(0)
-    w1[1].go(2)
-    w1[1].arrive(2)
+    go(BETWEEN)
+    whole(("w1a", "w1b"))
     keep_w[1].start()
 
     def second(i, carry):
-        @pl.when(i == 0)
-        def _():
-            w2[0].go(2)
-            w2[1].go(1)
-
-        @pl.when(i == 2)
-        def _():
-            w2[1].go(2)
-            rest[0].go(3)
-
-        @pl.when(i == 3)
-        def _():
-            rest[1].go(1)
-
-        @pl.when(i == 5)
-        def _():
-            w2[0].go(3)
-
-        @pl.when(i == 7)
-        def _():
-            w2[1].go(3)
-
+        tick_second(i)
         a_two_ref[i] = second_crop(
             c_one_ref[i], crop_x(i), gains_ref, wv1, l_ref.at[crop_rows(i)], a3, y32
         )
         return carry
 
     lax.fori_loop(0, count, second, 0)
-    rest[1].go(2)
-    w2[0].arrive(3)
-    w2[1].arrive(3)
+    whole(("w2a", "w2b"))
     keep_w[2].start()
     down_dot(l_ref, wv2, s_ref)
-    for part in (w0, w1, w2):
-        for g in part:
-            g.finish()
-    for g in rest:
-        g.arrive(g.steps - 1)
-        g.finish()
+    go(AFTER)
+    whole(("r0", "r1", "r2", "r3"))
+    for job in jobs.values():
+        job.finish()
     for copy in cells:
         if copy.is_remote:
             copy.wait_send()
@@ -766,8 +765,8 @@
             pltpu.VMEM((ch // 128, ranks * cells, 128), F32),
             pltpu.SemaphoreType.DMA((8,)),
             pltpu.SemaphoreType.DMA((8,)),
-            pltpu.SemaphoreType.DMA((8, 8)),
-            pltpu.SemaphoreType.DMA((8, 8)),
+            pltpu.SemaphoreType.DMA((len(PARTS), 8)),
+            pltpu.SemaphoreType.DMA((len(PARTS), 8)),
             pltpu.SemaphoreType.DMA((4,)),
         ],
         compiler_params=pltpu.CompilerParams(
@@ -790,7 +789,8 @@
     l_ref,
     ds_ref,
     loss_ref,
-    rg_ref,
+    dp_ref,
+    small_ref,
     dw_ref,
     tab,
     stage,
@@ -837,7 +837,7 @@
     def pick(b, carry):
         for j in range(8):
             for k in range(4):
-                row = codes_ref[(b * 8 + j) * 4 + k]
+                row = codes_ref[k * cells + b * 8 + j]
                 e_ref[k, pl.ds(b * 8 + j, 1), :] = tab[pl.ds(row, 1), :]
         return carry
 
@@ -877,34 +877,12 @@
     tail = None
     for k in (3, 2, 1, 0):
         tail = resid[k] if tail is None else tail + resid[k]
-        e_ref[k] = tail * (-2.0 / lat_count)
-
-    def clear(p, carry):
-        tab[pl.ds(pl.multiple_of(p * n_code, n_code), n_code), :] = jnp.zeros((n_code, lat), F32)
-        return carry
-
-    lax.fori_loop(0, pieces, clear, 0)
-
-    def scatter(b, carry):
-        for j in range(8):
-            for k in range(4):
-                row = codes_ref[(b * 8 + j) * 4 + k]
-                tab[pl.ds(row, 1), :] += e_ref[k, pl.ds(b * 8 + j, 1), :]
-        return carry
-
-    lax.fori_loop(0, cells // 8, scatter, 0)
-
-    def narrow(p, carry):
-        at = pl.ds(pl.multiple_of(p * n_code, n_code), n_code)
-        rg_ref[p, :n_code] = tab[at, :].astype(BF)
-        return carry
-
-    lax.fori_loop(0, pieces, narrow, 0)
-    rg_ref[:, n_code : n_code + 16] = d_proj.astype(BF).reshape(pieces, 16, lat)
+        dp_ref[k * cells : (k + 1) * cells, :] = (tail * (-2.0 / lat_count)).astype(BF)
+    small_ref[:, :16] = d_proj.astype(BF).reshape(pieces, 16, lat)
     d_head = jnp.concatenate([d_head, jnp.zeros((d_head.shape[0], lat - 128), F32)], axis=1)
     d_head = d_head.reshape(pieces, 8, lat)
     d_head = jnp.concatenate([d_head, jnp.zeros((pieces, 8, lat), F32)], axis=1)
-    rg_ref[:, n_code + 16 :] = d_head.astype(BF)
+    small_ref[:, 16:] = d_head.astype(BF)
     down_weight_grad(l_ref, ds_ref, dw_ref)
 
 
@@ -914,14 +892,15 @@
     outs = [
         jax.ShapeDtypeStruct((cells, ch), BF),
         jax.ShapeDtypeStruct((8, ch), F32),
-        jax.ShapeDtypeStruct((pieces, rows, lat), BF),
+        jax.ShapeDtypeStruct((4 * cells, lat), BF),
+        jax.ShapeDtypeStruct((pieces, 32, lat), BF),
         jax.ShapeDtypeStruct((9 * ch, ch), BF),
     ]
     return pl.pallas_call(
         functools.partial(quantizer_kernel, (lat_count, pix_count, rgb, n_code)),
         out_shape=outs,
         in_specs=[pl.BlockSpec(memory_space=pltpu.SMEM), ANY, VM, VM, VM],
-        out_specs=[VM] * 4,
+        out_specs=[VM] * 5,
         scratch_shapes=[
             pltpu.VMEM((pieces * n_code, lat), F32),
             pltpu.VMEM((4, n_code, lat), BF),
@@ -936,94 +915,266 @@
 
 
 def second_back_kernel(
+    n_code,
     ds_ref,
     w_down_ref,
     w_ref,
     c_ref,
     a_ref,
     gains_ref,
+    codes_ref,
+    dp_ref,
     down_src,
-    rest_src,
+    small_src,
     din_ref,
-    dw_ref,
     dg_ref,
-    g_down_ref,
+    g_down0_ref,
+    g_down1_ref,
+    kept0_ref,
+    kept1_ref,
     rest_kept_ref,
-    dc,
+    dw,
     d3,
     y32,
+    dp_all,
+    codes_all,
+    quarter,
+    quarter_in,
+    small_in,
+    e_send,
+    e_recv,
     *bufs,
 ):
     place = Place()
-    down = Reduce(place, down_src, g_down_ref, *bufs[:8])
-    early, sems = bufs[8:12], bufs[12:]
-    rest = Reduce(place, rest_src.at[..., :128], None, *early, rest_kept_ref, None, *sems)
+    bufs = list(bufs)
+
+    def take(n):
+        out = bufs[:n]
+        del bufs[:n]
+        return out
+
+    half = down_src.shape[-1] // 2
+    view = dw.reshape(4, 2, 2, 2, dw.shape[0] // 32, dw.shape[1])
+    down0 = Reduce(place, down_src.at[..., :half], g_down0_ref, *take(8), turn=False)
+    down1 = Reduce(place, down_src.at[..., half:], g_down1_ref, *take(8), turn=False)
+    early, sems = take(4), take(2)
+    low = Reduce(place, view.at[..., :half], None, *early, kept0_ref, None, *sems)
+    early, sems = take(4), take(2)
+    high = Reduce(place, view.at[..., half:], None, *early, kept1_ref, None, *sems)
+
+    across = place.at(x=1 - place.x)
+    other = place.at(c=1 - place.c)
+    two = pl.ds(2 * place.c, 2)
+    entries = [(dp_ref, dp_all, 0), (codes_ref, codes_all, 1)]
+    out_x = [
+        remote(src, dst.at[place.part], e_send.at[k], e_recv.at[k], across) for src, dst, k in entries
+    ]
+    out_x += [
+        pltpu.make_async_copy(src, dst.at[place.part], e_recv.at[2 + k]) for src, dst, k in entries
+    ]
+    out_c = [
+        remote(dst.at[two], dst.at[two], e_send.at[4 + k], e_recv.at[4 + k], other)
+        for _, dst, k in entries
+    ]
+    small = []
+    for k, (x, c) in enumerate(
+        ((place.x, 1 - place.c), (1 - place.x, place.c), (1 - place.x, 1 - place.c))
+    ):
+        small.append(
+            remote(
+                small_src.at[:, :, c, x],
+                small_in.at[k],
+                e_send.at[6 + k],
+                e_recv.at[6 + k],
+                place.at(x=x, c=c),
+            )
+        )
+    small.append(
+        pltpu.make_async_copy(small_src.at[:, :, place.c, place.x], small_in.at[3], e_recv.at[9])
+    )
+    out_y = [
+        remote(
+            quarter.at[1 - place.y, pl.ds(2 * k, 2)],
+            quarter_in.at[pl.ds(2 * k, 2)],
+            e_send.at[10 + k],
+            e_recv.at[10 + k],
+            place.at(y=1 - place.y),
+        )
+        for k in range(2)
+    ]
+
     place.greet()
-    down.start(0)
-    rest.start(0)
+    down0.start(0)
+    down1.start(0)
+    for copy in out_x + small:
+        copy.start()
+
+    def piece(z, y):
+        base = ((z * 2 + y) * 4 + place.part) * n_code
+        row = lax.broadcasted_iota(jnp.int32, (n_code, dp_ref.shape[0]), 0) + base
+
+        def add(k, total):
+            hot = jnp.where(row == codes_all[k], 1.0, 0.0).astype(BF)
+            return total + jnp.dot(hot, dp_all[k], preferred_element_type=F32)
+
+        total = lax.fori_loop(0, 4, add, jnp.zeros((n_code, dp_ref.shape[1]), F32))
+        quarter[y, z, :n_code] = total.astype(BF)
+        total = small_in[3, z, y].astype(F32)
+        for k in range(3):
+            total = total + small_in[k, z, y].astype(F32)
+        quarter[y, z, n_code:] = total.astype(BF)
+
+    def codebook_grad():
+        def away(z, carry):
+            piece(z, 1 - place.y)
+
+            for k in range(2):
+
+                @pl.when(z == 2 * k + 1)
+                def _():
+                    out_y[k].start()
+
+            return carry
+
+        def here(z, carry):
+            piece(z, place.y)
+
+            @pl.when(z == 0)
+            def _():
+                low.go(2)
+
+            @pl.when(z == 2)
+            def _():
+                high.go(2)
+
+            return carry
+
+        lax.fori_loop(0, 4, away, 0)
+        lax.fori_loop(0, 4, here, 0)
 
     def tick_down(i):
-        @pl.when(i == 4)
+        @pl.when(i == 5)
         def _():
-            down.go(1)
+            down0.go(1)
+
+        @pl.when(i == 6)
+        def _():
+            down1.go(1)
+
+    def tick_low(dx):
+        @pl.when(dx == 2)
+        def _():
+            down0.go(2)
+
+    def tick_high(dx):
+        @pl.when(dx == 1)
+        def _():
+            low.arrive(0)
 
     def tick_crop(i):
         @pl.when(i == 0)
         def _():
-            rest.arrive(0)
+            low.start(1)
+
+        @pl.when(i == 1)
+        def _():
+            high.go(1)
+            for copy in out_x:
+                copy.wait_recv()
+            for copy in out_c:
+                copy.start()
 
         @pl.when(i == 3)
         def _():
-            down.go(2)
-            rest.start(1)
+            down1.go(2)
+            down0.go(3)
+            for copy in out_c:
+                copy.wait_recv()
+            for copy in small:
+                copy.wait_recv()
+            codebook_grad()
+
+        @pl.when(i == 4)
+        def _():
+            down1.go(3)
+            down0.go(4)
 
         @pl.when(i == 6)
         def _():
-            down.go(3)
-
-    down_input_grad(ds_ref, w_down_ref, dc, y32, tick_down)
-    unit_back(dc, lambda i: c_ref[i], gains_ref, w_ref, dg_ref, d3, 2, din_ref, tick_crop)
-    conv_weight_grad(a_ref, d3, dw_ref, 0)
-    rest.go(2)
-    conv_weight_grad(a_ref, d3, dw_ref, 1)
-    down.go(4)
-    rest.arrive(2)
-    down.go(5)
-    down.arrive(5)
-    down.sent(0, 6)
-    rest.sent(0, 3)
-
-
-def second_back_call(ds, w_down, w, c_one, a_two, gains, down_src, rest_src):
+            down0.go(5)
+            down1.go(4)
+
+        @pl.when(i == 7)
+        def _():
+            low.arrive(2)
+            down1.go(5)
+
+    down_input_grad(ds_ref, w_down_ref, din_ref, y32, tick_down)
+    shift_all(din_ref, d3)
+    conv_weight_grad(a_ref, d3, dw, 0, tick_low)
+    low.start(0)
+    conv_weight_grad(a_ref, d3, dw, 1, tick_high)
+    high.start(0)
+    unit_back(lambda i: c_ref[i], gains_ref, w_ref, dg_ref, d3, 2, din_ref, tick_crop)
+    for copy in out_y:
+        copy.wait_recv()
+    for z in range(4):
+        total = quarter[place.y, z].astype(F32) + quarter_in[z].astype(F32)
+        rest_kept_ref[z] = total.astype(BF)
+    high.arrive(2)
+    down0.arrive(5)
+    down1.arrive(5)
+    for job in (down0, down1):
+        job.sent(0, 6)
+    for job in (low, high):
+        job.sent(0, 3)
+    for copy in out_x[:2] + out_c + small[:3] + out_y:
+        copy.wait_send()
+
+
+def second_back_call(n_code, ds, w_down, w, c_one, a_two, gains, codes, dp, down_src, small_src):
     crops, cells, ch = c_one.shape
-    n_conv, n_rest = down_src.shape[-2], rest_src.shape[-2]
+    n_conv, lat = down_src.shape[-2], dp.shape[-1]
+    n_rest = n_code + small_src.shape[-2]
+
+    def shape(*dims, dtype=BF):
+        return jax.ShapeDtypeStruct(dims, dtype)
+
     outs = [
-        jax.ShapeDtypeStruct((crops, cells, ch), BF),
-        jax.ShapeDtypeStruct(w.shape, BF),
-        jax.ShapeDtypeStruct((2, ch), F32),
-        jax.ShapeDtypeStruct((4, n_conv, ch), BF),
-        jax.ShapeDtypeStruct((4, n_rest, 128), BF),
+        shape(crops, cells, ch),
+        shape(2, ch, dtype=F32),
+        shape(4, n_conv, ch // 2),
+        shape(4, n_conv, ch // 2),
+        shape(4, n_conv, ch // 2),
+        shape(4, n_conv, ch // 2),
+        shape(4, n_rest, lat),
     ]
+    whole = Reduce.early(n_conv, ch // 2) + Reduce.late(n_conv, ch // 2, 1) + Reduce.sems()
+    begun = Reduce.early(n_conv, ch // 2) + Reduce.sems()
     return pl.pallas_call(
-        second_back_kernel,
+        functools.partial(second_back_kernel, n_code),
         out_shape=outs,
-        in_specs=[VM] * 6 + [ANY] * 2,
-        out_specs=[VM] * 5,
+        in_specs=[VM] * 8 + [ANY] * 2,
+        out_specs=[VM] * 7,
         scratch_shapes=[
-            pltpu.VMEM((crops, cells, ch), BF),
+            pltpu.VMEM(w.shape, BF),
             pltpu.VMEM((crops, 18, 16, 3 * ch), BF),
             pltpu.VMEM((ch // 128, cells, 128), F32),
+            pltpu.VMEM((4,) + dp.shape, BF),
+            pltpu.VMEM((4,) + codes.shape, jnp.int32),
+            pltpu.VMEM((2, 4, n_rest, lat), BF),
+            pltpu.VMEM((4, n_rest, lat), BF),
+            pltpu.VMEM((4, 4, 2, small_src.shape[-2], lat), BF),
+            pltpu.SemaphoreType.DMA((12,)),
+            pltpu.SemaphoreType.DMA((12,)),
         ]
-        + Reduce.early(n_conv, ch)
-        + Reduce.late(n_conv, ch, 1)
-        + Reduce.sems()
-        + Reduce.early(n_rest, 128)
-        + Reduce.sems(),
+        + whole * 2
+        + begun * 2,
         compiler_params=pltpu.CompilerParams(
-            vmem_limit_bytes=58 * MIB, collective_id=3, has_side_effects=True
+            vmem_limit_bytes=61 * MIB, collective_id=3, has_side_effects=True
         ),
-        cost_estimate=pl.CostEstimate(flops=2 * 10**10, bytes_accessed=0, transcendentals=0),
-    )(ds, w_down, w, c_one, a_two, gains, down_src, rest_src)
+        cost_estimate=pl.CostEstimate(flops=4 * 10**10, bytes_accessed=0, transcendentals=0),
+    )(ds, w_down, w, c_one, a_two, gains, codes, dp, down_src, small_src)
 
 
 def first_back_kernel(
@@ -1033,18 +1184,20 @@
     gains_ref,
     w_ref,
     a_ref,
+    kept0_ref,
+    kept1_ref,
     rest_kept_ref,
-    g_down_ref,
+    g_down0,
+    g_down1,
     dg_two_ref,
     loss_ref,
     wt_ref,
     conv_row_ref,
     rest_row_ref,
-    rest_src,
-    second_src,
     g_first0,
     g_first1,
-    g_second,
+    g_second0,
+    g_second1,
     g_rest0,
     g_rest1,
     conv_new_ref,
@@ -1069,53 +1222,70 @@
         del bufs[:n]
         return out
 
-    half = rest_src.shape[-1] // 2
+    half = rest_kept_ref.shape[-1] // 2
     ch = tv_ref.shape[1]
     view = dw.reshape(4, 2, 2, 2, dw.shape[0] // 32, ch)
-    four, sems = take(1), take(2)
-    rest0 = Reduce(place, None, g_rest0, *[None] * 4, rest_kept_ref, *four, *sems)
-    rest1 = Reduce(place, rest_src.at[..., half:], g_rest1, *take(8))
-    second = Reduce(place, second_src, g_second, *take(8))
+    none = [None] * 4
+    second0 = Reduce(place, None, g_second0, *none, kept0_ref, *take(3))
+    second1 = Reduce(place, None, g_second1, *none, kept1_ref, *take(3))
+    rest0 = Reduce(place, None, g_rest0, *none, rest_kept_ref.at[..., :half], *take(3))
+    rest1 = Reduce(place, None, g_rest1, *none, rest_kept_ref.at[..., half:], *take(3))
     low = Reduce(place, view.at[..., : ch // 2], g_first0, *take(8))
     high = Reduce(place, view.at[..., ch // 2 :], g_first1, *take(8))
+    late = (second0, second1, rest0, rest1)
     place.greet()
-    rest0.start(3)
-    rest1.start(0)
-    second.start(0)
+    for job in late:
+        job.start(3)
+
+    def tick_high(dx):
+        @pl.when(dx == 1)
+        def _():
+            low.go(1)
+
+        @pl.when(dx == 2)
+        def _():
+            second0.go(4)
 
     def tick_crop(i):
+        @pl.when(i == 0)
+        def _():
+            second1.go(4)
+
+        @pl.when(i == 1)
+        def _():
+            high.go(1)
+            second0.go(5)
+
         @pl.when(i == 2)
         def _():
-            rest1.go(1)
-            second.arrive(0)
+            low.go(2)
+
+        @pl.when(i == 3)
+        def _():
+            second1.go(5)
+
+        @pl.when(i == 5)
+        def _():
+            low.go(3)
+            high.go(2)
 
         @pl.when(i == 6)
         def _():
             rest0.go(4)
 
-    def tick_low(dx):
-        @pl.when(dx == 0)
+        @pl.when(i == 7)
         def _():
-            rest1.go(2)
-            second.start(1)
-
-        @pl.when(dx == 1)
-        def _():
-            rest0.go(5)
-
-    def tick_high(dx):
-        @pl.when(dx == 0)
-        def _():
-            rest1.go(3)
-
-        @pl.when(dx == 1)
-        def _():
-            low.go(1)
+            high.go(3)
 
     def v_of(i):
         return x_ref[i].astype(F32)
 
-    unit_back(dc_ref, v_of, gains_ref, w_ref, dg, d3, 0, None, tick_crop)
+    shift_all(dc_ref, d3)
+    conv_weight_grad(a_ref, d3, dw, 0)
+    low.start(0)
+    conv_weight_grad(a_ref, d3, dw, 1, tick_high)
+    high.start(0)
+    unit_back(v_of, gains_ref, w_ref, dg, d3, 0, None, tick_crop)
     vec[...] = jnp.zeros_like(vec)
     vec[0:2] = dg[...]
     vec[2:4] = dg_two_ref[...]
@@ -1126,13 +1296,6 @@
     ]
     for copy in small:
         copy.start()
-    conv_weight_grad(a_ref, d3, dw, 0, tick_low)
-    low.start(0)
-    conv_weight_grad(a_ref, d3, dw, 1, tick_high)
-    high.start(0)
-    second.go(2)
-    high.go(1)
-
     tv_ref[...] = jnp.zeros_like(tv_ref)
     for copy in small:
         copy.wait_recv()
@@ -1178,22 +1341,17 @@
             size = rest_row_ref.shape[1] - n_code - n_proj - n_head
             rest_new_ref[k, rest_row_ref.shape[1] - size :] = jnp.ones((size, 1), F32)
 
-    fold_conv(2, [g_down_ref])
+    rest0.go(5)
+    fold_conv(2, [g_down0, g_down1])
+    second0.arrive(5)
+    second1.arrive(5)
+    fold_conv(1, [g_second0, g_second1])
+    rest1.go(4)
     rest0.arrive(5)
-    rest1.go(4)
-    second.go(3)
-    low.go(2)
-    low.go(3)
-    high.go(2)
     rest1.go(5)
-    high.go(3)
+    low.go(4)
     rest1.arrive(5)
     fold_rest()
-    second.go(4)
-    second.go(5)
-    low.go(4)
-    second.arrive(5)
-    fold_conv(1, [g_second])
     low.go(5)
     high.go(4)
     low.arrive(5)
@@ -1216,40 +1374,30 @@
     tv_ref[...] += tv_in[1] + tv_in[2] + tv_in[3]
     for copy in small:
         copy.wait_send()
-    rest0.sent(3, 6)
-    for job in (rest1, second, low, high):
+    for job in late:
+        job.sent(3, 6)
+    for job in (low, high):
         job.sent(0, 6)
 
 
-def first_back_call(
-    sizes, dc, x, gains, w, a_one, rest_kept, g_down, dg_two, loss, wt, conv_row, rest_row,
-    rest_src, second_src
-):
+def first_back_call(sizes, dc, x, gains, w, a_one, kept, g_down, dg_two, loss, wt, rows):
     crops, cells, ch = x.shape
-    n_conv, n_rest = second_src.shape[-2], rest_src.shape[-2]
+    n_conv, n_rest = g_down[0].shape[-2], kept[2].shape[-2]
 
     def shape(*dims, dtype=BF):
         return jax.ShapeDtypeStruct(dims, dtype)
 
-    outs = [
-        shape(4, n_conv, ch // 2),
-        shape(4, n_conv, ch // 2),
-        shape(4, n_conv, ch),
-        shape(4, n_rest, 128),
-        shape(4, n_rest, 128),
-        shape(*conv_row.shape, dtype=F32),
-        shape(*rest_row.shape, dtype=F32),
-        shape(32, ch, dtype=F32),
-    ]
-
-    def job(rows, lanes):
-        return Reduce.early(rows, lanes) + Reduce.late(rows, lanes, 1) + Reduce.sems()
-
+    conv_half = shape(4, n_conv, ch // 2)
+    rest_half = shape(4, n_rest, 128)
+    outs = [conv_half] * 4 + [rest_half] * 2
+    outs += [shape(*v.shape, dtype=F32) for v in rows] + [shape(32, ch, dtype=F32)]
+    args = [dc, x, gains, w, a_one, *kept, *g_down, dg_two, loss, wt, *rows]
+    whole = Reduce.early(n_conv, ch // 2) + Reduce.late(n_conv, ch // 2, 1) + Reduce.sems()
     return pl.pallas_call(
         functools.partial(first_back_kernel, sizes),
         out_shape=outs,
-        in_specs=[VM] * 12 + [ANY] * 2,
-        out_specs=[VM] * 8,
+        in_specs=[VM] * len(args),
+        out_specs=[VM] * len(outs),
         scratch_shapes=[
             pltpu.VMEM(w.shape, BF),
             pltpu.VMEM((crops, 18, 16, 3 * ch), BF),
@@ -1260,28 +1408,24 @@
             pltpu.SemaphoreType.DMA((7,)),
             pltpu.SemaphoreType.DMA((7,)),
         ]
-        + Reduce.late(n_rest, 128, 0)
-        + Reduce.sems()
-        + job(n_rest, 128)
-        + job(n_conv, ch)
-        + job(n_conv, ch // 2)
-        + job(n_conv, ch // 2),
+        + (Reduce.late(n_conv, ch // 2, 0) + Reduce.sems()) * 2
+        + (Reduce.late(n_rest, 128, 0) + Reduce.sems()) * 2
+        + whole * 2,
         compiler_params=pltpu.CompilerParams(
             vmem_limit_bytes=60 * MIB, collective_id=4, has_side_effects=True
         ),
         cost_estimate=pl.CostEstimate(flops=2 * 10**10, bytes_accessed=0, transcendentals=0),
-    )(
-        dc, x, gains, w, a_one, rest_kept, g_down, dg_two, loss, wt, conv_row, rest_row,
-        rest_src, second_src
-    )
+    )(*args)
 
 
 def finish_kernel(
     sizes,
     g_first0,
     g_first1,
-    g_second,
-    g_down,
+    g_second0,
+    g_second1,
+    g_down0,
+    g_down1,
     g_rest0,
     g_rest1,
     conv_ref,
@@ -1320,7 +1464,7 @@
         return tv_ref[k : k + 1, :]
 
     cg, cc, cn, cl = conv_outs
-    for j, parts in enumerate(((g_first0, g_first1), (g_second,), (g_down,))):
+    for j, parts in enumerate(((g_first0, g_first1), (g_second0, g_second1), (g_down0, g_down1))):
         n = conv_ref.shape[1]
         col_new, q, row_mean = scales(
             conv_col_ref[j : j + 1, :], line(j), line(3 + j), line(6 + j)[:, :1], line(24 + j), n, ch
@@ -1711,9 +1855,9 @@
     side = out[1].reshape(lat_cells, 128)
     w_all, rest = out[2:5], out[5]
     a_one, c_one, a_two, windows, s_low, wt = out[6:]
-    codes = side[:, 32:36].astype(jnp.int32).reshape(-1)
+    codes = jnp.transpose(side[:, 32:36]).astype(jnp.int32).reshape(-1)
     n_rest = rest.shape[-2]
-    d_s, loss, rest_grad, d_down = quantizer_call(
+    d_s, loss, dp, d_small, d_down = quantizer_call(
         codes,
         rest.reshape(-1, n_rest, lat),
         side,
@@ -1728,9 +1872,18 @@
     def shards_of(v):
         return v.reshape(4, 2, 2, 2, -1, v.shape[-1])
 
-    rest_src = shards_of(rest_grad)
-    d_c_one, d_second, dg_two, g_down, rest_kept = second_back_call(
-        d_s, w_all[2], w_all[1], c_one, a_two, gains, shards_of(d_down), rest_src
+    d_c_one, dg_two, g_down0, g_down1, *kept = second_back_call(
+        n_code,
+        d_s,
+        w_all[2],
+        w_all[1],
+        c_one,
+        a_two,
+        gains,
+        codes[None],
+        dp,
+        shards_of(d_down),
+        d_small.reshape(4, 2, 2, 2, -1, lat),
     )
     conv_row4 = jnp.transpose(conv_row).reshape(3, 4, -1, 1)
     rest_row4 = [v.reshape(4, -1) for v in (code_row, proj_row, head_row)]
@@ -1743,21 +1896,18 @@
         gains,
         w_all[0],
         a_one,
-        rest_kept,
-        g_down,
+        kept,
+        (g_down0, g_down1),
         dg_two,
         loss,
         wt,
-        conv_row4,
-        rest_row4,
-        rest_src,
-        shards_of(d_second),
+        (conv_row4, rest_row4),
     )
-    g_first0, g_first1, g_second, g_rest0, g_rest1, conv_rn, rest_rn, tv = out
+    conv_rn, rest_rn, tv = out[6:]
     head_col_wide = jnp.pad(head_col, (0, lat - rgb), constant_values=1.0)
     loss, conv_outs, rest_outs, gain_outs = finish_call(
         sizes + (shards,),
-        (g_first0, g_first1, g_second, g_down, g_rest0, g_rest1),
+        (*out[:4], g_down0, g_down1, *out[4:6]),
         (conv_rows, code_w, proj_w, head_wide),
         (conv_rn, rest_rn),
         tv,

time: 398 us -> 369 us (0.927)
  Pallas kernels: 377 us -> 348 us
    pallas_call x1, Pallas kernels: 108 us -> 84.7 us  [first_back_call(): pl.pallas_call(functools.partial(first_back_kernel, sizes), out_shape=out...]
    pallas_call x1, Pallas kernels: 77.4 us -> 94.1 us  [second_back_call(): pl.pallas_call(functools.partial(second_back_kernel, n_code), out_shape=o...]
    pallas_call x1, Pallas kernels: 37.5 us -> 24 us  [quantizer_call(): pl.pallas_call(functools.partial(quantizer_kernel, (lat_count, pix_count,...]
    pallas_call x1, Pallas kernels: 144 us -> 135 us  [forward_call(): pl.pallas_call(forward_kernel, out_shape=outs, in_specs=[ANY] * 2 + [VM]...]
where the time goes in v3:
time: 369 us
  Pallas kernels  348 us (94%)
  local copies, waits for them, and re-layouts  15.5 us (4%)
  other arithmetic  4.5 us (1%)
    pallas_call x1, Pallas kernels, forward_call(): pl.pallas_call(forward_kernel, out_shape=outs, in_specs=[ANY] * 2 + [VM]...  135 us
    pallas_call x1, Pallas kernels, second_back_call(): pl.pallas_call(functools.partial(second_back_kernel, n_code), out_shape=o...  94.1 us
    pallas_call x1, Pallas kernels, first_back_call(): pl.pallas_call(functools.partial(first_back_kernel, sizes), out_shape=out...  84.7 us
    pallas_call x1, Pallas kernels, quantizer_call(): pl.pallas_call(functools.partial(quantizer_kernel, (lat_count, pix_count,...  24 us
    pallas_call x1, Pallas kernels, finish_call(): pl.pallas_call(functools.partial(finish_kernel, sizes), out_shape=outs, i...  10.2 us

profile of v3, /device:TPU:0, one launch (start us, length us, event | category | flops | bytes accessed | tf_op | source)
XLA Modules:
  0.0 368.5 jit_solution(11037846119153073206)
XLA Ops:
  0.7 0.8 copy.53
  1.4 0.6 pad.22.head_ref
  2.1 0.8 convert_element_type.19
  2.8 0.8 convert_element_type.20
  3.6 0.9 fusion
  4.5 0.2 copy.61
  4.8 0.7 pad.21.clone
  5.5 134.7 %shard_map.361 = (bf16[8,4,64,512]{3,2,1,0:T(8,128)(2,1)}, f32[8,4,16,128]{3,2,1,0:T(8,128)}, bf16[4608,512]{1,0:T(8,128)(2,1)}, bf16[4608,512]{1,0:T(8,128)(2,1...) custom-call(bf16[4,8,64,512]{3,2,1,0:T(8,128)(2,1)} %bitcast.52, ...), custom_call_target="tpu_custom_call" | custom-call | flops 24159191040 | tf_op jit(solution)/shard_map/pallas_call | solution.py:752
  140.2 1.1 fusion.2
  141.3 0.1 copy.54
  141.4 0.6 copy.62
  142.0 24.0 %shard_map.362 = (bf16[512,512]{1,0:T(8,128)(2,1)}, f32[8,512]{1,0:T(8,128)}, bf16[2048,256]{1,0:T(8,128)(2,1)}, bf16[32,32,256]{2,1,0:T(8,128)(2,1)}, bf16[4608,512]{1,0:T(8,128)(2,1)}) custom-call(s32[2048]{0:T(1024)} %bitcast.46, bf16[32,544,256]{2,1,0:T(8,128)(2,1)} %bitcast.56, f32[512,128]{1,0:T(8,128)} %bitcast.39, ...), custom_call_target="tpu_custom_call" | custom-call | flops 10000000000 | bytes 10000000 | tf_op jit(solution)/shard_map/pallas_call | solution.py:899
  166.0 0.6 copy.63
  166.6 0.0 copy-start.3
  166.6 0.0 copy-start.4
  166.6 0.0 copy-start.5
  166.6 94.1 %shard_map.363 = (bf16[8,256,512]{2,1,0:T(8,128)(2,1)}, f32[2,512]{1,0:T(2,128)}, bf16[4,144,256]{2,1,0:T(8,128)(2,1)}, bf16[4,144,256]{2,1,0:T(8,128)(2,1)}, bf...) custom-call(bf16[512,512]{1,0:T(8,128)(2,1)} %get-tuple-element.81.ds_ref, ...), custom_call_target="tpu_custom_call" | custom-call | flops 40000000000 | tf_op jit(solution)/shard_map/pallas_call | solution.py:1154
  260.8 0.0 copy-done.3
  260.8 0.1 pad.27.clone
  260.9 0.0 copy-done.4
  260.9 0.1 reshape.110
  261.0 0.0 copy-done.5
  261.0 0.1 reshape.111
  261.1 0.1 maximum_bitcast_fusion
  261.1 1.4 copy.57.rest_row_ref
  262.5 0.0 copy-done.2
  262.5 1.7 reshape.116.conv_row_ref
  264.2 0.0 copy-start.6
  264.2 84.7 %shard_map.364 = (bf16[4,144,256]{2,1,0:T(8,128)(2,1)}, bf16[4,144,256]{2,1,0:T(8,128)(2,1)}, bf16[4,144,256]{2,1,0:T(8,128)(2,1)}, bf16[4,144,256]{2,1,0:T(8,12...) custom-call(bf16[8,256,512]{2,1,0:T(8,128)(2,1)} %get-tuple-element., ...), custom_call_target="tpu_custom_call" | custom-call | flops 20000000000 | tf_op jit(solution)/shard_map/pallas_call | solution.py:1396
  348.9 0.0 copy-done.6
  348.9 0.6 pad.23
  349.4 10.2 %shard_map.365 = (f32[1,1]{1,0:T(1,128)}, f32[3,576,512]{2,1,0:T(8,128)}, f32[3,512]{1,0:T(4,128)}, f32[3,576,512]{2,1,0:T(8,128)}, bf16[3,576,512]{2,1,0:T(8,12...) custom-call(bf16[4,144,256]{2,1,0:T(8,128)(2,1)} %get-tuple-element., ...), custom_call_target="tpu_custom_call" | custom-call | flops 10000000 | bytes 20000000 | tf_op jit(solution)/shard_map/pallas_call | solution.py:1544
  359.7 0.7 slice.16
  360.4 0.7 copy.58
  361.1 0.7 slice.18
  361.8 0.7 copy.59
  362.5 0.7 slice.19
  363.2 0.7 copy.60
  363.9 1.2 slice_bitcast_fusion.1
  365.0 0.0 copy-done
  365.0 0.4 reduce.1
  365.5 0.6 copy.64
  366.1 0.0 copy-done.1
  366.1 0.5 reduce
  366.6 0.7 reshape.112
  367.3 0.6 reshape.113
  367.9 0.1 split.14
  367.9 0.6 reshape.115
  (10 shorter events, 0.0 us)
Async XLA Ops:
  166.6 94.2 %copy-start.3 = (f32[2048]{0:T(1024)S(1)}, f32[2048]{0:T(1024)}, u32[]{:S(2)}) copy-start(f32[2048]{0:T(1024)} %param.31) | copy-start | bytes 24580
  166.6 94.3 %copy-start.4 = (f32[64]{0:T(128)S(1)}, f32[64]{0:T(128)}, u32[]{:S(2)}) copy-start(f32[64]{0:T(128)} %param.29) | copy-start | bytes 772
  166.6 94.3 %copy-start.5 = (f32[32]{0:T(128)S(1)}, f32[32]{0:T(128)}, u32[]{:S(2)}) copy-start(f32[32]{0:T(128)} %param.33) | copy-start | bytes 388
  166.6 95.9 %copy-start.2 = (f32[576,3]{0,1:T(4,128)S(1)}, f32[576,3]{0,1:T(4,128)}, u32[]{:S(2)}) copy-start(f32[576,3]{0,1:T(4,128)} %param.27) | copy-start | bytes 20740
  264.2 84.7 %copy-start.6 = (f32[12]{0:T(128)S(1)}, f32[12]{0:T(128)}, u32[]{:S(2)}) copy-start(f32[12]{0:T(128)} %param.34) | copy-start | bytes 148
  349.4 15.6 %copy-start = (f32[4,544,1]{2,1,0:T(8,128)S(1)}, f32[4,544,1]{2,1,0:T(8,128)}, u32[]{:S(2)}) copy-start(f32[4,544,1]{2,1,0:T(8,128)} %get-tuple-element.108.rest_row_ref) | copy-start | bytes 26116
  349.4 16.6 %copy-start.1 = (f32[3,4,144,1]{3,2,1,0:T(8,128)S(1)}, f32[3,4,144,1]{3,2,1,0:T(8,128)}, u32[]{:S(2)}) copy-start(f32[3,4,144,1]{3,2,1,0:T(8,128)} %get-tuple-element.107.conv_row_ref) | copy-start | bytes 20740

commit v4 on v3

--- a/solution.py
+++ b/solution.py
@@ -538,23 +538,64 @@
                     copy.wait_send()
 
 
-PARTS = (
-    ("w0b", "yx", 1, None),
-    ("w1a", "yx", 0, None),
-    ("w0a", "y", 0, None),
-    ("w1b", "yx", 1, None),
-    ("w2b", "yx", 1, None),
-    ("r0", "y", 0, 0),
-    ("r2", "yx", 0, 1),
-    ("r1", "yx", 1, 0),
-    ("w2a", "y", 0, None),
-    ("r3", "y", 1, 1),
-)
-BEFORE = ("w0b1", "w1a1", "w0b2", "w1a2", "w0a1", "w1b1", "w0b3", "w2b1", "w0a2")
-FIRST = {1: ("w1a3", "w1b2"), 2: ("r01",), 4: ("w2b2", "r21"), 7: ("r11", "w1b3")}
-BETWEEN = ("r02",)
-SECOND = {1: ("r22",), 2: ("w2a1",), 3: ("w2b3", "r12"), 6: ("r31", "r23"), 7: ("w2a2",)}
-AFTER = ("r13", "r32")
+class ReduceZ(Reduce):
+    def copies(self, step):
+        p, send, recv = self.p, self.send, self.recv
+        if step == 1:
+            out = []
+            for d, peer in zip((1, 2, 3), p.z_peers()):
+                part = self.mine.at[:, (p.z + d) % 4]
+                out.append(remote(part, self.four.at[d - 1], send.at[5 + d], recv.at[5 + d], peer))
+            return out
+        if step == 2:
+            part = self.kept.at[pl.ds(2 * (1 - self.f), 2)]
+            return [remote(part, self.two, send.at[4], recv.at[4], self.f_peer)]
+        if step == 3:
+            part = self.pair.at[1 - self.g]
+            return [remote(part, self.three, send.at[5], recv.at[5], self.g_peer)]
+        return super().copies(step)
+
+    def arrive(self, step):
+        if step not in (1, 2, 3):
+            super().arrive(step)
+            return
+        for copy in self.copies(step):
+            copy.wait_recv()
+        if step == 1:
+
+            def body(i, carry):
+                total = self.mine[i, self.p.z].astype(F32)
+                for d in range(3):
+                    total = total + self.four[d, i].astype(F32)
+                self.kept[i] = total.astype(BF)
+                return carry
+
+            lax.fori_loop(0, 4, body, 0)
+        if step == 2:
+            for copy in self.copies(step):
+                copy.wait_send()
+            for k in range(2):
+                at = 2 * self.f + k
+                self.pair[k] = (self.kept[at].astype(F32) + self.two[k].astype(F32)).astype(BF)
+        if step == 3:
+            total = self.pair[self.g].astype(F32) + self.three[...].astype(F32)
+            self.out[self.p.part] = total.astype(BF)
+
+    def sent(self, first, last):
+        for step in range(first, last):
+            if step == 2:
+                continue
+            for copy in self.copies(step):
+                if copy.is_remote:
+                    copy.wait_send()
+
+
+PARTS = (('w0b', 'yx', 1, None), ('w0a', 'yx', 0, None), ('r1', 'yx', 1, 0), ('w1b', 'yx', 1, None), ('w2b', 'yx', 1, None), ('w2a', 'yx', 0, None), ('w1a', 'y', 0, None), ('r3', 'y', 1, 1), ('r0', 'y', 0, 0), ('r2', 'y', 0, 1))
+BEFORE = ('w0b1', 'w0a1', 'w0b2', 'r11', 'w0a2', 'w1b1', 'r12', 'w2b1', 'w0b3', 'w1b2', 'w2a1', 'w2b2', 'w0a3', 'w2a2', 'w1a1')
+FIRST = {3: ('r13',), 4: ('r31',), 6: ('w1a2',), 7: ('w1b3',)}
+BETWEEN = ('r01',)
+SECOND = {1: ('r32',), 3: ('w2b3', 'r21'), 5: ('r02',), 6: ('w2a3',)}
+AFTER = ('r22',)
 
 
 def forward_kernel(
@@ -571,12 +612,17 @@
     w_out1,
     w_out2,
     rest_out,
+    a_one_out,
+    c_one_out,
+    a_two_out,
+    l_out,
+    s_ref,
+    wt_ref,
     a_one_ref,
     c_one_ref,
     a_two_ref,
     l_ref,
-    s_ref,
-    wt_ref,
+    k_sem,
     w_mine,
     rest_mine,
     xv,
@@ -630,9 +676,10 @@
         rest = name[0] == "r"
         src = rest_mine if rest else w_mine.at[int(name[1])]
         dst = views[3] if rest else views[int(name[1])]
-        n, m = src.shape[-2], src.shape[-1] // 2
-        rows = pl.ds(0, n) if row is None else pl.ds(row * n // 2, n // 2)
-        at = (..., rows, pl.ds(lane * m, m))
+        n = src.shape[-2]
+        parts, which = (2, lane) if row is None else (4, 2 * row + lane)
+        cut = [k * n // (16 * parts) * 16 for k in range(parts)] + [n]
+        at = (..., pl.ds(cut[which], cut[which + 1] - cut[which]), slice(None))
         jobs[name] = Gather(place, src.at[at], dst.at[at], g_send.at[k], g_recv.at[k], route)
 
     def go(words):
@@ -662,15 +709,16 @@
             )
         cells.append(pltpu.make_async_copy(src.at[rank], dst.at[:, rank], x_recv.at[base + 3]))
 
-    jobs["w0b"].start(0)
+    started = PARTS[0][0]
+    jobs[started].start(0)
     for copy in cells:
         copy.start()
-    cast_conv(1)
-    for name in ("w1a", "w0a", "w1b"):
-        jobs[name].start(0)
-    cast_conv(2)
-    cast_rest()
-    for name, *_ in PARTS[4:]:
+    cast = {"0"}
+    for name, *_ in PARTS[1:]:
+        which = name[1] if name[0] == "w" else "rest"
+        if which not in cast:
+            cast_rest() if which == "rest" else cast_conv(int(which))
+            cast.add(which)
         jobs[name].start(0)
     go(BEFORE)
     zero_edges(a3)
@@ -691,9 +739,24 @@
 
     tick_first, tick_second = ticks(FIRST), ticks(SECOND)
 
+    def keep_first(i):
+        return [
+            pltpu.make_async_copy(v.at[i], o.at[i], k_sem.at[k, i])
+            for k, (v, o) in enumerate(((a_one_ref, a_one_out), (c_one_ref, c_one_out)))
+        ]
+
+    def keep_second(i):
+        rows = crop_rows(i)
+        return [
+            pltpu.make_async_copy(a_two_ref.at[i], a_two_out.at[i], k_sem.at[2, i]),
+            pltpu.make_async_copy(l_ref.at[rows], l_out.at[rows], k_sem.at[3, i]),
+        ]
+
     def first(i, carry):
         tick_first(i)
         a_one_ref[i], c_one_ref[i] = first_crop(crop_x(i), gains_ref, wv0, a3)
+        for copy in keep_first(i):
+            copy.start()
         return carry
 
     lax.fori_loop(0, count, first, 0)
@@ -706,6 +769,8 @@
         a_two_ref[i] = second_crop(
             c_one_ref[i], crop_x(i), gains_ref, wv1, l_ref.at[crop_rows(i)], a3, y32
         )
+        for copy in keep_second(i):
+            copy.start()
         return carry
 
     lax.fori_loop(0, count, second, 0)
@@ -722,6 +787,13 @@
     keep_x.wait()
     for copy in keep_w:
         copy.wait()
+
+    def kept(i, carry):
+        for copy in keep_first(i) + keep_second(i):
+            copy.wait()
+        return carry
+
+    lax.fori_loop(0, count, kept, 0)
 
 
 def forward_call(feat, side, conv_w, code_w, proj_w, head_w, gains):
@@ -753,8 +825,13 @@
         forward_kernel,
         out_shape=outs,
         in_specs=[ANY] * 2 + [VM] * 5,
-        out_specs=[ANY] * 6 + [VM] * 6,
+        out_specs=[ANY] * 10 + [VM] * 2,
         scratch_shapes=[
+            pltpu.VMEM((crops, ranks * cells, ch), BF),
+            pltpu.VMEM((crops, ranks * cells, ch), F32),
+            pltpu.VMEM((crops, ranks * cells, ch), BF),
+            pltpu.VMEM((lat_cells, 9 * ch), BF),
+            pltpu.SemaphoreType.DMA((4, crops)),
             pltpu.VMEM((3, 2, 2, n_conv, ch), BF),
             pltpu.VMEM((2, 2, n_rest, lat), BF),
             pltpu.VMEM((crops, ranks, cells, ch), BF),
@@ -917,22 +994,26 @@
 def second_back_kernel(
     n_code,
     ds_ref,
+    gains_ref,
+    codes_ref,
+    dp_ref,
+    w_down_in,
+    w_in,
+    c_in,
+    a_in,
+    down_src,
+    small_src,
+    din_ref,
+    dg_ref,
+    down_kept_ref,
+    kept0_ref,
+    kept1_ref,
+    rest_kept_ref,
     w_down_ref,
     w_ref,
     c_ref,
     a_ref,
-    gains_ref,
-    codes_ref,
-    dp_ref,
-    down_src,
-    small_src,
-    din_ref,
-    dg_ref,
-    g_down0_ref,
-    g_down1_ref,
-    kept0_ref,
-    kept1_ref,
-    rest_kept_ref,
+    l_sem,
     dw,
     d3,
     y32,
@@ -953,10 +1034,18 @@
         del bufs[:n]
         return out
 
+    loads = [
+        pltpu.make_async_copy(src, dst, l_sem.at[k])
+        for k, (src, dst) in enumerate(
+            ((w_down_in, w_down_ref), (a_in, a_ref), (w_in, w_ref), (c_in, c_ref))
+        )
+    ]
+    for copy in loads:
+        copy.start()
     half = down_src.shape[-1] // 2
     view = dw.reshape(4, 2, 2, 2, dw.shape[0] // 32, dw.shape[1])
-    down0 = Reduce(place, down_src.at[..., :half], g_down0_ref, *take(8), turn=False)
-    down1 = Reduce(place, down_src.at[..., half:], g_down1_ref, *take(8), turn=False)
+    mine, one, four, send, recv = take(5)
+    down = ReduceZ(place, down_src, None, mine, one, None, None, down_kept_ref, four, send, recv)
     early, sems = take(4), take(2)
     low = Reduce(place, view.at[..., :half], None, *early, kept0_ref, None, *sems)
     early, sems = take(4), take(2)
@@ -1004,8 +1093,7 @@
     ]
 
     place.greet()
-    down0.start(0)
-    down1.start(0)
+    down.start(0)
     for copy in out_x + small:
         copy.start()
 
@@ -1053,29 +1141,16 @@
         lax.fori_loop(0, 4, here, 0)
 
     def tick_down(i):
-        @pl.when(i == 5)
+        @pl.when(i == 4)
         def _():
-            down0.go(1)
-
-        @pl.when(i == 6)
-        def _():
-            down1.go(1)
-
-    def tick_low(dx):
+            down.go(1)
+
+    def tick_high(dx):
         @pl.when(dx == 2)
         def _():
-            down0.go(2)
-
-    def tick_high(dx):
-        @pl.when(dx == 1)
-        def _():
-            low.arrive(0)
+            low.go(1)
 
     def tick_crop(i):
-        @pl.when(i == 0)
-        def _():
-            low.start(1)
-
         @pl.when(i == 1)
         def _():
             high.go(1)
@@ -1086,35 +1161,27 @@
 
         @pl.when(i == 3)
         def _():
-            down1.go(2)
-            down0.go(3)
             for copy in out_c:
                 copy.wait_recv()
             for copy in small:
                 copy.wait_recv()
             codebook_grad()
 
-        @pl.when(i == 4)
-        def _():
-            down1.go(3)
-            down0.go(4)
-
-        @pl.when(i == 6)
-        def _():
-            down0.go(5)
-            down1.go(4)
-
         @pl.when(i == 7)
         def _():
             low.arrive(2)
-            down1.go(5)
-
+            down.arrive(1)
+
+    loads[0].wait()
     down_input_grad(ds_ref, w_down_ref, din_ref, y32, tick_down)
     shift_all(din_ref, d3)
-    conv_weight_grad(a_ref, d3, dw, 0, tick_low)
+    loads[1].wait()
+    conv_weight_grad(a_ref, d3, dw, 0)
     low.start(0)
     conv_weight_grad(a_ref, d3, dw, 1, tick_high)
     high.start(0)
+    loads[2].wait()
+    loads[3].wait()
     unit_back(lambda i: c_ref[i], gains_ref, w_ref, dg_ref, d3, 2, din_ref, tick_crop)
     for copy in out_y:
         copy.wait_recv()
@@ -1122,10 +1189,7 @@
         total = quarter[place.y, z].astype(F32) + quarter_in[z].astype(F32)
         rest_kept_ref[z] = total.astype(BF)
     high.arrive(2)
-    down0.arrive(5)
-    down1.arrive(5)
-    for job in (down0, down1):
-        job.sent(0, 6)
+    down.sent(0, 2)
     for job in (low, high):
         job.sent(0, 3)
     for copy in out_x[:2] + out_c + small[:3] + out_y:
@@ -1143,20 +1207,23 @@
     outs = [
         shape(crops, cells, ch),
         shape(2, ch, dtype=F32),
-        shape(4, n_conv, ch // 2),
-        shape(4, n_conv, ch // 2),
+        shape(4, n_conv, ch),
         shape(4, n_conv, ch // 2),
         shape(4, n_conv, ch // 2),
         shape(4, n_rest, lat),
     ]
-    whole = Reduce.early(n_conv, ch // 2) + Reduce.late(n_conv, ch // 2, 1) + Reduce.sems()
     begun = Reduce.early(n_conv, ch // 2) + Reduce.sems()
     return pl.pallas_call(
         functools.partial(second_back_kernel, n_code),
         out_shape=outs,
-        in_specs=[VM] * 8 + [ANY] * 2,
-        out_specs=[VM] * 7,
+        in_specs=[VM] * 4 + [ANY] * 6,
+        out_specs=[VM] * 6,
         scratch_shapes=[
+            pltpu.VMEM(w_down.shape, BF),
+            pltpu.VMEM(w.shape, BF),
+            pltpu.VMEM(c_one.shape, F32),
+            pltpu.VMEM(a_two.shape, BF),
+            pltpu.SemaphoreType.DMA((4,)),
             pltpu.VMEM(w.shape, BF),
             pltpu.VMEM((crops, 18, 16, 3 * ch), BF),
             pltpu.VMEM((ch // 128, cells, 128), F32),
@@ -1168,27 +1235,27 @@
             pltpu.SemaphoreType.DMA((12,)),
             pltpu.SemaphoreType.DMA((12,)),
         ]
-        + whole * 2
+        + [pltpu.VMEM((k, 4, n_conv, ch), BF) for k in (4, 4, 3)]
+        + Reduce.sems()
         + begun * 2,
         compiler_params=pltpu.CompilerParams(
             vmem_limit_bytes=61 * MIB, collective_id=3, has_side_effects=True
         ),
         cost_estimate=pl.CostEstimate(flops=4 * 10**10, bytes_accessed=0, transcendentals=0),
-    )(ds, w_down, w, c_one, a_two, gains, codes, dp, down_src, small_src)
+    )(ds, gains, codes, dp, w_down, w, c_one, a_two, down_src, small_src)
 
 
 def first_back_kernel(
     sizes,
-    dc_ref,
-    x_ref,
+    dc_in,
+    x_in,
+    w_in,
+    a_in,
     gains_ref,
-    w_ref,
-    a_ref,
     kept0_ref,
     kept1_ref,
     rest_kept_ref,
-    g_down0,
-    g_down1,
+    down_kept_ref,
     dg_two_ref,
     loss_ref,
     wt_ref,
@@ -1198,11 +1265,17 @@
     g_first1,
     g_second0,
     g_second1,
+    g_down,
     g_rest0,
     g_rest1,
     conv_new_ref,
     rest_new_ref,
     tv_ref,
+    dc_ref,
+    x_ref,
+    w_ref,
+    a_ref,
+    l_sem,
     dw,
     d3,
     dg,
@@ -1222,6 +1295,14 @@
         del bufs[:n]
         return out
 
+    loads = [
+        pltpu.make_async_copy(src, dst, l_sem.at[k])
+        for k, (src, dst) in enumerate(
+            ((dc_in, dc_ref), (a_in, a_ref), (w_in, w_ref), (x_in, x_ref))
+        )
+    ]
+    for copy in loads:
+        copy.start()
     half = rest_kept_ref.shape[-1] // 2
     ch = tv_ref.shape[1]
     view = dw.reshape(4, 2, 2, 2, dw.shape[0] // 32, ch)
@@ -1233,9 +1314,18 @@
     low = Reduce(place, view.at[..., : ch // 2], g_first0, *take(8))
     high = Reduce(place, view.at[..., ch // 2 :], g_first1, *take(8))
     late = (second0, second1, rest0, rest1)
+    two, three, pair, send, recv = take(5)
+    down = ReduceZ(place, None, g_down, None, None, two, three, down_kept_ref, None, send, recv)
+    down.pair = pair
     place.greet()
     for job in late:
         job.start(3)
+    down.start(2)
+
+    def tick_low(dx):
+        @pl.when(dx == 2)
+        def _():
+            down.go(4)
 
     def tick_high(dx):
         @pl.when(dx == 1)
@@ -1245,6 +1335,7 @@
         @pl.when(dx == 2)
         def _():
             second0.go(4)
+            down.go(5)
 
     def tick_crop(i):
         @pl.when(i == 0)
@@ -1280,11 +1371,16 @@
     def v_of(i):
         return x_ref[i].astype(F32)
 
+    loads[0].wait()
     shift_all(dc_ref, d3)
-    conv_weight_grad(a_ref, d3, dw, 0)
+    loads[1].wait()
+    down.go(3)
+    conv_weight_grad(a_ref, d3, dw, 0, tick_low)
     low.start(0)
     conv_weight_grad(a_ref, d3, dw, 1, tick_high)
     high.start(0)
+    loads[2].wait()
+    loads[3].wait()
     unit_back(v_of, gains_ref, w_ref, dg, d3, 0, None, tick_crop)
     vec[...] = jnp.zeros_like(vec)
     vec[0:2] = dg[...]
@@ -1342,7 +1438,8 @@
             rest_new_ref[k, rest_row_ref.shape[1] - size :] = jnp.ones((size, 1), F32)
 
     rest0.go(5)
-    fold_conv(2, [g_down0, g_down1])
+    down.arrive(5)
+    fold_conv(2, [g_down])
     second0.arrive(5)
     second1.arrive(5)
     fold_conv(1, [g_second0, g_second1])
@@ -1374,31 +1471,37 @@
     tv_ref[...] += tv_in[1] + tv_in[2] + tv_in[3]
     for copy in small:
         copy.wait_send()
+    down.sent(2, 6)
     for job in late:
         job.sent(3, 6)
     for job in (low, high):
         job.sent(0, 6)
 
 
-def first_back_call(sizes, dc, x, gains, w, a_one, kept, g_down, dg_two, loss, wt, rows):
+def first_back_call(sizes, dc, x, gains, w, a_one, kept, down_kept, dg_two, loss, wt, rows):
     crops, cells, ch = x.shape
-    n_conv, n_rest = g_down[0].shape[-2], kept[2].shape[-2]
+    n_conv, n_rest = down_kept.shape[-2], kept[2].shape[-2]
 
     def shape(*dims, dtype=BF):
         return jax.ShapeDtypeStruct(dims, dtype)
 
     conv_half = shape(4, n_conv, ch // 2)
     rest_half = shape(4, n_rest, 128)
-    outs = [conv_half] * 4 + [rest_half] * 2
+    outs = [conv_half] * 4 + [shape(4, n_conv, ch)] + [rest_half] * 2
     outs += [shape(*v.shape, dtype=F32) for v in rows] + [shape(32, ch, dtype=F32)]
-    args = [dc, x, gains, w, a_one, *kept, *g_down, dg_two, loss, wt, *rows]
+    args = [dc, x, w, a_one, gains, *kept, down_kept, dg_two, loss, wt, *rows]
     whole = Reduce.early(n_conv, ch // 2) + Reduce.late(n_conv, ch // 2, 1) + Reduce.sems()
     return pl.pallas_call(
         functools.partial(first_back_kernel, sizes),
         out_shape=outs,
-        in_specs=[VM] * len(args),
+        in_specs=[ANY] * 4 + [VM] * (len(args) - 4),
         out_specs=[VM] * len(outs),
         scratch_shapes=[
+            pltpu.VMEM(dc.shape, BF),
+            pltpu.VMEM(x.shape, BF),
+            pltpu.VMEM(w.shape, BF),
+            pltpu.VMEM(a_one.shape, BF),
+            pltpu.SemaphoreType.DMA((4,)),
             pltpu.VMEM(w.shape, BF),
             pltpu.VMEM((crops, 18, 16, 3 * ch), BF),
             pltpu.VMEM((2, ch), F32),
@@ -1410,7 +1513,13 @@
         ]
         + (Reduce.late(n_conv, ch // 2, 0) + Reduce.sems()) * 2
         + (Reduce.late(n_rest, 128, 0) + Reduce.sems()) * 2
-        + whole * 2,
+        + whole * 2
+        + [
+            pltpu.VMEM((2, n_conv, ch), BF),
+            pltpu.VMEM((n_conv, ch), BF),
+            pltpu.VMEM((2, n_conv, ch), BF),
+        ]
+        + Reduce.sems(),
         compiler_params=pltpu.CompilerParams(
             vmem_limit_bytes=60 * MIB, collective_id=4, has_side_effects=True
         ),
@@ -1424,8 +1533,7 @@
     g_first1,
     g_second0,
     g_second1,
-    g_down0,
-    g_down1,
+    g_down,
     g_rest0,
     g_rest1,
     conv_ref,
@@ -1464,7 +1572,7 @@
         return tv_ref[k : k + 1, :]
 
     cg, cc, cn, cl = conv_outs
-    for j, parts in enumerate(((g_first0, g_first1), (g_second0, g_second1), (g_down0, g_down1))):
+    for j, parts in enumerate(((g_first0, g_first1), (g_second0, g_second1), (g_down,))):
         n = conv_ref.shape[1]
         col_new, q, row_mean = scales(
             conv_col_ref[j : j + 1, :], line(j), line(3 + j), line(6 + j)[:, :1], line(24 + j), n, ch
@@ -1872,7 +1980,7 @@
     def shards_of(v):
         return v.reshape(4, 2, 2, 2, -1, v.shape[-1])
 
-    d_c_one, dg_two, g_down0, g_down1, *kept = second_back_call(
+    d_c_one, dg_two, down_kept, *kept = second_back_call(
         n_code,
         d_s,
         w_all[2],
@@ -1897,17 +2005,17 @@
         w_all[0],
         a_one,
         kept,
-        (g_down0, g_down1),
+        down_kept,
         dg_two,
         loss,
         wt,
         (conv_row4, rest_row4),
     )
-    conv_rn, rest_rn, tv = out[6:]
+    conv_rn, rest_rn, tv = out[7:]
     head_col_wide = jnp.pad(head_col, (0, lat - rgb), constant_values=1.0)
     loss, conv_outs, rest_outs, gain_outs = finish_call(
         sizes + (shards,),
-        (*out[:4], g_down0, g_down1, *out[4:6]),
+        out[:7],
         (conv_rows, code_w, proj_w, head_wide),
         (conv_rn, rest_rn),
         tv,

time: 369 us -> 346 us (0.938)
  Pallas kernels: 348 us -> 324 us
    pallas_call x1, Pallas kernels: 94.1 us -> 80.3 us  [second_back_call(): pl.pallas_call(functools.partial(second_back_kernel, n_code), out_shape=o...]
    pallas_call x1, Pallas kernels: 135 us -> 128 us  [forward_call(): pl.pallas_call(forward_kernel, out_shape=outs, in_specs=[ANY] * 2 + [VM]...]
where the time goes in v4:
time: 346 us; the launch traced here: 345 us
  Pallas kernels  324 us (94%)
  local copies, waits for them, and re-layouts  15.5 us (4%)
  other arithmetic  4.5 us (1%)
    pallas_call x1, Pallas kernels, forward_call(): pl.pallas_call(forward_kernel, out_shape=outs, in_specs=[ANY] * 2 + [VM]...  128 us
    pallas_call x1, Pallas kernels, first_back_call(): pl.pallas_call(functools.partial(first_back_kernel, sizes), out_shape=out...  81.8 us
    pallas_call x1, Pallas kernels, second_back_call(): pl.pallas_call(functools.partial(second_back_kernel, n_code), out_shape=o...  80.3 us
    pallas_call x1, Pallas kernels, quantizer_call(): pl.pallas_call(functools.partial(quantizer_kernel, (lat_count, pix_count,...  24 us
    pallas_call x1, Pallas kernels, finish_call(): pl.pallas_call(functools.partial(finish_kernel, sizes), out_shape=outs, i...  10.3 us

profile of v4, /device:TPU:0, one launch (start us, length us, event | category | flops | bytes accessed | tf_op | source)
XLA Modules:
  0.0 345.0 jit_solution(13968113050599664697)
XLA Ops:
  0.7 0.8 copy.53
  1.4 0.6 pad.22.head_ref
  2.1 0.8 convert_element_type.19
  2.8 0.8 convert_element_type.20
  3.6 0.9 fusion
  4.5 0.2 copy.61
  4.8 0.7 pad.21.clone
  5.5 127.8 %shard_map.361 = (bf16[8,4,64,512]{3,2,1,0:T(8,128)(2,1)}, f32[8,4,16,128]{3,2,1,0:T(8,128)}, bf16[4608,512]{1,0:T(8,128)(2,1)}, bf16[4608,512]{1,0:T(8,128)(2,1...) custom-call(bf16[4,8,64,512]{3,2,1,0:T(8,128)(2,1)} %bitcast.52, ...), custom_call_target="tpu_custom_call" | custom-call | flops 24159191040 | tf_op jit(solution)/shard_map/pallas_call | solution.py:824
  133.3 1.1 fusion.2
  134.4 0.1 copy.54
  134.5 0.6 copy.62
  135.1 24.0 %shard_map.362 = (bf16[512,512]{1,0:T(8,128)(2,1)}, f32[8,512]{1,0:T(8,128)}, bf16[2048,256]{1,0:T(8,128)(2,1)}, bf16[32,32,256]{2,1,0:T(8,128)(2,1)}, bf16[4608,512]{1,0:T(8,128)(2,1)}) custom-call(s32[2048]{0:T(1024)} %bitcast.46, bf16[32,544,256]{2,1,0:T(8,128)(2,1)} %bitcast.56, f32[512,128]{1,0:T(8,128)} %bitcast.39, ...), custom_call_target="tpu_custom_call" | custom-call | flops 10000000000 | bytes 10000000 | tf_op jit(solution)/shard_map/pallas_call | solution.py:976
  159.1 0.6 copy.63
  159.7 0.0 copy-start.3
  159.7 0.0 copy-start.5
  159.7 0.0 copy-start.2
  159.7 80.3 %shard_map.363 = (bf16[8,256,512]{2,1,0:T(8,128)(2,1)}, f32[2,512]{1,0:T(2,128)}, bf16[4,144,512]{2,1,0:T(8,128)(2,1)}, bf16[4,144,256]{2,1,0:T(8,128)(2,1)}, bf...) custom-call(bf16[512,512]{1,0:T(8,128)(2,1)} %get-tuple-element.81.ds_ref, f32[4,512]{1,0:T(4,128)} %gains_ref.7, ...), custom_call_target="tpu_custom_call" | custom-call | flops 40000000000 | tf_op jit(solution)/shard_map/pallas_call | solution.py:1216
  240.1 0.0 copy-done.3
  240.1 0.1 pad.27.clone
  240.2 0.0 copy-done.4
  240.2 0.1 reshape.110
  240.3 0.0 copy-done.5
  240.3 0.1 reshape.111
  240.4 0.1 maximum_bitcast_fusion
  240.5 1.4 copy.57.rest_row_ref
  241.8 0.0 copy-done.2
  241.8 1.7 reshape.116.conv_row_ref
  243.5 0.0 copy-start.6
  243.5 81.8 %shard_map.364 = (bf16[4,144,256]{2,1,0:T(8,128)(2,1)}, bf16[4,144,256]{2,1,0:T(8,128)(2,1)}, bf16[4,144,256]{2,1,0:T(8,128)(2,1)}, bf16[4,144,256]{2,1,0:T(8,12...) custom-call(bf16[8,256,512]{2,1,0:T(8,128)(2,1)} %get-tuple-element., ...), custom_call_target="tpu_custom_call" | custom-call | flops 20000000000 | tf_op jit(solution)/shard_map/pallas_call | solution.py:1494
  325.4 0.0 copy-done.6
  325.4 0.6 pad.23
  325.9 10.3 %shard_map.365 = (f32[1,1]{1,0:T(1,128)}, f32[3,576,512]{2,1,0:T(8,128)}, f32[3,512]{1,0:T(4,128)}, f32[3,576,512]{2,1,0:T(8,128)}, bf16[3,576,512]{2,1,0:T(8,12...) custom-call(bf16[4,144,256]{2,1,0:T(8,128)(2,1)} %get-tuple-element., ...), custom_call_target="tpu_custom_call" | custom-call | flops 10000000 | bytes 20000000 | tf_op jit(solution)/shard_map/pallas_call | solution.py:1652
  336.2 0.7 slice.16
  336.9 0.7 copy.58
  337.6 0.7 slice.18
  338.3 0.7 copy.59
  339.0 0.7 slice.19
  339.7 0.7 copy.60
  340.4 1.2 slice_bitcast_fusion.1
  341.5 0.0 copy-done
  341.5 0.4 reduce.1
  342.0 0.6 copy.64
  342.6 0.0 copy-done.1
  342.6 0.5 reduce
  343.1 0.7 reshape.112
  343.8 0.6 reshape.113
  344.4 0.1 split.14
  344.4 0.6 reshape.115
  (10 shorter events, 0.0 us)
Async XLA Ops:
  159.7 80.4 %copy-start.3 = (f32[2048]{0:T(1024)S(1)}, f32[2048]{0:T(1024)}, u32[]{:S(2)}) copy-start(f32[2048]{0:T(1024)} %param.31) | copy-start | bytes 24580
  159.7 80.5 %copy-start.4 = (f32[64]{0:T(128)S(1)}, f32[64]{0:T(128)}, u32[]{:S(2)}) copy-start(f32[64]{0:T(128)} %param.29) | copy-start | bytes 772
  159.7 80.6 %copy-start.5 = (f32[32]{0:T(128)S(1)}, f32[32]{0:T(128)}, u32[]{:S(2)}) copy-start(f32[32]{0:T(128)} %param.33) | copy-start | bytes 388
  159.7 82.1 %copy-start.2 = (f32[576,3]{0,1:T(4,128)S(1)}, f32[576,3]{0,1:T(4,128)}, u32[]{:S(2)}) copy-start(f32[576,3]{0,1:T(4,128)} %param.27) | copy-start | bytes 20740
  243.5 81.8 %copy-start.6 = (f32[12]{0:T(128)S(1)}, f32[12]{0:T(128)}, u32[]{:S(2)}) copy-start(f32[12]{0:T(128)} %param.34) | copy-start | bytes 148
  325.9 15.6 %copy-start = (f32[4,544,1]{2,1,0:T(8,128)S(1)}, f32[4,544,1]{2,1,0:T(8,128)}, u32[]{:S(2)}) copy-start(f32[4,544,1]{2,1,0:T(8,128)} %get-tuple-element.108.rest_row_ref) | copy-start | bytes 26116
  325.9 16.7 %copy-start.1 = (f32[3,4,144,1]{3,2,1,0:T(8,128)S(1)}, f32[3,4,144,1]{3,2,1,0:T(8,128)}, u32[]{:S(2)}) copy-start(f32[3,4,144,1]{3,2,1,0:T(8,128)} %get-tuple-element.107.conv_row_ref) | copy-start | bytes 20740

commit v5 on v4

--- a/solution.py
+++ b/solution.py
@@ -196,9 +196,10 @@
     down_dot(l_ref, w_down_ref, s_ref)
 
 
-def down_input_grad(ds_ref, w_ref, dc_ref, y32, tick=None):
+def down_input_grad(ds_ref, w_ref, dc_ref, y32):
     cells, ch = ds_ref.shape
-    crops = cells // 64
+    group = 4 if cells % 256 == 0 else 1
+    size = 64 * group
 
     def dot_t(lhs, tap):
         return lax.dot_general(
@@ -208,17 +209,15 @@
             preferred_element_type=F32,
         )
 
-    def crop(i, carry):
-        if tick is not None:
-            tick(i)
-        here = ds_ref[pl.ds(pl.multiple_of(i * 64, 64), 64), :].astype(F32)
+    def crops(i, carry):
+        here = ds_ref[pl.ds(pl.multiple_of(i * size, size), size), :].astype(F32)
         at = lax.broadcasted_iota(jnp.int32, here.shape, 0)
 
         def next_col(v):
-            return jnp.where((at & 7) == 7, 0.0, pltpu.roll(v, 63, 0))
+            return jnp.where((at & 7) == 7, 0.0, pltpu.roll(v, size - 1, 0))
 
         right = next_col(here)
-        under = jnp.concatenate([here[8:], jnp.zeros((8, ch), F32)], axis=0)
+        under = jnp.where((at & 63) >= 56, 0.0, pltpu.roll(here, size - 8, 0))
         corner = next_col(under)
         ee = dot_t(here, 4)
         eo = dot_t(here, 5) + dot_t(right, 3)
@@ -229,12 +228,14 @@
             top, bottom = top.reshape(8, 1, 8, ch), bottom.reshape(8, 1, 8, ch)
             return jnp.concatenate([top, bottom], axis=1).reshape(128, ch)
 
-        put_lanes(y32, pl.ds(0, 128, stride=2), both_rows(ee, oe))
-        put_lanes(y32, pl.ds(1, 128, stride=2), both_rows(eo, oo))
-        dc_ref[i] = get_lanes(y32, slice(None)).astype(BF)
+        for k in range(group):
+            rows = slice(64 * k, 64 * k + 64)
+            put_lanes(y32, pl.ds(0, 128, stride=2), both_rows(ee[rows], oe[rows]))
+            put_lanes(y32, pl.ds(1, 128, stride=2), both_rows(eo[rows], oo[rows]))
+            dc_ref[i * group + k] = get_lanes(y32, slice(None)).astype(BF)
         return carry
 
-    lax.fori_loop(0, crops, crop, 0)
+    lax.fori_loop(0, cells // size, crops, 0)
 
 
 def down_weight_grad(l_ref, ds_ref, dw_ref):
@@ -590,6 +591,14 @@
                     copy.wait_send()
 
 
+def stand(flat_ref, pad_ref, width):
+    rows, lanes = flat_ref.shape
+    pad_ref[...] = jnp.zeros_like(pad_ref)
+    pad_ref[:rows, :lanes] = flat_ref[...]
+    turned = jnp.transpose(pad_ref[...])[:lanes]
+    return jnp.concatenate([turned, jnp.zeros((lanes, width - turned.shape[1]), F32)], axis=1)
+
+
 PARTS = (('w0b', 'yx', 1, None), ('w0a', 'yx', 0, None), ('r1', 'yx', 1, 0), ('w1b', 'yx', 1, None), ('w2b', 'yx', 1, None), ('w2a', 'yx', 0, None), ('w1a', 'y', 0, None), ('r3', 'y', 1, 1), ('r0', 'y', 0, 0), ('r2', 'y', 0, 1))
 BEFORE = ('w0b1', 'w0a1', 'w0b2', 'r11', 'w0a2', 'w1b1', 'r12', 'w2b1', 'w0b3', 'w1b2', 'w2a1', 'w2b2', 'w0a3', 'w2a2', 'w1a1')
 FIRST = {3: ('r13',), 4: ('r31',), 6: ('w1a2',), 7: ('w1b3',)}
@@ -604,7 +613,7 @@
     conv_ref,
     code_ref,
     proj_ref,
-    head_ref,
+    head_flat_ref,
     gains_ref,
     x_out,
     side_out,
@@ -623,6 +632,8 @@
     a_two_ref,
     l_ref,
     k_sem,
+    head_pad,
+    head_ref,
     w_mine,
     rest_mine,
     xv,
@@ -651,6 +662,7 @@
             wt_ref[j : j + 1, :] += jnp.sum(v * v, axis=0, keepdims=True)
 
     def cast_rest():
+        head_ref[...] = stand(head_flat_ref, head_pad, lat)
         for k in range(4):
             low = 0
             for m, (ref, n) in enumerate(
@@ -832,6 +844,8 @@
             pltpu.VMEM((crops, ranks * cells, ch), BF),
             pltpu.VMEM((lat_cells, 9 * ch), BF),
             pltpu.SemaphoreType.DMA((4, crops)),
+            pltpu.VMEM((128, 128), F32),
+            pltpu.VMEM((head_w.shape[1], lat), F32),
             pltpu.VMEM((3, 2, 2, n_conv, ch), BF),
             pltpu.VMEM((2, 2, n_rest, lat), BF),
             pltpu.VMEM((crops, ranks, cells, ch), BF),
@@ -863,7 +877,7 @@
     rest,
     side_ref,
     sl_ref,
-    l_ref,
+    l_in,
     ds_ref,
     loss_ref,
     dp_ref,
@@ -874,6 +888,7 @@
     proj_v,
     head_v,
     e_ref,
+    l_ref,
     sems,
 ):
     lat_count, pix_count, rgb, n_code = consts
@@ -885,6 +900,7 @@
         pltpu.make_async_copy(rest.at[:, n_code : n_code + 16], proj_v, sems.at[slots]),
         pltpu.make_async_copy(rest.at[:, n_code + 16 :], head_v, sems.at[slots + 1]),
     ]
+    windows = pltpu.make_async_copy(l_in, l_ref, sems.at[slots + 2])
     for copy in small:
         copy.start()
 
@@ -894,6 +910,7 @@
 
     for p in range(slots):
         fetch(p).start()
+    windows.start()
 
     def widen(p, carry):
         fetch(p).wait()
@@ -960,6 +977,7 @@
     d_head = d_head.reshape(pieces, 8, lat)
     d_head = jnp.concatenate([d_head, jnp.zeros((pieces, 8, lat), F32)], axis=1)
     small_ref[:, 16:] = d_head.astype(BF)
+    windows.wait()
     down_weight_grad(l_ref, ds_ref, dw_ref)
 
 
@@ -976,7 +994,7 @@
     return pl.pallas_call(
         functools.partial(quantizer_kernel, (lat_count, pix_count, rgb, n_code)),
         out_shape=outs,
-        in_specs=[pl.BlockSpec(memory_space=pltpu.SMEM), ANY, VM, VM, VM],
+        in_specs=[pl.BlockSpec(memory_space=pltpu.SMEM), ANY, VM, VM, ANY],
         out_specs=[VM] * 5,
         scratch_shapes=[
             pltpu.VMEM((pieces * n_code, lat), F32),
@@ -984,7 +1002,8 @@
             pltpu.VMEM((pieces, 16, lat), BF),
             pltpu.VMEM((pieces, rows - n_code - 16, lat), BF),
             pltpu.VMEM((4, cells, lat), F32),
-            pltpu.SemaphoreType.DMA((6,)),
+            pltpu.VMEM(windows.shape, BF),
+            pltpu.SemaphoreType.DMA((7,)),
         ],
         compiler_params=pltpu.CompilerParams(vmem_limit_bytes=58 * MIB),
         cost_estimate=pl.CostEstimate(flops=10**10, bytes_accessed=10**7, transcendentals=0),
@@ -1140,11 +1159,6 @@
         lax.fori_loop(0, 4, away, 0)
         lax.fori_loop(0, 4, here, 0)
 
-    def tick_down(i):
-        @pl.when(i == 4)
-        def _():
-            down.go(1)
-
     def tick_high(dx):
         @pl.when(dx == 2)
         def _():
@@ -1173,7 +1187,8 @@
             down.arrive(1)
 
     loads[0].wait()
-    down_input_grad(ds_ref, w_down_ref, din_ref, y32, tick_down)
+    down_input_grad(ds_ref, w_down_ref, din_ref, y32)
+    down.go(1)
     shift_all(din_ref, d3)
     loads[1].wait()
     conv_weight_grad(a_ref, d3, dw, 0)
@@ -1536,10 +1551,10 @@
     g_down,
     g_rest0,
     g_rest1,
-    conv_ref,
-    code_ref,
+    conv_in,
+    code_in,
     proj_ref,
-    head_ref,
+    head_flat_ref,
     conv_row_ref,
     rest_row_ref,
     tv_ref,
@@ -1553,8 +1568,30 @@
     conv_outs,
     rest_outs,
     gain_outs,
+    conv_ref,
+    code_ref,
+    head_ref,
+    head_pad,
+    cg,
+    cn,
+    cl,
+    kg,
+    kn,
+    kl,
+    l_sem,
+    s_sem,
 ):
     n_code, n_proj, n_head, rgb, shards = sizes
+    loads = [pltpu.make_async_copy(conv_in.at[j], conv_ref.at[j], l_sem.at[j]) for j in range(3)]
+    loads.append(pltpu.make_async_copy(code_in, code_ref, l_sem.at[3]))
+    for copy in loads:
+        copy.start()
+    stores = []
+
+    def store(src, dst):
+        stores.append(pltpu.make_async_copy(src, dst, s_sem.at[len(stores)]))
+        stores[-1].start()
+
     ch = conv_ref.shape[2]
     lat = code_ref.shape[1]
 
@@ -1571,7 +1608,7 @@
     def line(k):
         return tv_ref[k : k + 1, :]
 
-    cg, cc, cn, cl = conv_outs
+    cg_out, cc, cn_out, cl_out = conv_outs
     for j, parts in enumerate(((g_first0, g_first1), (g_second0, g_second1), (g_down,))):
         n = conv_ref.shape[1]
         col_new, q, row_mean = scales(
@@ -1579,6 +1616,7 @@
         )
         cc[j : j + 1, :] = col_new
         m = n // 4
+        loads[j].wait()
         for k in range(4):
             r = lax.rsqrt(conv_row_ref[j, k] / row_mean)
             rows = slice(k * m, (k + 1) * m)
@@ -1590,10 +1628,16 @@
                 cg[j, rows, lanes] = g
                 cn[j, rows, lanes] = new
                 cl[j, rows, lanes] = new.astype(BF)
+        for src, dst in ((cg, cg_out), (cn, cn_out), (cl, cl_out)):
+            store(src.at[j], dst.at[j])
+    loads[3].wait()
+    head_ref[...] = stand(head_flat_ref, head_pad, lat)
     cols = (code_col_ref, proj_col_ref, head_col_ref)
     spans = ((0, n_code, lat), (n_code, n_proj, lat), (n_code + n_proj, n_head, rgb))
     for m, (w_ref, (start, size, width)) in enumerate(zip((code_ref, proj_ref, head_ref), spans)):
         og, oc, on, ol = rest_outs[m]
+        if m == 0:
+            code_outs, (og, on, ol) = (og, on, ol), (kg, kn, kl)
         col_new, q, row_mean = scales(
             cols[m][...],
             line(9 + m)[:, :lat],
@@ -1604,21 +1648,29 @@
             width,
         )
         oc[...] = col_new
-        news = []
+        both = []
         for k in range(4):
             g = jnp.concatenate([g_rest0[k].astype(F32), g_rest1[k].astype(F32)], axis=1)
             g = g[start : start + size]
             r = lax.rsqrt(rest_row_ref[k, start : start + size] / row_mean)
             rows = slice(k * size, (k + 1) * size)
             new = w_ref[rows, :] - g * r * q
-            og[rows, :] = g
-            on[rows, :] = new
-            if size % 16:
-                news.append(new)
+            if m == 2:
+                both.append((g, new))
             else:
+                og[rows, :] = g
+                on[rows, :] = new
                 ol[rows, :] = new.astype(BF)
-        if news:
-            ol[...] = jnp.concatenate(news, axis=0).astype(BF)
+        if m == 0:
+            for src, dst in zip((og, on, ol), code_outs):
+                store(src, dst)
+        if m == 2:
+            for ref, values in zip((og, on), zip(*both)):
+                tall = jnp.concatenate(values, axis=0)[:, :128]
+                tall = jnp.concatenate([tall, jnp.zeros((128 - tall.shape[0], 128), F32)], axis=0)
+                head_pad[...] = jnp.transpose(tall)
+                ref[...] = head_pad[: ref.shape[0], : ref.shape[1]]
+            ol[...] = on[...].astype(BF)
     loss_ref[...] = jnp.sum(line(20), axis=1, keepdims=True)
     grad = tv_ref[16:20, :]
     state = 0.5 * state_ref[...] + 0.5 * (grad * grad + EPS_SQ)
@@ -1633,6 +1685,8 @@
     gain_outs[0][...] = grad
     gain_outs[1][...] = state
     gain_outs[2][...] = gains - RATE * rms(gains) * update / jnp.maximum(1.0, rms(update))
+    for copy in stores:
+        copy.wait()
 
 
 def finish_call(sizes, grads, weights, rows, tv, cols, gains, state):
@@ -1649,11 +1703,25 @@
     outs += [[matrix(w, (1, lat)) for w in (code_w, proj_w, head_w)]]
     outs += [[shape(gains.shape)] * 3]
     args = [*grads, *weights, *rows, tv, *cols, gains, state]
+    specs = jax.tree.map(lambda _: VM, outs)
+    streamed = [ANY, VM, ANY, ANY]
+    specs[1] = streamed
+    specs[2] = [streamed] + specs[2][1:]
+    in_specs = [VM] * len(args)
+    in_specs[len(grads)] = in_specs[len(grads) + 1] = ANY
     return pl.pallas_call(
         functools.partial(finish_kernel, sizes),
         out_shape=outs,
-        in_specs=[VM] * len(args),
-        out_specs=jax.tree.map(lambda _: VM, outs),
+        in_specs=in_specs,
+        out_specs=specs,
+        scratch_shapes=[
+            pltpu.VMEM(conv_w.shape, F32),
+            pltpu.VMEM(code_w.shape, F32),
+            pltpu.VMEM((head_w.shape[1], lat), F32),
+            pltpu.VMEM((128, 128), F32),
+        ]
+        + [pltpu.VMEM(w.shape, t) for w in (conv_w, code_w) for t in (F32, F32, BF)]
+        + [pltpu.SemaphoreType.DMA((4,)), pltpu.SemaphoreType.DMA((12,))],
         compiler_params=pltpu.CompilerParams(vmem_limit_bytes=56 * MIB),
         cost_estimate=pl.CostEstimate(flops=10**7, bytes_accessed=2 * 10**7, transcendentals=0),
     )(*args)
@@ -1943,7 +2011,7 @@
     n_code, n_proj, n_head = (v.shape[0] // ranks for v in (code_w, proj_w, head_w))
     sizes = (n_code, n_proj, n_head, rgb)
     conv_rows = jnp.transpose(conv_w, (1, 0, 2))
-    head_wide = jnp.pad(head_w, ((0, 0), (0, lat - rgb)))
+    head_flat = jnp.transpose(head_w)
 
     def lanes(v, n):
         return jnp.pad(v, ((0, 0),) * (v.ndim - 1) + ((0, n - v.shape[-1]),))
@@ -1956,7 +2024,7 @@
         conv_rows,
         code_w,
         proj_w,
-        head_wide,
+        head_flat,
         gains,
     )
     x = out[0].reshape(crops, cells, ch)
@@ -2016,7 +2084,7 @@
     loss, conv_outs, rest_outs, gain_outs = finish_call(
         sizes + (shards,),
         out[:7],
-        (conv_rows, code_w, proj_w, head_wide),
+        (conv_rows, code_w, proj_w, head_flat),
         (conv_rn, rest_rn),
         tv,
         (conv_col, code_col[None], proj_col[None], head_col_wide[None]),
@@ -2050,11 +2118,11 @@
         code_o[1][0],
         code_o[2],
         code_o[3],
-        head_o[0][:, :rgb],
+        jnp.transpose(head_o[0]),
         head_r,
         head_o[1][0, :rgb],
-        head_o[2][:, :rgb],
-        head_o[3][:, :rgb],
+        jnp.transpose(head_o[2]),
+        jnp.transpose(head_o[3]),
         *gain_outs,
     )
 

time: 346 us -> 336 us (0.971)
  local copies, waits for them, and re-layouts: 15.5 us -> 9.94 us
  Pallas kernels: 324 us -> 320 us
where the time goes in v5:
time: 336 us
  Pallas kernels  320 us (95%)
  local copies, waits for them, and re-layouts  9.94 us (3%)
  other arithmetic  4.5 us (1%)
    pallas_call x1, Pallas kernels, forward_call(): pl.pallas_call(forward_kernel, out_shape=outs, in_specs=[ANY] * 2 + [VM]...  128 us
    pallas_call x1, Pallas kernels, first_back_call(): pl.pallas_call(functools.partial(first_back_kernel, sizes), out_shape=out...  81.3 us
    pallas_call x1, Pallas kernels, second_back_call(): pl.pallas_call(functools.partial(second_back_kernel, n_code), out_shape=o...  77.8 us
    pallas_call x1, Pallas kernels, quantizer_call(): pl.pallas_call(functools.partial(quantizer_kernel, (lat_count, pix_count,...  23.4 us
    pallas_call x1, Pallas kernels, finish_call(): pl.pallas_call(functools.partial(finish_kernel, sizes), out_shape=outs, i...  10 us

profile of v5, /device:TPU:0, one launch (start us, length us, event | category | flops | bytes accessed | tf_op | source)
XLA Modules:
  0.0 335.5 jit_solution(2188804046157115332)
XLA Ops:
  0.7 0.8 convert_element_type.17
  1.4 0.8 convert_element_type.18
  2.2 0.9 fusion
  3.1 0.2 copy.53
  3.4 0.7 pad.17.clone
  4.1 127.8 %shard_map.361 = (bf16[8,4,64,512]{3,2,1,0:T(8,128)(2,1)}, f32[8,4,16,128]{3,2,1,0:T(8,128)}, bf16[4608,512]{1,0:T(8,128)(2,1)}, bf16[4608,512]{1,0:T(8,128)(2,1...) custom-call(bf16[4,8,64,512]{3,2,1,0:T(8,128)(2,1)} %bitcast.58, ...), custom_call_target="tpu_custom_call" | custom-call | flops 24159191040 | tf_op jit(solution)/shard_map/pallas_call | solution.py:836
  131.9 1.1 fusion.2
  133.0 0.1 copy.49
  133.1 0.6 copy.54
  133.7 23.4 %shard_map.362 = (bf16[512,512]{1,0:T(8,128)(2,1)}, f32[8,512]{1,0:T(8,128)}, bf16[2048,256]{1,0:T(8,128)(2,1)}, bf16[32,32,256]{2,1,0:T(8,128)(2,1)}, bf16[4608,512]{1,0:T(8,128)(2,1)}) custom-call(s32[2048]{0:T(1024)} %bitcast.52, bf16[32,544,256]{2,1,0:T(8,128)(2,1)} %bitcast.65, f32[512,128]{1,0:T(8,128)} %bitcast.43, ...), custom_call_target="tpu_custom_call" | custom-call | flops 10000000000 | bytes 10000000 | tf_op jit(solution)/shard_map/pallas_call | solution.py:994
  157.1 0.6 copy.55
  157.7 0.0 copy-start.3
  157.7 0.0 copy-start.4
  157.7 0.0 copy-start.5
  157.7 0.0 copy-start.2
  157.7 77.8 %shard_map.363 = (bf16[8,256,512]{2,1,0:T(8,128)(2,1)}, f32[2,512]{1,0:T(2,128)}, bf16[4,144,512]{2,1,0:T(8,128)(2,1)}, bf16[4,144,256]{2,1,0:T(8,128)(2,1)}, bf...) custom-call(bf16[512,512]{1,0:T(8,128)(2,1)} %get-tuple-element.81.ds_ref, f32[4,512]{1,0:T(4,128)} %gains_ref.7, ...), custom_call_target="tpu_custom_call" | custom-call | flops 40000000000 | tf_op jit(solution)/shard_map/pallas_call | solution.py:1231
  235.5 0.0 copy-done.3
  235.6 0.1 pad.22.clone
  235.6 0.0 copy-done.4
  235.6 0.1 reshape.110
  235.7 0.0 copy-done.5
  235.7 0.1 reshape.111
  235.8 0.1 maximum_bitcast_fusion
  235.9 1.4 copy.52.rest_row_ref
  237.3 0.0 copy-done.2
  237.3 1.7 reshape.116.conv_row_ref
  238.9 0.0 copy-start.6
  238.9 81.3 %shard_map.364 = (bf16[4,144,256]{2,1,0:T(8,128)(2,1)}, bf16[4,144,256]{2,1,0:T(8,128)(2,1)}, bf16[4,144,256]{2,1,0:T(8,128)(2,1)}, bf16[4,144,256]{2,1,0:T(8,12...) custom-call(bf16[8,256,512]{2,1,0:T(8,128)(2,1)} %get-tuple-element., ...), custom_call_target="tpu_custom_call" | custom-call | flops 20000000000 | tf_op jit(solution)/shard_map/pallas_call | solution.py:1509
  320.3 0.0 copy-done.6
  320.3 0.6 pad.18
  320.8 0.0 copy-start
  320.8 0.0 copy-start.1
  320.8 10.0 %shard_map.365 = (f32[1,1]{1,0:T(1,128)}, f32[3,576,512]{2,1,0:T(8,128)}, f32[3,512]{1,0:T(4,128)}, f32[3,576,512]{2,1,0:T(8,128)}, bf16[3,576,512]{2,1,0:T(8,12...) custom-call(bf16[4,144,256]{2,1,0:T(8,128)(2,1)} %get-tuple-element., ...), custom_call_target="tpu_custom_call" | custom-call | flops 10000000 | bytes 20000000 | tf_op jit(solution)/shard_map/pallas_call | solution.py:1712
  330.9 1.2 slice_bitcast_fusion.1
  332.0 0.0 copy-done
  332.0 0.4 reduce.1
  332.5 0.6 copy.56
  333.1 0.0 copy-done.1
  333.1 0.5 reduce
  333.6 0.7 reshape.112
  334.3 0.6 reshape.113
  334.9 0.1 split.14
  334.9 0.6 reshape.115
  (7 shorter events, 0.0 us)
Async XLA Ops:
  157.7 77.8 %copy-start.3 = (f32[2048]{0:T(1024)S(1)}, f32[2048]{0:T(1024)}, u32[]{:S(2)}) copy-start(f32[2048]{0:T(1024)} %param.31) | copy-start | bytes 24580
  157.7 77.9 %copy-start.4 = (f32[64]{0:T(128)S(1)}, f32[64]{0:T(128)}, u32[]{:S(2)}) copy-start(f32[64]{0:T(128)} %param.29) | copy-start | bytes 772
  157.7 78.0 %copy-start.5 = (f32[32]{0:T(128)S(1)}, f32[32]{0:T(128)}, u32[]{:S(2)}) copy-start(f32[32]{0:T(128)} %param.33) | copy-start | bytes 388
  157.7 79.5 %copy-start.2 = (f32[576,3]{0,1:T(4,128)S(1)}, f32[576,3]{0,1:T(4,128)}, u32[]{:S(2)}) copy-start(f32[576,3]{0,1:T(4,128)} %param.27) | copy-start | bytes 20740
  238.9 81.3 %copy-start.6 = (f32[12]{0:T(128)S(1)}, f32[12]{0:T(128)}, u32[]{:S(2)}) copy-start(f32[12]{0:T(128)} %param.34) | copy-start | bytes 148
  320.8 11.2 %copy-start = (f32[4,544,1]{2,1,0:T(8,128)S(1)}, f32[4,544,1]{2,1,0:T(8,128)}, u32[]{:S(2)}) copy-start(f32[4,544,1]{2,1,0:T(8,128)} %get-tuple-element.108.rest_row_ref) | copy-start | bytes 26116
  320.8 12.2 %copy-start.1 = (f32[3,4,144,1]{3,2,1,0:T(8,128)S(1)}, f32[3,4,144,1]{3,2,1,0:T(8,128)}, u32[]{:S(2)}) copy-start(f32[3,4,144,1]{3,2,1,0:T(8,128)} %get-tuple-element.107.conv_row_ref) | copy-start | bytes 20740

commit v6 on v5

--- a/solution.py
+++ b/solution.py
@@ -238,7 +238,7 @@
     lax.fori_loop(0, cells // size, crops, 0)
 
 
-def down_weight_grad(l_ref, ds_ref, dw_ref):
+def down_weight_grad(l_ref, ds_ref, dw_ref, after=None):
     ch = ds_ref.shape[1]
 
     def block(t, carry):
@@ -250,6 +250,8 @@
             preferred_element_type=F32,
         )
         dw_ref[pl.ds(lane, ch), :] = d.astype(BF)
+        if after is not None:
+            after(t)
         return carry
 
     lax.fori_loop(0, 9, block, 0)
@@ -882,14 +884,16 @@
     loss_ref,
     dp_ref,
     small_ref,
-    dw_ref,
+    dw_out,
     tab,
     stage,
     proj_v,
     head_v,
     e_ref,
     l_ref,
+    dw_ref,
     sems,
+    w_sems,
 ):
     lat_count, pix_count, rgb, n_code = consts
     cells = sl_ref.shape[0]
@@ -978,7 +982,15 @@
     d_head = jnp.concatenate([d_head, jnp.zeros((pieces, 8, lat), F32)], axis=1)
     small_ref[:, 16:] = d_head.astype(BF)
     windows.wait()
-    down_weight_grad(l_ref, ds_ref, dw_ref)
+
+    def keep(t):
+        ch = dw_ref.shape[1]
+        rows = pl.ds(pl.multiple_of(t * ch, ch), ch)
+        return pltpu.make_async_copy(dw_ref.at[rows], dw_out.at[rows], w_sems.at[t])
+
+    down_weight_grad(l_ref, ds_ref, dw_ref, lambda t: keep(t).start())
+    for t in range(9):
+        keep(t).wait()
 
 
 def quantizer_call(codes, rest, side, s_low, windows, lat_count, pix_count, rgb, n_code):
@@ -995,7 +1007,7 @@
         functools.partial(quantizer_kernel, (lat_count, pix_count, rgb, n_code)),
         out_shape=outs,
         in_specs=[pl.BlockSpec(memory_space=pltpu.SMEM), ANY, VM, VM, ANY],
-        out_specs=[VM] * 5,
+        out_specs=[VM] * 4 + [ANY],
         scratch_shapes=[
             pltpu.VMEM((pieces * n_code, lat), F32),
             pltpu.VMEM((4, n_code, lat), BF),
@@ -1003,7 +1015,9 @@
             pltpu.VMEM((pieces, rows - n_code - 16, lat), BF),
             pltpu.VMEM((4, cells, lat), F32),
             pltpu.VMEM(windows.shape, BF),
+            pltpu.VMEM((9 * ch, ch), BF),
             pltpu.SemaphoreType.DMA((7,)),
+            pltpu.SemaphoreType.DMA((9,)),
         ],
         compiler_params=pltpu.CompilerParams(vmem_limit_bytes=58 * MIB),
         cost_estimate=pl.CostEstimate(flops=10**10, bytes_accessed=10**7, transcendentals=0),

time: 336 us -> 336 us (level)
  no operation moved by 1% of the time
where the time goes in v6:
time: 336 us; the launch traced here: 335 us
  Pallas kernels  320 us (95%)
  local copies, waits for them, and re-layouts  9.94 us (3%)
  other arithmetic  4.5 us (1%)
    pallas_call x1, Pallas kernels, forward_call(): pl.pallas_call(forward_kernel, out_shape=outs, in_specs=[ANY] * 2 + [VM]...  128 us
    pallas_call x1, Pallas kernels, first_back_call(): pl.pallas_call(functools.partial(first_back_kernel, sizes), out_shape=out...  81.3 us
    pallas_call x1, Pallas kernels, second_back_call(): pl.pallas_call(functools.partial(second_back_kernel, n_code), out_shape=o...  77.8 us
    pallas_call x1, Pallas kernels, quantizer_call(): pl.pallas_call(functools.partial(quantizer_kernel, (lat_count, pix_count,...  23.2 us
    pallas_call x1, Pallas kernels, finish_call(): pl.pallas_call(functools.partial(finish_kernel, sizes), out_shape=outs, i...  10 us

profile of v6, /device:TPU:0, one launch (start us, length us, event | category | flops | bytes accessed | tf_op | source)
XLA Modules:
  0.0 335.3 jit_solution(8754136163562788115)
XLA Ops:
  0.7 0.8 convert_element_type.17
  1.4 0.8 convert_element_type.18
  2.2 0.9 fusion
  3.1 0.2 copy.53
  3.4 0.7 pad.17.clone
  4.1 127.8 %shard_map.361 = (bf16[8,4,64,512]{3,2,1,0:T(8,128)(2,1)}, f32[8,4,16,128]{3,2,1,0:T(8,128)}, bf16[4608,512]{1,0:T(8,128)(2,1)}, bf16[4608,512]{1,0:T(8,128)(2,1...) custom-call(bf16[4,8,64,512]{3,2,1,0:T(8,128)(2,1)} %bitcast.58, ...), custom_call_target="tpu_custom_call" | custom-call | flops 24159191040 | tf_op jit(solution)/shard_map/pallas_call | solution.py:838
  131.9 1.1 fusion.2
  133.0 0.1 copy.49
  133.1 0.6 copy.54
  133.7 23.2 %shard_map.362 = (bf16[512,512]{1,0:T(8,128)(2,1)}, f32[8,512]{1,0:T(8,128)}, bf16[2048,256]{1,0:T(8,128)(2,1)}, bf16[32,32,256]{2,1,0:T(8,128)(2,1)}, bf16[4608,512]{1,0:T(8,128)(2,1)}) custom-call(s32[2048]{0:T(1024)} %bitcast.52, bf16[32,544,256]{2,1,0:T(8,128)(2,1)} %bitcast.65, f32[512,128]{1,0:T(8,128)} %bitcast.43, ...), custom_call_target="tpu_custom_call" | custom-call | flops 10000000000 | bytes 10000000 | tf_op jit(solution)/shard_map/pallas_call | solution.py:1006
  156.9 0.6 copy.55
  157.5 0.0 copy-start.3
  157.5 0.0 copy-start.4
  157.5 0.0 copy-start.5
  157.5 0.0 copy-start.2
  157.5 77.8 %shard_map.363 = (bf16[8,256,512]{2,1,0:T(8,128)(2,1)}, f32[2,512]{1,0:T(2,128)}, bf16[4,144,512]{2,1,0:T(8,128)(2,1)}, bf16[4,144,256]{2,1,0:T(8,128)(2,1)}, bf...) custom-call(bf16[512,512]{1,0:T(8,128)(2,1)} %get-tuple-element.81.ds_ref, f32[4,512]{1,0:T(4,128)} %gains_ref.7, ...), custom_call_target="tpu_custom_call" | custom-call | flops 40000000000 | tf_op jit(solution)/shard_map/pallas_call | solution.py:1245
  235.3 0.0 copy-done.3
  235.3 0.1 pad.22.clone
  235.4 0.0 copy-done.4
  235.4 0.1 reshape.110
  235.5 0.0 copy-done.5
  235.5 0.1 reshape.111
  235.6 0.1 maximum_bitcast_fusion
  235.7 1.4 copy.52.rest_row_ref
  237.1 0.0 copy-done.2
  237.1 1.7 reshape.116.conv_row_ref
  238.7 0.0 copy-start.6
  238.7 81.3 %shard_map.364 = (bf16[4,144,256]{2,1,0:T(8,128)(2,1)}, bf16[4,144,256]{2,1,0:T(8,128)(2,1)}, bf16[4,144,256]{2,1,0:T(8,128)(2,1)}, bf16[4,144,256]{2,1,0:T(8,12...) custom-call(bf16[8,256,512]{2,1,0:T(8,128)(2,1)} %get-tuple-element., ...), custom_call_target="tpu_custom_call" | custom-call | flops 20000000000 | tf_op jit(solution)/shard_map/pallas_call | solution.py:1523
  320.0 0.0 copy-done.6
  320.1 0.6 pad.18
  320.6 0.0 copy-start
  320.6 0.0 copy-start.1
  320.6 10.0 %shard_map.365 = (f32[1,1]{1,0:T(1,128)}, f32[3,576,512]{2,1,0:T(8,128)}, f32[3,512]{1,0:T(4,128)}, f32[3,576,512]{2,1,0:T(8,128)}, bf16[3,576,512]{2,1,0:T(8,12...) custom-call(bf16[4,144,256]{2,1,0:T(8,128)(2,1)} %get-tuple-element., ...), custom_call_target="tpu_custom_call" | custom-call | flops 10000000 | bytes 20000000 | tf_op jit(solution)/shard_map/pallas_call | solution.py:1726
  330.6 1.2 slice_bitcast_fusion.1
  331.8 0.0 copy-done
  331.8 0.4 reduce.1
  332.2 0.6 copy.56
  332.8 0.0 copy-done.1
  332.8 0.5 reduce
  333.3 0.7 reshape.112
  334.0 0.6 reshape.113
  334.6 0.1 split.14
  334.7 0.6 reshape.115
  (7 shorter events, 0.0 us)
Async XLA Ops:
  157.5 77.8 %copy-start.3 = (f32[2048]{0:T(1024)S(1)}, f32[2048]{0:T(1024)}, u32[]{:S(2)}) copy-start(f32[2048]{0:T(1024)} %param.31) | copy-start | bytes 24580
  157.5 77.9 %copy-start.4 = (f32[64]{0:T(128)S(1)}, f32[64]{0:T(128)}, u32[]{:S(2)}) copy-start(f32[64]{0:T(128)} %param.29) | copy-start | bytes 772
  157.5 78.0 %copy-start.5 = (f32[32]{0:T(128)S(1)}, f32[32]{0:T(128)}, u32[]{:S(2)}) copy-start(f32[32]{0:T(128)} %param.33) | copy-start | bytes 388
  157.5 79.5 %copy-start.2 = (f32[576,3]{0,1:T(4,128)S(1)}, f32[576,3]{0,1:T(4,128)}, u32[]{:S(2)}) copy-start(f32[576,3]{0,1:T(4,128)} %param.27) | copy-start | bytes 20740
  238.7 81.3 %copy-start.6 = (f32[12]{0:T(128)S(1)}, f32[12]{0:T(128)}, u32[]{:S(2)}) copy-start(f32[12]{0:T(128)} %param.34) | copy-start | bytes 148
  320.6 11.2 %copy-start = (f32[4,544,1]{2,1,0:T(8,128)S(1)}, f32[4,544,1]{2,1,0:T(8,128)}, u32[]{:S(2)}) copy-start(f32[4,544,1]{2,1,0:T(8,128)} %get-tuple-element.108.rest_row_ref) | copy-start | bytes 26116
  320.6 12.2 %copy-start.1 = (f32[3,4,144,1]{3,2,1,0:T(8,128)S(1)}, f32[3,4,144,1]{3,2,1,0:T(8,128)}, u32[]{:S(2)}) copy-start(f32[3,4,144,1]{3,2,1,0:T(8,128)} %get-tuple-element.107.conv_row_ref) | copy-start | bytes 20740
